TPU v7x, 256 devices: a whole 4x4x8 slice. The times are simulated.
256 devices in a mesh: blk: 256 (over z, y, x, core).
Axes of the slice: x: 4, y: 4, z: 8, core: 2. Of those that a mesh axis runs over, the one named last changes fastest.
Arguments:
- frames: bfloat16 [131072, 1536], P('blk'), may hold values from -6 to 6
- head: bfloat16 [1536, 768], replicated, may hold values from -0.15625 to 0.15625
- offsets: int32 [131072], P('blk'), may hold values from 1 to 1024, as said below
Outputs:
- losses: float32 [131072], P('blk')
- frame_grad: bfloat16 [131072, 1536], P('blk')
- head_grad: bfloat16 [1536, 768], replicated
Inputs may be any that keep to these rules, and one draw needn't show every extreme that they name: `offsets`: the positive of row i is row (i + offsets_i) mod 131072, always a later frame within 1024 rows.
All inputs are finite; a program needn't handle non-finite values.
Results may differ from a plain program's by a relative error of at most 0.0061.
Values may be sent and summed in bfloat16 or wider, within the bound.
No kernel may reach another device: no remote copies, remote signals or barrier semaphores. Data moves between devices by JAX's collectives and lax.ppermute only.
A program may use at most 64 MiB of HBM per device.

v0:
```python
import jax
import jax.numpy as jnp
from jax import lax
from jax.sharding import Mesh, PartitionSpec as P

SCALE = 50.0
ALL = ("z", "y", "x", "core")
SIZES = (8, 4, 4, 2)
F32, BF16 = jnp.float32, jnp.bfloat16


def send(x, to):
    return lax.ppermute(x, ALL, [(i, to(i) % 256) for i in range(256)])


def in_chip(x):
    return send(x, lambda i: i ^ 1)


def ahead(x, by):
    return send(x, lambda i: i + by)


def dot(left, right):
    return jnp.dot(left, right, preferred_element_type=F32)


def dot_nt(left, right):
    return lax.dot_general(left, right, (((1,), (1,)), ((), ())), preferred_element_type=F32)


def dot_tn(left, right):
    return lax.dot_general(left, right, (((0,), (0,)), ((), ())), preferred_element_type=F32)


def scatter_sum(part, axes):
    n = lax.axis_size(axes)
    shares = part.astype(BF16).reshape(n, part.shape[0] // n, part.shape[1])
    got = lax.all_to_all(shares, axes, split_axis=0, concat_axis=0)
    return jnp.sum(got.astype(F32), axis=0)


def gather(piece, axes):
    n = lax.axis_size(axes)
    copies = jnp.broadcast_to(piece[None], (n,) + piece.shape)
    got = lax.all_to_all(copies, axes, split_axis=0, concat_axis=0)
    return got.reshape((n * piece.shape[0],) + piece.shape[1:])


def on_device(frames, head, offsets):
    rows, depth = frames.shape
    width = head.shape[1]
    core = lax.axis_index("core")
    even = core == 0
    z = dot(frames, head)
    norm = jnp.sqrt(jnp.sum(z * z, axis=1, keepdims=True) + 1e-06)
    unit = z / norm
    emb = unit.astype(BF16)

    swapped = in_chip(emb)
    first = send(emb, lambda i: i - 2 if i % 2 == 0 else i + 2)
    second = send(emb, lambda i: i + 2 if i % 2 == 0 else i - 2)
    relayed = in_chip(first)
    blocks = [emb, swapped, first, relayed, second]
    place = [0, jnp.where(even, 1, -1), jnp.where(even, 2, -2), jnp.where(even, -1, 1), jnp.where(even, -2, 2)]

    half = depth // 2
    mine = lax.dynamic_slice_in_dim(frames, core * half, half, 1)
    theirs = in_chip(lax.dynamic_slice_in_dim(frames, (1 - core) * half, half, 1))

    rowids = jnp.arange(rows, dtype=jnp.int32)
    target = rowids + offsets
    exps, total, score_pos = [], jnp.zeros((rows,), F32), jnp.zeros((rows,), F32)
    for block, at in zip(blocks, place):
        score = SCALE * dot_nt(emb, block)
        hit = (rowids + at * rows)[None, :] == target[:, None]
        score_pos = score_pos + jnp.sum(jnp.where(hit, score, 0.0), axis=1)
        e = jnp.exp(score)
        if block is emb:
            e = jnp.where(rowids[None, :] == rowids[:, None], 0.0, e)
        total = total + jnp.sum(e, axis=1)
        exps.append(e)
    losses = jnp.log(total) - score_pos
    inv = 1.0 / total
    note = jnp.stack([inv, target.astype(F32)])
    peer_note = in_chip(note)
    pair = jnp.concatenate([jnp.where(even, note, peer_note), jnp.where(even, peer_note, note)])
    behind, beyond = ahead(pair, 2), ahead(pair, -2)
    b1, b2 = jnp.where(even, behind[2:], peer_note), jnp.where(even, behind[:2], behind[2:])
    f1, f2 = jnp.where(even, peer_note[0], beyond[0]), jnp.where(even, beyond[0], beyond[2])
    back1, back2 = b1[1].astype(jnp.int32), b2[1].astype(jnp.int32)
    b1, b2 = b1[0], b2[0]
    invs = [inv, jnp.where(even, f1, b1), jnp.where(even, f2, b2), jnp.where(even, b1, f1), jnp.where(even, b2, f2)]
    never = jnp.full_like(target, -1)
    targets = [
        target,
        jnp.where(even, never, back1 - rows),
        jnp.where(even, never, back2 - 2 * rows),
        jnp.where(even, back1 - rows, never),
        jnp.where(even, back2 - 2 * rows, never),
    ]
    demb = jnp.zeros((rows, width), F32)
    for block, at, e, other, goal in zip(blocks, place, exps, invs, targets):
        hit = (rowids + at * rows)[None, :] == target[:, None]
        hit_back = rowids[:, None] == goal[None, :]
        g = e * (inv[:, None] + other[None, :]) - hit.astype(F32) - hit_back.astype(F32)
        demb = demb + dot(g.astype(BF16), block)
    demb = SCALE * demb
    dz = ((demb - unit * jnp.sum(unit * demb, axis=1, keepdims=True)) / norm).astype(BF16)
    frame_grad = dot_nt(dz, head).astype(BF16)

    dz_other = in_chip(dz)
    part = dot_tn(mine, dz) + dot_tn(theirs, dz_other)
    share = scatter_sum(scatter_sum(part, ("y", "x")), "z").astype(BF16)
    own = gather(gather(share, "z"), ("y", "x"))
    peer = in_chip(own)
    head_grad = jnp.concatenate([jnp.where(even, own, peer), jnp.where(even, peer, own)], axis=0)
    return (losses, frame_grad, head_grad)


def solution(mesh):
    torus = Mesh(mesh.devices.reshape(SIZES), ALL)
    return jax.shard_map(
        on_device,
        mesh=torus,
        in_specs=(P(ALL, None), P(), P(ALL)),
        out_specs=(P(ALL), P(ALL, None), P()),
        check_vma=False,
    )
```

profile of v0, /device:TPU:1, one launch (start us, length us, event | category | flops | bytes accessed | tf_op | source)
XLA Modules:
  0.0 142.7 jit_solution(3670881064424863106)
XLA Ops:
  0.6 0.0 copy-start
  0.6 1.7 %copy-done = bf16[1536,768]{1,0:T(8,128)(2,1)S(1)} copy-done((bf16[1536,768]{1,0:T(8,128)(2,1)S(1)}, bf16[1536,768]{1,0:T(8,128)(2,1)}, u32[]{:S(2)}) %copy-start) | copy-done | bytes 2359320
  2.3 2.9 %multiply_reduce_fusion.1 = (f32[512]{0:T(512)S(1)}, f32[512,768]{1,0:T(8,128)S(1)}) fusion(bf16[512,1536]{1,0:T(8,128)(2,1)} %param.3, bf16[1536,768]{1,0:T(8,128)(2,1)S(1)} %copy-done), kind=kOutput, calls=%fused_computation.6 | convolution fusion | flops 1208745472 | bytes 5507072 | tf_op jit(solution)/shard_map/dot_general | solution.py:25
  5.2 0.2 fusion.57
  5.4 0.0 copy-start.6
  5.4 2.1 %collective-permute-start.1 = (bf16[512,768]{1,0:T(8,128)(2,1)S(1)}, bf16[512,768]{1,0:T(8,128)(2,1)}, u32[]{:S(2)}, u32[]{:S(2)}) collective-permute-start(bf16[512,768]{1,0:T(8,128)(2,1)S(1)} %fusion.57), channel_id=1, source_target_pairs={{0,254},{1,3},{2,0},{3,5},{4,2},{5,7},{6,4},{7,9},{8,6},{9,11},{10... | collective-permute-start | bytes 2359304 | tf_op jit(solution)/shard_map/ppermute | solution.py:13
  7.5 9.9 %collective-permute-start.3 = (bf16[512,768]{1,0:T(8,128)(2,1)S(1)}, bf16[512,768]{1,0:T(8,128)(2,1)}, u32[]{:S(2)}, u32[]{:S(2)}) collective-permute-start(bf16[512,768]{1,0:T(8,128)(2,1)S(1)} %fusion.57), channel_id=1, source_target_pairs={{0,2},{1,255},{2,4},{3,1},{4,6},{5,3},{6,8},{7,5},{8,10},{9,7},{10... | collective-permute-start | bytes 2359304 | tf_op jit(solution)/shard_map/ppermute | solution.py:13
  17.4 0.1 collective-permute-start
  17.5 0.6 convolution_multiply_fusion.4
  18.1 8.2 %collective-permute-done.1 = bf16[512,768]{1,0:T(8,128)(2,1)} collective-permute-done((bf16[512,768]{1,0:T(8,128)(2,1)S(1)}, bf16[512,768]{1,0:T(8,128)(2,1)}, u32[]{:S(2)}, u32[]{:S(2)}) %collective-permute-start.1) | collective-permute-done | bytes 786464 | tf_op jit(solution)/shard_map/ppermute | solution.py:13
  26.3 8.8 %collective-permute-start.2 = (bf16[512,768]{1,0:T(8,128)(2,1)}, bf16[512,768]{1,0:T(8,128)(2,1)S(1)}, u32[]{:S(2)}, u32[]{:S(2)}) collective-permute-start(bf16[512,768]{1,0:T(8,128)(2,1)} %collective-permute-done.1), channel_id=1, source_target_pairs={{0,1},{1,0},{2,3},{3,2},{4,5},{5,4},{6,7},{7,6},{8,9},{9,8},{10,11... | collective-permute-start | bytes 2359304 | tf_op jit(solution)/shard_map/ppermute | solution.py:13
  35.1 1.7 %convolution_multiply_fusion.2 = f32[512,512]{0,1:T(8,128)S(1)} fusion(bf16[512,768]{1,0:T(8,128)(2,1)S(1)} %fusion.57, bf16[512,768]{1,0:T(8,128)(2,1)} %collective-permute-done.1), kind=kOutput, calls=%fused_computation.9 | convolution fusion | flops 402915328 | bytes 2621440 | tf_op jit(solution)/shard_map/dot_general | solution.py:29
  36.9 1.7 %convolution_multiply_fusion = f32[512,512]{0,1:T(8,128)S(1)} fusion(bf16[512,768]{1,0:T(8,128)(2,1)S(1)} %fusion.57, bf16[512,768]{1,0:T(8,128)(2,1)} %collective-permute-done.3), kind=kOutput, calls=%fused_computation.7 | convolution fusion | flops 402915328 | bytes 2621440 | tf_op jit(solution)/shard_map/dot_general | solution.py:29
  38.6 0.6 convolution_multiply_fusion.1
  39.3 0.0 copy-start.5
  39.3 3.2 %exponential_reduce_fusion.3 = (f32[512]{0:T(512)S(1)}, f32[512]{0:T(512)S(1)}, f32[512]{0:T(512)S(1)}, f32[512]{0:T(512)S(1)}, f32[512]{0:T(512)S(1)}, /*index=...) fusion(s32[512]{0:T(512)S(1)} %get-tuple-element.32, ...), kind=kOutput, calls=%fused_computation.51 | convolution fusion | flops 408677376 | bytes 6846464 | tf_op jit(solution)/shard_map/dot_general | solution.py:29
  42.5 0.1 collective-permute-start.4
  42.6 0.9 constant_dynamic-slice_fusion
  43.5 0.5 collective-permute-start.7
  44.1 0.1 collective-permute-start.6
  44.1 0.9 fusion.19
  45.1 8.0 %collective-permute-start.5 = (f32[4,512]{1,0:T(4,128)S(1)}, f32[4,512]{1,0:T(4,128)S(1)}, u32[]{:S(2)}, u32[]{:S(2)}) collective-permute-start(f32[4,512]{1,0:T(4,128)S(1)} %pad_maximum_fusion.1), channel_id=1, source_target_pairs={{0,254},{1,255},{2,0},{3,1},{4,2},{5,3},{6,4},{7,5},{8,6},{9,7},{1... | collective-permute-start | bytes 24584 | tf_op jit(solution)/shard_map/ppermute | solution.py:13
  53.1 0.8 collective-permute-done.5
  53.8 2.1 %fusion.20 = f32[512,768]{1,0:T(8,128)S(1)} fusion(bf16[512,768]{1,0:T(8,128)(2,1)} %collective-permute-done.3, f32[512,512]{0,1:T(8,128)S(1)} %convolution_multiply_fusion, s32[512]{0:T(512)S(1)} %bitcast.47, f32[512]{0:T(512)S(1)} %bitcast.49, f32[512]{0:T(512)S(1)} %get-tuple-element.13, s32[512]{0:T(512)S(1)} %get-tuple-element.32, s32[512]{0:T(512)S(1)} %iota_add_fusion), kind=kOutput, calls=%fused_computation.57 | convolution fusion | flops 405012480 | bytes 3418112 | tf_op jit(solution)/shard_map/dot_general | solution.py:25
  56.0 2.1 %fusion.23 = f32[512,768]{1,0:T(8,128)S(1)} fusion(bf16[512,768]{1,0:T(8,128)(2,1)} %collective-permute-done.1, f32[512,512]{0,1:T(8,128)S(1)} %convolution_multiply_fusion.2, s32[512]{0:T(512)S(1)} %bitcast.45, f32[512]{0:T(512)S(1)} %bitcast.48, f32[512]{0:T(512)S(1)} %get-tuple-element.13, s32[512]{0:T(512)S(1)} %get-tuple-element.32, ...), kind=kOutput, calls=%fused_computation.58 | convolution fusion | flops 405012480 | bytes 3418112 | tf_op jit(solution)/shard_map/dot_general | solution.py:25
  58.1 0.0 copy-start.2
  58.1 2.2 %fusion.25 = f32[512,768]{1,0:T(8,128)S(1)} fusion(bf16[512,768]{1,0:T(8,128)(2,1)} %collective-permute-done, f32[512,512]{0,1:T(8,128)S(1)} %get-tuple-element.43, s32[512]{0:T(512)S(1)} %bitcast.44, f32[512]{0:T(512)S(1)} %bitcast.46, f32[512]{0:T(512)S(1)} %get-tuple-element.13, s32[512]{0:T(512)S(1)} %get-tuple-element.32, s32[512]{0:T(512)S(1)} %iota_add_fusion.3), kind=kOutput, calls=%fused_computation.59 | convolution fusion | flops 405012480 | bytes 3418112 | tf_op jit(solution)/shard_map/dot_general | solution.py:25
  60.3 1.5 %multiply_reduce_fusion = (f32[512]{0:T(512)S(1)}, f32[512,768]{1,0:T(8,128)S(1)}) fusion(f32[512,768]{1,0:T(8,128)S(1)} %copy-done.2, f32[512]{0:T(512)S(1)} %add_sqrt_fusion, f32[512,768]{1,0:T(8,128)S(1)} %fusion.20, bf16[512,768]{1,0:T(8,128)(2,1)S(1)} %collective-permute-done.2, f32[512,512]{0,1:T(8,128)S(1)} %convolution_multiply_fusion.1, ...), kind=kOutput, calls=%fused_computation.4 | convolution fusion | flops 408157696 | bytes 11286528 | tf_op jit(solution)/shard_map/dot_general | solution.py:25
  61.9 0.3 divide_convert_fusion
  62.2 0.0 copy-start.3
  62.2 1.0 collective-permute-start.8
  63.2 1.9 %fusion.17 = f32[768,768]{1,0:T(8,128)S(1)} fusion(bf16[512,768]{1,0:T(8,128)(2,1)S(1)} %divide_convert_fusion, bf16[512,1536]{1,0:T(8,128)(2,1)} %param.3, s32[]{:T(128)S(6)} %select_n.156), kind=kOutput, calls=%fused_computation.53 | convolution fusion | flops 603979776 | bytes 3932164 | tf_op jit(solution)/shard_map/dot_general | solution.py:33
  65.1 0.1 collective-permute-done.8
  65.2 2.2 %add_convert_fusion = bf16[768,768]{1,0:T(8,128)(2,1)S(1)} fusion(f32[768,768]{1,0:T(8,128)S(1)} %fusion.17, bf16[512,768]{1,0:T(8,128)(2,1)} %collective-permute-done.7, bf16[512,768]{1,0:T(8,128)(2,1)} %collective-permute-done.8), kind=kOutput, calls=%fused_computation.2 | convolution fusion | flops 605159424 | bytes 5111808 | tf_op jit(solution)/shard_map/dot_general | solution.py:33
  67.5 20.9 %all_to_all.20 = bf16[16,48,768]{2,1,0:T(8,128)(2,1)S(1)} all-to-all(bf16[16,48,768]{2,1,0:T(8,128)(2,1)S(1)} %bitcast.37), channel_id=1, replica_groups=mesh['z'=8,'y'=4,'x'=4,'core'=2] {'y','x'}, dimensions={0} | all-to-all | bytes 2359296 | tf_op jit(solution)/shard_map/all_to_all | solution.py:39
  88.4 0.8 reduce_sum.144
  89.2 0.9 reshape.97
  90.1 14.7 %all_to_all.21 = bf16[8,6,768]{2,1,0:T(8,128)(2,1)S(1)} all-to-all(bf16[8,6,768]{2,1,0:T(8,128)(2,1)S(1)} %reshape.97), channel_id=1, replica_groups=mesh['z'=8,'y'=4,'x'=4,'core'=2] {'z'}, dimensions={0} | all-to-all | bytes 147456 | tf_op jit(solution)/shard_map/all_to_all | solution.py:39
  104.8 10.1 %all_to_all.22 = bf16[8,6,768]{2,1,0:T(8,128)(2,1)S(1)} all-to-all(bf16[8,6,768]{2,1,0:T(8,128)(2,1)S(1)} %broadcast_in_dim.20), channel_id=1, replica_groups=mesh['z'=8,'y'=4,'x'=4,'core'=2] {'z'}, dimensions={0} | all-to-all | bytes 147456 | tf_op jit(solution)/shard_map/all_to_all | solution.py:46
  114.9 0.0 copy-start.7
  114.9 0.0 copy-start.4
  114.9 0.1 broadcast_in_dim.22
  115.0 17.8 %all_to_all.23 = bf16[16,48,768]{2,1,0:T(8,128)(2,1)S(1)} all-to-all(bf16[16,48,768]{2,1,0:T(8,128)(2,1)S(1)} %broadcast_in_dim.22), channel_id=1, replica_groups=mesh['z'=8,'y'=4,'x'=4,'core'=2] {'y','x'}, dimensions={0} | all-to-all | bytes 2359296 | tf_op jit(solution)/shard_map/all_to_all | solution.py:46
  132.8 5.0 %collective-permute-start.9 = (bf16[768,768]{1,0:T(8,128)(2,1)S(1)}, bf16[768,768]{1,0:T(8,128)(2,1)S(1)}, u32[]{:S(2)}, u32[]{:S(2)}) collective-permute-start(bf16[768,768]{1,0:T(8,128)(2,1)S(1)} %bitcast.36), channel_id=1, source_target_pairs={{0,1},{1,0},{2,3},{3,2},{4,5},{5,4},{6,7},{7,6},{8,9},{9,8},{10,11... | collective-permute-start | bytes 3538952 | tf_op jit(solution)/shard_map/ppermute | solution.py:13
  137.8 0.6 add_subtract_fusion
  138.4 2.6 %convolution_convert_fusion = bf16[512,1536]{1,0:T(8,128)(2,1)} fusion(bf16[512,768]{1,0:T(8,128)(2,1)S(1)} %copy-done.4, bf16[1536,768]{1,0:T(8,128)(2,1)S(1)} %copy-done), kind=kOutput, calls=%fused_computation | convolution fusion | flops 1208745984 | bytes 4718592 | tf_op jit(solution)/shard_map/dot_general | solution.py:29
  141.0 0.2 broadcast_select_fusion.1
  141.2 1.6 %pad_maximum_fusion = bf16[1536,768]{1,0:T(8,128)(2,1)} fusion(bf16[768,768]{1,0:T(8,128)(2,1)S(1)} %get-tuple-element.16, bf16[768,768]{1,0:T(8,128)(2,1)S(1)} %get-tuple-element.15), kind=kLoop, calls=%fused_computation.1 | loop fusion | flops 4718592 | bytes 4718592 | tf_op jit(solution)/shard_map/concatenate | solution.py:117
  (33 shorter events, 0.2 us)
Async XLA Ops:
  0.6 1.7 %copy-start = (bf16[1536,768]{1,0:T(8,128)(2,1)S(1)}, bf16[1536,768]{1,0:T(8,128)(2,1)}, u32[]{:S(2)}) copy-start(bf16[1536,768]{1,0:T(8,128)(2,1)} %param.4) | copy-start | bytes 7077892
  5.2 2.3 %copy-start.1 = (f32[512,768]{1,0:T(8,128)}, f32[512,768]{1,0:T(8,128)S(1)}, u32[]{:S(2)}) copy-start(f32[512,768]{1,0:T(8,128)S(1)} %get-tuple-element.42) | copy-start | bytes 4718596
  5.4 29.8 %copy-start.6 = (s32[512]{0:T(512)S(1)}, s32[512]{0:T(512)}, u32[]{:S(2)}) copy-start(s32[512]{0:T(512)} %param.5) | copy-start | bytes 6148
  5.4 21.0 %collective-permute-start.1 = (bf16[512,768]{1,0:T(8,128)(2,1)S(1)}, bf16[512,768]{1,0:T(8,128)(2,1)}, u32[]{:S(2)}, u32[]{:S(2)}) collective-permute-start(bf16[512,768]{1,0:T(8,128)(2,1)S(1)} %fusion.57), channel_id=1, source_target_pairs={{0,254},{1,3},{2,0},{3,5},{4,2},{5,7},{6,4},{7,9},{8,6},{9,11},{10... | collective-permute-start | bytes 2359304 | tf_op jit(solution)/shard_map/ppermute | solution.py:13
  7.5 29.4 %collective-permute-start.3 = (bf16[512,768]{1,0:T(8,128)(2,1)S(1)}, bf16[512,768]{1,0:T(8,128)(2,1)}, u32[]{:S(2)}, u32[]{:S(2)}) collective-permute-start(bf16[512,768]{1,0:T(8,128)(2,1)S(1)} %fusion.57), channel_id=1, source_target_pairs={{0,2},{1,255},{2,4},{3,1},{4,6},{5,3},{6,8},{7,5},{8,10},{9,7},{10... | collective-permute-start | bytes 2359304 | tf_op jit(solution)/shard_map/ppermute | solution.py:13
  17.4 21.9 %collective-permute-start = (bf16[512,768]{1,0:T(8,128)(2,1)S(1)}, bf16[512,768]{1,0:T(8,128)(2,1)}, u32[]{:S(2)}, u32[]{:S(2)}) collective-permute-start(bf16[512,768]{1,0:T(8,128)(2,1)S(1)} %fusion.57), channel_id=1, source_target_pairs={{0,1},{1,0},{2,3},{3,2},{4,5},{5,4},{6,7},{7,6},{8,9},{9,8},{10,11... | collective-permute-start | bytes 2359304 | tf_op jit(solution)/shard_map/ppermute | solution.py:13
  26.3 12.3 %collective-permute-start.2 = (bf16[512,768]{1,0:T(8,128)(2,1)}, bf16[512,768]{1,0:T(8,128)(2,1)S(1)}, u32[]{:S(2)}, u32[]{:S(2)}) collective-permute-start(bf16[512,768]{1,0:T(8,128)(2,1)} %collective-permute-done.1), channel_id=1, source_target_pairs={{0,1},{1,0},{2,3},{3,2},{4,5},{5,4},{6,7},{7,6},{8,9},{9,8},{10,11... | collective-permute-start | bytes 2359304 | tf_op jit(solution)/shard_map/ppermute | solution.py:13
  39.3 3.3 %copy-start.5 = (bf16[512,1536]{1,0:T(8,128)(2,1)S(1)}, bf16[512,1536]{1,0:T(8,128)(2,1)}, u32[]{:S(2)}) copy-start(bf16[512,1536]{1,0:T(8,128)(2,1)} %param.3) | copy-start | bytes 4718596
  42.5 1.5 %collective-permute-start.4 = (f32[2,512]{1,0:T(2,128)S(1)}, f32[2,512]{1,0:T(2,128)S(1)}, u32[]{:S(2)}, u32[]{:S(2)}) collective-permute-start(f32[2,512]{1,0:T(2,128)S(1)} %pad_maximum_fusion.2), channel_id=1, source_target_pairs={{0,1},{1,0},{2,3},{3,2},{4,5},{5,4},{6,7},{7,6},{8,9},{9,8},{10,11... | collective-permute-start | bytes 12296 | tf_op jit(solution)/shard_map/ppermute | solution.py:13
  43.5 21.6 %collective-permute-start.7 = (bf16[512,768]{1,0:T(8,128)(2,1)}, bf16[512,768]{1,0:T(8,128)(2,1)}, u32[]{:S(2)}, u32[]{:S(2)}) collective-permute-start(bf16[512,768]{1,0:T(8,128)(2,1)} %constant_dynamic-slice_fusion), channel_id=1, source_target_pairs={{0,1},{1,0},{2,3},{3,2},{4,5},{5,4},{6,7},{7,6},{8,9},{9,8},{10,11... | collective-permute-start | bytes 2359304 | tf_op jit(solution)/shard_map/ppermute | solution.py:13
  44.1 9.0 %collective-permute-start.6 = (f32[4,512]{1,0:T(4,128)S(1)}, f32[4,512]{1,0:T(4,128)S(1)}, u32[]{:S(2)}, u32[]{:S(2)}) collective-permute-start(f32[4,512]{1,0:T(4,128)S(1)} %pad_maximum_fusion.1), channel_id=1, source_target_pairs={{0,2},{1,3},{2,4},{3,5},{4,6},{5,7},{6,8},{7,9},{8,10},{9,11},{10,... | collective-permute-start | bytes 24584 | tf_op jit(solution)/shard_map/ppermute | solution.py:13
  45.1 8.8 %collective-permute-start.5 = (f32[4,512]{1,0:T(4,128)S(1)}, f32[4,512]{1,0:T(4,128)S(1)}, u32[]{:S(2)}, u32[]{:S(2)}) collective-permute-start(f32[4,512]{1,0:T(4,128)S(1)} %pad_maximum_fusion.1), channel_id=1, source_target_pairs={{0,254},{1,255},{2,0},{3,1},{4,2},{5,3},{6,4},{7,5},{8,6},{9,7},{1... | collective-permute-start | bytes 24584 | tf_op jit(solution)/shard_map/ppermute | solution.py:13
  58.1 2.3 %copy-start.2 = (f32[512,768]{1,0:T(8,128)S(1)}, f32[512,768]{1,0:T(8,128)}, u32[]{:S(2)}) copy-start(f32[512,768]{1,0:T(8,128)} %copy-done.1) | copy-start | bytes 4718596
  62.2 2.9 %copy-start.3 = (bf16[512,768]{1,0:T(8,128)(2,1)}, bf16[512,768]{1,0:T(8,128)(2,1)S(1)}, u32[]{:S(2)}) copy-start(bf16[512,768]{1,0:T(8,128)(2,1)S(1)} %divide_convert_fusion) | copy-start | bytes 2359300
  62.2 3.0 %collective-permute-start.8 = (bf16[512,768]{1,0:T(8,128)(2,1)S(1)}, bf16[512,768]{1,0:T(8,128)(2,1)}, u32[]{:S(2)}, u32[]{:S(2)}) collective-permute-start(bf16[512,768]{1,0:T(8,128)(2,1)S(1)} %divide_convert_fusion), channel_id=1, source_target_pairs={{0,1},{1,0},{2,3},{3,2},{4,5},{5,4},{6,7},{7,6},{8,9},{9,8},{10,11... | collective-permute-start | bytes 2359304 | tf_op jit(solution)/shard_map/ppermute | solution.py:13
  114.9 22.9 %copy-start.7 = (f32[512]{0:T(512)S(1)}, f32[512]{0:T(512)}, u32[]{:S(2)}) copy-start(f32[512]{0:T(512)} %get-tuple-element.37) | copy-start | bytes 6148
  114.9 22.9 %copy-start.8 = (f32[512]{0:T(512)S(1)}, f32[512]{0:T(512)}, u32[]{:S(2)}) copy-start(f32[512]{0:T(512)} %get-tuple-element.39) | copy-start | bytes 6148
  114.9 23.4 %copy-start.4 = (bf16[512,768]{1,0:T(8,128)(2,1)S(1)}, bf16[512,768]{1,0:T(8,128)(2,1)}, u32[]{:S(2)}) copy-start(bf16[512,768]{1,0:T(8,128)(2,1)} %copy-done.3) | copy-start | bytes 2359300
  132.8 8.2 %collective-permute-start.9 = (bf16[768,768]{1,0:T(8,128)(2,1)S(1)}, bf16[768,768]{1,0:T(8,128)(2,1)S(1)}, u32[]{:S(2)}, u32[]{:S(2)}) collective-permute-start(bf16[768,768]{1,0:T(8,128)(2,1)S(1)} %bitcast.36), channel_id=1, source_target_pairs={{0,1},{1,0},{2,3},{3,2},{4,5},{5,4},{6,7},{7,6},{8,9},{9,8},{10,11... | collective-permute-start | bytes 3538952 | tf_op jit(solution)/shard_map/ppermute | solution.py:13
where the time goes:
time: 143 us
  blocking collectives  63.4 us (44%)
  starting transfers between devices  35.5 us (25%)
  matrix products  26.4 us (18%)
  waiting for transfers between devices  9.1 us (6%)
  other arithmetic  3.78 us (3%)
  local copies, waits for them, and re-layouts  3.68 us (3%)
    all_to_all x2, blocking collectives, scatter_sum(): got = lax.all_to_all(shares, axes, split_axis=0, concat_axis=0)  35.6 us
    ppermute x10, starting transfers between devices, send(): return lax.ppermute(x, ALL, [(i, to(i) % 256) for i in range(256)])  35.5 us
    all_to_all x2, blocking collectives, gather(): got = lax.all_to_all(copies, axes, split_axis=0, concat_axis=0)  27.8 us
    dot_general x6, matrix products, dot(): return jnp.dot(left, right, preferred_element_type=F32)  11.8 us
    dot_general x6, matrix products, dot_nt(): lax.dot_general(left, right, (((1,), (1,)), ((), ())), preferred_element_...  10.4 us
    ppermute x10, waiting for transfers between devices, send(): return lax.ppermute(x, ALL, [(i, to(i) % 256) for i in range(256)])  9.1 us
    dot_general x2, matrix products, dot_tn(): lax.dot_general(left, right, (((0,), (0,)), ((), ())), preferred_element_...  4.15 us
  transfers between devices with their start and end apart: 10, of which 3 were waited for; matrix products, arithmetic and copies ran while one was open for 14% of the time, Pallas kernels for 0%

commit v1 on v0

v1 whole, which is shorter than its diff:
```python
import jax
import jax.numpy as jnp
from jax import lax
from jax.experimental import pallas as pl
from jax.experimental.pallas import tpu as pltpu
from jax.sharding import Mesh, PartitionSpec as P

SCALE = 50.0
ALL = ("z", "y", "x", "core")
SIZES = (8, 4, 4, 2)
F32, BF16 = jnp.float32, jnp.bfloat16
TILE = 128


def send(x, to):
    return lax.ppermute(x, ALL, [(i, to(i) % 256) for i in range(256)])


def in_chip(x):
    return send(x, lambda i: i ^ 1)


def inward(x):
    return send(x, lambda i: i - 2 if i % 2 == 0 else i + 2)


def outward(x):
    return send(x, lambda i: i + 2 if i % 2 == 0 else i - 2)


def dot(left, right):
    return jnp.dot(left, right, preferred_element_type=F32)


def dot_nt(left, right):
    return lax.dot_general(left, right, (((1,), (1,)), ((), ())), preferred_element_type=F32)


def to_row(column):
    return jnp.broadcast_to(column, (column.shape[0], 128)).T[:1]


def to_column(row):
    return jnp.broadcast_to(row, (128, row.shape[1])).T[:, :1]


def call(body, out, scalars, *arrays, scratch=(), flops=0, name=None):
    vmem = pl.BlockSpec(memory_space=pltpu.VMEM)
    smem = pl.BlockSpec(memory_space=pltpu.SMEM)
    size = sum(a.size * a.dtype.itemsize for a in (*arrays, *out))
    specs = [smem] * len(scalars) + [vmem] * len(arrays)
    return pl.pallas_call(
        body,
        out_shape=out,
        in_specs=specs,
        out_specs=[vmem] * len(out),
        scratch_shapes=scratch,
        name=name,
        compiler_params=pltpu.CompilerParams(vmem_limit_bytes=16 * 2**20),
        cost_estimate=pl.CostEstimate(flops=flops, bytes_accessed=size, transcendentals=0),
    )(*scalars, *arrays)


def after(x, *others):
    anywhere = pl.BlockSpec(memory_space=pl.ANY)
    return pl.pallas_call(
        lambda *refs: None,
        out_shape=jax.ShapeDtypeStruct(x.shape, x.dtype),
        in_specs=[anywhere] * (1 + len(others)),
        out_specs=anywhere,
        input_output_aliases={0: 0},
        name="after",
        compiler_params=pltpu.CompilerParams(vmem_limit_bytes=2**20),
    )(x, *others)


def embed(frames, head, emb, unit, rnorm, acc):
    k = pl.program_id(0)

    @pl.when(k == 0)
    def _():
        acc[...] = dot(frames[...], head[...])

    @pl.when(k > 0)
    def _():
        acc[...] += dot(frames[...], head[...])

    @pl.when(k == pl.num_programs(0) - 1)
    def _():
        for r in range(0, acc.shape[0], TILE):
            rows = pl.ds(r, TILE)
            z = acc[rows, :]
            norm = jnp.sqrt(jnp.sum(z * z, axis=1, keepdims=True) + 1e-06)
            inverse = 1.0 / norm
            u = z * inverse
            unit[rows, :] = u
            emb[rows, :] = u.astype(BF16)
            rnorm[rows, :] = inverse


def score_tile(at, emb, block, goal, rows):
    score = SCALE * dot_nt(emb[rows, :], block[...])
    cols = lax.broadcasted_iota(jnp.int32, score.shape, 1) + at * block.shape[0]
    hit = cols == goal[rows, :]
    return score, jnp.sum(jnp.where(hit, score, 0.0), axis=1, keepdims=True)


def near(at, emb, peer, goal, e_own, e_peer, total, pos):
    for r in range(0, emb.shape[0], TILE):
        rows = pl.ds(r, TILE)
        score, p0 = score_tile(0, emb, emb, goal, rows)
        e = jnp.exp(score)
        i = lax.broadcasted_iota(jnp.int32, e.shape, 0) + r
        e = jnp.where(i == lax.broadcasted_iota(jnp.int32, e.shape, 1), 0.0, e)
        e_own[rows, :] = e
        t0 = jnp.sum(e, axis=1, keepdims=True)
        score, p1 = score_tile(at[0], emb, peer, goal, rows)
        e = jnp.exp(score)
        e_peer[rows, :] = e
        total[rows, :] = t0 + jnp.sum(e, axis=1, keepdims=True)
        pos[rows, :] = p0 + p1


def across(at, emb, block, goal, total, pos, e_out, total_out, pos_out, column_sum):
    columns = jnp.zeros((1, block.shape[0]), F32)
    for r in range(0, emb.shape[0], TILE):
        rows = pl.ds(r, TILE)
        score, p = score_tile(at[0], emb, block, goal, rows)
        e = jnp.exp(score)
        e_out[rows, :] = e
        total_out[rows, :] = total[rows, :] + jnp.sum(e, axis=1, keepdims=True)
        pos_out[rows, :] = pos[rows, :] + p
        columns += jnp.sum(e, axis=0, keepdims=True)
    column_sum[...] = columns


def relayed(at, emb, block, goal, total, pos, e_out, total_out, pos_out):
    for r in range(0, emb.shape[0], TILE):
        rows = pl.ds(r, TILE)
        score, p = score_tile(at[0], emb, block, goal, rows)
        e = jnp.exp(score)
        e_out[rows, :] = e
        total_out[rows, :] = total[rows, :] + jnp.sum(e, axis=1, keepdims=True)
        pos_out[rows, :] = pos[rows, :] + p


def close(total, last_sum, goal_row, inverse, note, log_total):
    whole = to_row(total[...]) + last_sum[...]
    inv = 1.0 / whole
    note[0:1, :] = inv
    note[1:2, :] = goal_row[...].astype(F32)
    inverse[...] = to_column(inv)
    log_total[...] = jnp.log(whole)


def slope(e, at, goal, inverse, their_inverse, their_goal, rows):
    width = e.shape[1]
    i = lax.broadcasted_iota(jnp.int32, e.shape, 0) + rows.start
    j = lax.broadcasted_iota(jnp.int32, e.shape, 1) + at * width
    ours = (j == goal[rows, :]).astype(F32)
    theirs = (i == their_goal + at * width).astype(F32)
    return e * (inverse[rows, :] + their_inverse) - ours - theirs


def gather_slopes(
    at, goal, inverse, own_note, peer_note, first_note, relay_note, e0, e1, e2, e3, b0, b1, b2, b3, out, g
):
    notes = (own_note, peer_note, first_note, relay_note)
    for k, (note, e, block) in enumerate(zip(notes, (e0, e1, e2, e3), (b0, b1, b2, b3))):
        place = 0 if k == 0 else at[k - 1]
        their_inverse, their_goal = note[0:1, :], note[1:2, :].astype(jnp.int32)
        for r in range(0, e.shape[0], TILE):
            rows = pl.ds(r, TILE)
            g[rows, :] = slope(e[rows, :], place, goal, inverse, their_inverse, their_goal, rows).astype(BF16)
        if k == 0:
            out[...] = dot(g[...], block[...])
        else:
            out[...] += dot(g[...], block[...])


def finish(
    at, emb, block, goal, inverse, note, pos, log_total, unit, rnorm, part, dz, losses, g, pos_all
):
    their_inverse, their_goal = note[0:1, :], note[1:2, :].astype(jnp.int32)
    for r in range(0, emb.shape[0], TILE):
        rows = pl.ds(r, TILE)
        score, p = score_tile(at[0], emb, block, goal, rows)
        pos_all[rows, :] = pos[rows, :] + p
        g[rows, :] = slope(jnp.exp(score), at[0], goal, inverse, their_inverse, their_goal, rows).astype(BF16)
    for r in range(0, emb.shape[0], 256):
        rows = pl.ds(r, 256)
        demb = SCALE * (part[rows, :] + dot(g[rows, :], block[...]))
        u = unit[rows, :]
        along = jnp.sum(u * demb, axis=1, keepdims=True)
        dz[rows, :] = ((demb - u * along) * rnorm[rows, :]).astype(BF16)
    losses[...] = log_total[...] - to_row(pos_all[...])


def turn(core, frames, mine, theirs):
    half = mine.shape[0]
    for out, k in ((mine, core[0]), (theirs, 1 - core[0])):
        for c in range(0, half, 256):
            columns = pl.ds(pl.multiple_of(k * half + c, 128), 256)
            out[pl.ds(c, 256), :] = frames[:, columns].T


def head_own(left, dz, out):
    out[...] = dot(left[...], dz[...])


def head_both(part, left, dz, out):
    for r in range(0, out.shape[0], 256):
        rows = pl.ds(r, 256)
        out[rows, :] = (part[rows, :] + dot(left[rows, :], dz[...])).astype(BF16)


def lay_out(core, own, other, out, sems):
    half = own.shape[0]
    copies = []
    for k, src in enumerate((own, other)):
        start = pl.multiple_of((core[0] if k == 0 else 1 - core[0]) * half, half)
        copies.append(pltpu.make_async_copy(src, out.at[pl.ds(start, half), :], sems.at[k]))
    for c in copies:
        c.start()
    for c in copies:
        c.wait()


def on_device(frames, head, offsets):
    rows, depth = frames.shape
    width = head.shape[1]
    core = lax.axis_index("core")
    even = core == 0
    shape = jax.ShapeDtypeStruct
    col, row = shape((rows, 1), F32), shape((1, rows), F32)
    square, tall = shape((rows, rows), F32), shape((rows, width), F32)
    note = shape((2, rows), F32)
    block_flops = 2 * rows * rows * width
    step, half = depth // 3, depth // 2
    emb, unit, rnorm = pl.pallas_call(
        embed,
        grid=(3,),
        in_specs=[
            pl.BlockSpec((rows, step), lambda k: (0, k)),
            pl.BlockSpec((step, width), lambda k: (k, 0)),
        ],
        out_specs=[pl.BlockSpec(memory_space=pltpu.VMEM)] * 3,
        out_shape=[shape((rows, width), BF16), tall, col],
        scratch_shapes=[pltpu.VMEM((rows, width), F32)],
        name="embed",
        compiler_params=pltpu.CompilerParams(vmem_limit_bytes=16 * 2**20),
        cost_estimate=pl.CostEstimate(flops=2 * rows * depth * width, bytes_accessed=2**22, transcendentals=0),
    )(frames, head)

    target = jnp.arange(rows, dtype=jnp.int32) + offsets
    goal, goal_row = target[:, None], target[None, :]
    sign = jnp.where(even, 1, -1).astype(jnp.int32)

    def at(k):
        return (sign * k).reshape(1)

    peer = in_chip(emb)
    first = inward(emb)
    e_own, e_peer, total, pos = call(
        near, [square, square, col, col], [at(1)], emb, peer, goal, flops=2 * block_flops, name="near"
    )
    mine, theirs = call(turn, [shape((half, rows), BF16)] * 2, [core.reshape(1)], frames, name="turn")
    emb = after(emb, total)
    last = outward(emb)
    first = after(first, total, theirs)
    relay = in_chip(first)
    theirs = in_chip(theirs)
    e_first, total, pos, column_sum = call(
        across, [square, col, col, row], [at(2)], emb, first, goal, total, pos, flops=block_flops, name="across"
    )
    last_sum = outward(column_sum)
    e_relay, total, pos = call(
        relayed, [square, col, col], [at(-1)], emb, relay, goal, total, pos, flops=block_flops, name="relayed"
    )
    inverse, own_note, log_total = call(close, [col, note, row], [], total, last_sum, goal_row, name="close")
    peer_note = in_chip(own_note)
    first_note = inward(own_note)
    both = outward(jnp.concatenate([own_note, peer_note], axis=0))
    last_note, relay_note = both[:2], both[2:]
    places = jnp.concatenate([at(1), at(2), at(-1)])
    (part,) = call(
        gather_slopes, [tall], [places], goal, inverse, own_note, peer_note, first_note, relay_note,
        e_own, e_peer, e_first, e_relay, emb, peer, first, relay,
        scratch=[pltpu.VMEM((rows, rows), BF16)], flops=4 * block_flops, name="slopes",
    )
    dz, losses = call(
        finish, [shape((rows, width), BF16), row], [at(-2)], emb, last, goal, inverse, last_note, pos, log_total,
        unit, rnorm, part, scratch=[pltpu.VMEM((rows, rows), BF16), pltpu.VMEM((rows, 1), F32)],
        flops=2 * block_flops, name="finish",
    )
    dz_other = in_chip(dz)
    frame_grad = dot_nt(dz, head).astype(BF16)

    (partial,) = call(head_own, [shape((half, width), F32)], [], mine, dz, flops=2 * half * rows * width, name="head_own")
    (partial,) = call(
        head_both, [shape((half, width), BF16)], [], partial, theirs, dz_other, flops=2 * half * rows * width, name="head_both"
    )
    shares = partial.reshape(16, half // 16, width)
    got = lax.all_to_all(shares, ("y", "x"), split_axis=0, concat_axis=0)
    share = jnp.sum(got.astype(F32), axis=0).astype(BF16)
    got = lax.all_to_all(jnp.broadcast_to(share[None], (8,) + share.shape), "z", split_axis=0, concat_axis=0)
    share = jnp.sum(got.astype(F32), axis=0).astype(BF16)
    copies = jnp.broadcast_to(share[None], (16,) + share.shape)
    own = lax.all_to_all(copies, ("y", "x"), split_axis=0, concat_axis=0).reshape(half, width)
    other = in_chip(own)
    anywhere = pl.BlockSpec(memory_space=pl.ANY)
    head_grad = pl.pallas_call(
        lay_out,
        out_shape=shape((depth, width), BF16),
        in_specs=[pl.BlockSpec(memory_space=pltpu.SMEM), anywhere, anywhere],
        out_specs=anywhere,
        scratch_shapes=[pltpu.SemaphoreType.DMA((2,))],
        name="lay_out",
        compiler_params=pltpu.CompilerParams(vmem_limit_bytes=2**20),
    )(core.reshape(1), own, other)
    return (losses.reshape(rows), frame_grad, head_grad)


def solution(mesh):
    torus = Mesh(mesh.devices.reshape(SIZES), ALL)
    return jax.shard_map(
        on_device,
        mesh=torus,
        in_specs=(P(ALL, None), P(), P(ALL)),
        out_specs=(P(ALL), P(ALL, None), P()),
        check_vma=False,
    )
```

time: 143 us -> 148 us (1.035)
  matrix products: 26.4 us -> 2.57 us
  Pallas kernels: 0 us -> 21.4 us
  waiting for transfers between devices: 9.1 us -> 26.4 us
  starting transfers between devices: 35.5 us -> 23.4 us
  local copies, waits for them, and re-layouts: 3.68 us -> 12.9 us
  blocking collectives: 63.4 us -> 59.4 us
  other arithmetic: 3.78 us -> 0.33 us
    pallas_call x0 -> x13, Pallas kernels: none -> 21.4 us  [the longest x9 17.8 us: call(): pl.pallas_call(body, out_shape=out, in_specs=specs, out_specs=[vmem] * le...]
    ppermute x10 -> x11, waiting for transfers between devices: 9.1 us -> 26.4 us  [send(): return lax.ppermute(x, ALL, [(i, to(i) % 256) for i in range(256)])]
    dot_general x8 -> x0, matrix products: 15.9 us -> none  [the longest x6 11.8 us: dot(): return jnp.dot(left, right, preferred_element_type=F32)]
    ppermute x10 -> x11, starting transfers between devices: 35.5 us -> 23.4 us  [send(): return lax.ppermute(x, ALL, [(i, to(i) % 256) for i in range(256)])]
    unnamed x18 -> x38, local copies, waits for them, and re-layouts: 1.71 us -> 12.7 us
    dot_general x6 -> x1, matrix products: 10.4 us -> 2.57 us  [dot_nt(): lax.dot_general(left, right, (((1,), (1,)), ((), ())), preferred_element_...]
    all_to_all x4 -> x3, blocking collectives: 63.4 us -> 59.4 us  [the longest x1 21.2 us: on_device(): got = lax.all_to_all(shares, ('y', 'x'), split_axis=0, concat_axis=0)]
    concatenate x2, other arithmetic: 1.57 us -> 0.08 us  [the longest x1 0.08 us: on_device(): places = jnp.concatenate([at(1), at(2), at(-1)])]
  transfers between devices with their start and end apart: 10 -> 11, of which waited for: 3 -> 6; matrix products, arithmetic and copies ran while one was open for 14% -> 2% of each run, Pallas kernels for 0% -> 11%
where the time goes in v1:
time: 148 us
  blocking collectives  59.4 us (40%)
  waiting for transfers between devices  26.4 us (18%)
  starting transfers between devices  23.4 us (16%)
  Pallas kernels  21.4 us (14%)
  local copies, waits for them, and re-layouts  12.9 us (9%)
  matrix products  2.57 us (2%)
    ppermute x11, waiting for transfers between devices, send(): return lax.ppermute(x, ALL, [(i, to(i) % 256) for i in range(256)])  26.4 us
    ppermute x11, starting transfers between devices, send(): return lax.ppermute(x, ALL, [(i, to(i) % 256) for i in range(256)])  23.4 us
    all_to_all x1, blocking collectives, on_device(): got = lax.all_to_all(shares, ('y', 'x'), split_axis=0, concat_axis=0)  21.2 us
    all_to_all x1, blocking collectives, on_device(): lax.all_to_all(jnp.broadcast_to(share[None], (8,) + share.shape), 'z', sp...  19.3 us
    all_to_all x1, blocking collectives, on_device(): lax.all_to_all(copies, ('y', 'x'), split_axis=0, concat_axis=0)  18.9 us
    pallas_call x9, Pallas kernels, call(): pl.pallas_call(body, out_shape=out, in_specs=specs, out_specs=[vmem] * le...  17.8 us
    unnamed x38, local copies, waits for them, and re-layouts  12.7 us
  transfers between devices with their start and end apart: 11, of which 6 were waited for; matrix products, arithmetic and copies ran while one was open for 2% of the time, Pallas kernels for 11%

profile of v1, /device:TPU:1, one launch (start us, length us, event | category | flops | bytes accessed | tf_op | source)
XLA Modules:
  0.0 147.5 jit_solution(7736379736583655599)
XLA Ops:
  0.6 1.4 copy-done
  2.0 1.7 %copy-done.16 = bf16[1536,768]{1,0:T(8,128)(2,1)S(1)} copy-done((bf16[1536,768]{1,0:T(8,128)(2,1)S(1)}, bf16[1536,768]{1,0:T(8,128)(2,1)}, u32[]{:S(2)}) %copy-start.16) | copy-done | bytes 2359320
  3.7 2.2 %embed.1 = (bf16[512,768]{1,0:T(8,128)(2,1)S(1)}, f32[512,768]{1,0:T(8,128)S(1)}, f32[512,1]{1,0:T(8,128)S(1)}) custom-call(bf16[512,1536]{1,0:T(8,128)(2,1)S(1)} %copy-done, bf16[1536,768]{1,0:T(8,128)(2,1)S(1)} %copy-done.16), custom_call_target="tpu_custom_call" | custom-call | flops 1207959552 | bytes 4194304 | tf_op jit(solution)/shard_map/embed/pallas_call | solution.py:240
  5.9 0.0 copy-start.2
  5.9 1.1 copy-done.2
  7.1 0.7 copy-done.14
  7.8 3.2 %collective-permute-start = (bf16[512,768]{1,0:T(8,128)(2,1)S(1)}, bf16[512,768]{1,0:T(8,128)(2,1)}, u32[]{:S(2)}, u32[]{:S(2)}) collective-permute-start(bf16[512,768]{1,0:T(8,128)(2,1)S(1)} %get-tuple-element.24.emb.refs_0_), channel_id=1, source_target_pairs={{0,1},{1,0},{2,3},{3,2},{4,5},{5,4},{6,7},{7,6},{8,9},{9,8},{10,11... | collective-permute-start | bytes 2359304 | tf_op jit(solution)/shard_map/ppermute | solution.py:16
  11.0 0.1 copy.13.goal
  11.2 1.4 turn.1
  12.5 0.9 copy-done.12
  13.4 3.5 %near.1 = (f32[512,512]{1,0:T(8,128)S(1)}, f32[512,512]{1,0:T(8,128)S(1)}, f32[512,1]{1,0:T(8,128)S(1)}, f32[512,1]{1,0:T(8,128)S(1)}) custom-call(s32[1]{0:T(128)} %bitcast.1.at, bf16[512,768]{1,0:T(8,128)(2,1)S(1)} %get-tuple-element.24.emb.refs_0_, bf16[512,768]{1,0:T(8,128)(2,1)} %collective-permute-done.peer.b1, s32[512,1]{1,0:T(8,128)S(1)} %copy.13.goal), custom_call_target="tpu_custom_call" | custom-call | flops 805306368 | bytes 3676160 | tf_op jit(solution)/shard_map/near/pallas_call | solution.py:52
  16.9 0.0 copy-start.4
  16.9 11.9 %collective-permute-done.2.refs_0_ = bf16[512,768]{1,0:T(8,128)(2,1)S(1)} collective-permute-done((bf16[512,768]{1,0:T(8,128)(2,1)S(1)}, bf16[512,768]{1,0:T(8,128)(2,1)S(1)}, u32[]{:S(2)}, u32[]{:S(2)}) %collective-permute-start.2) | collective-permute-done | bytes 786464 | tf_op jit(solution)/shard_map/ppermute | solution.py:16
  28.9 0.4 collective-permute-start.3
  29.3 7.6 %collective-permute-start.1 = (bf16[512,768]{1,0:T(8,128)(2,1)S(1)}, bf16[512,768]{1,0:T(8,128)(2,1)}, u32[]{:S(2)}, u32[]{:S(2)}) collective-permute-start(bf16[512,768]{1,0:T(8,128)(2,1)S(1)} %after.2.emb.b0), channel_id=1, source_target_pairs={{0,2},{1,255},{2,4},{3,1},{4,6},{5,3},{6,8},{7,5},{8,10},{9,7},{10... | collective-permute-start | bytes 2359304 | tf_op jit(solution)/shard_map/ppermute | solution.py:16
  36.9 1.3 across.1
  38.2 1.0 copy-done.8
  39.2 0.0 collective-permute-start.4
  39.2 1.3 relayed.1
  40.5 1.0 copy-done.10
  41.5 4.4 %collective-permute-done.4.last_sum = f32[1,512]{1,0:T(1,128)S(1)} collective-permute-done((f32[1,512]{1,0:T(1,128)S(1)}, f32[1,512]{1,0:T(1,128)S(1)}, u32[]{:S(2)}, u32[]{:S(2)}) %collective-permute-start.4) | collective-permute-done | bytes 2080 | tf_op jit(solution)/shard_map/ppermute | solution.py:16
  45.9 0.3 close.1
  46.2 1.6 %collective-permute-start.5 = (f32[2,512]{1,0:T(2,128)S(1)}, f32[2,512]{1,0:T(2,128)S(1)}, u32[]{:S(2)}, u32[]{:S(2)}) collective-permute-start(f32[2,512]{1,0:T(2,128)S(1)} %get-tuple-element.33.own_note), channel_id=1, source_target_pairs={{0,1},{1,0},{2,3},{3,2},{4,5},{5,4},{6,7},{7,6},{8,9},{9,8},{10,11... | collective-permute-start | bytes 12296 | tf_op jit(solution)/shard_map/ppermute | solution.py:16
  47.7 0.1 collective-permute-start.8
  47.8 0.7 collective-permute-done.5.peer_note
  48.6 6.4 %collective-permute-start.6 = (f32[4,512]{1,0:T(4,128)S(1)}, f32[4,512]{1,0:T(4,128)S(1)}, u32[]{:S(2)}, u32[]{:S(2)}) collective-permute-start(f32[4,512]{1,0:T(4,128)S(1)} %pad_maximum_fusion), channel_id=1, source_target_pairs={{0,2},{1,255},{2,4},{3,1},{4,6},{5,3},{6,8},{7,5},{8,10},{9,7},{10... | collective-permute-start | bytes 24584 | tf_op jit(solution)/shard_map/ppermute | solution.py:16
  54.9 0.1 pad_add_fusion.at
  55.0 0.2 collective-permute-start.7
  55.2 0.5 collective-permute-done.6
  55.7 7.4 %collective-permute-done.7.first_note = f32[2,512]{1,0:T(2,128)S(1)} collective-permute-done((f32[2,512]{1,0:T(2,128)S(1)}, f32[2,512]{1,0:T(2,128)S(1)}, u32[]{:S(2)}, u32[]{:S(2)}) %collective-permute-start.7) | collective-permute-done | bytes 4128 | tf_op jit(solution)/shard_map/ppermute | solution.py:16
  63.1 1.2 copy-done.5
  64.3 1.2 copy-done.7
  65.5 1.2 copy-done.9
  66.8 1.2 copy-done.11
  68.0 3.5 %slopes.1.part = f32[512,768]{1,0:T(8,128)S(1)} custom-call(s32[3]{0:T(128)S(1)} %pad_add_fusion.at, s32[512,1]{1,0:T(8,128)S(1)} %copy.13.goal, f32[512,1]{1,0:T(8,128)S(1)} %get-tuple-element.32.inverse, f32[2,512]{1,0:T(2,128)S(1)} %get-tuple-element.33.own_note, f32[2,512]{1,0:T(2,128)S(1)} %collective-permute-done.5.peer_note, ...), custom_call_target="tpu_custom_call" | custom-call | flops 1610612736 | bytes 8933376 | tf_op jit(solution)/shard_map/slopes/pallas_call | solution.py:52
  71.6 3.9 %finish.1 = (bf16[512,768]{1,0:T(8,128)(2,1)S(1)}, f32[1,512]{1,0:T(1,128)}) custom-call(s32[1]{0:T(128)} %bitcast.at, bf16[512,768]{1,0:T(8,128)(2,1)S(1)} %after.2.emb.b0, bf16[512,768]{1,0:T(8,128)(2,1)} %collective-permute-done.1.block, s32[512,1]{1,0:T(8,128)S(1)} %copy.13.goal, f32[512,1]{1,0:T(8,128)S(1)} %get-tuple-element.32.inverse, ...), custom_call_target="tpu_custom_call" | custom-call | flops 805306368 | bytes 5521408 | tf_op jit(solution)/shard_map/finish/pallas_call | solution.py:52
  75.4 0.8 head_own.1.part
  76.2 1.5 %collective-permute-done.9.dz = bf16[512,768]{1,0:T(8,128)(2,1)S(1)} collective-permute-done((bf16[512,768]{1,0:T(8,128)(2,1)S(1)}, bf16[512,768]{1,0:T(8,128)(2,1)S(1)}, u32[]{:S(2)}, u32[]{:S(2)}) %collective-permute-start.9) | collective-permute-done | bytes 786464 | tf_op jit(solution)/shard_map/ppermute | solution.py:16
  77.7 1.9 %head_both.1 = bf16[768,768]{1,0:T(8,128)(2,1)S(1)} custom-call(f32[768,768]{1,0:T(8,128)S(1)} %head_own.1.part, bf16[768,512]{1,0:T(8,128)(2,1)} %collective-permute-done.8.left, bf16[512,768]{1,0:T(8,128)(2,1)S(1)} %collective-permute-done.9.dz), custom_call_target="tpu_custom_call" | custom-call | flops 603979776 | bytes 5111808 | tf_op jit(solution)/shard_map/head_both/pallas_call | solution.py:52
  79.6 21.2 %all_to_all.15 = bf16[16,48,768]{2,1,0:T(8,128)(2,1)S(1)} all-to-all(bf16[16,48,768]{2,1,0:T(8,128)(2,1)S(1)} %bitcast.14), channel_id=1, replica_groups=mesh['z'=8,'y'=4,'x'=4,'core'=2] {'y','x'}, dimensions={0} | all-to-all | bytes 2359296 | tf_op jit(solution)/shard_map/all_to_all | solution.py:304
  100.8 0.2 reduce_sum.24
  101.0 19.3 %all_to_all.16 = bf16[8,48,768]{2,1,0:T(8,128)(2,1)S(1)} all-to-all(bf16[8,48,768]{2,1,0:T(8,128)(2,1)S(1)} %broadcast_in_dim.20), channel_id=1, replica_groups=mesh['z'=8,'y'=4,'x'=4,'core'=2] {'z'}, dimensions={0} | all-to-all | bytes 1179648 | tf_op jit(solution)/shard_map/all_to_all | solution.py:306
  120.3 0.1 reduce_sum.25
  120.4 0.1 broadcast_in_dim.21
  120.5 18.9 %all_to_all.17 = bf16[16,48,768]{2,1,0:T(8,128)(2,1)S(1)} all-to-all(bf16[16,48,768]{2,1,0:T(8,128)(2,1)S(1)} %broadcast_in_dim.21), channel_id=1, replica_groups=mesh['z'=8,'y'=4,'x'=4,'core'=2] {'y','x'}, dimensions={0} | all-to-all | bytes 2359296 | tf_op jit(solution)/shard_map/all_to_all | solution.py:309
  139.4 3.9 %collective-permute-start.10 = (bf16[768,768]{1,0:T(8,128)(2,1)S(1)}, bf16[768,768]{1,0:T(8,128)(2,1)S(1)}, u32[]{:S(2)}, u32[]{:S(2)}) collective-permute-start(bf16[768,768]{1,0:T(8,128)(2,1)S(1)} %bitcast.12), channel_id=1, source_target_pairs={{0,1},{1,0},{2,3},{3,2},{4,5},{5,4},{6,7},{7,6},{8,9},{9,8},{10,11... | collective-permute-start | bytes 3538952 | tf_op jit(solution)/shard_map/ppermute | solution.py:16
  143.4 2.6 %convolution_convert_fusion = bf16[512,1536]{1,0:T(8,128)(2,1)} fusion(bf16[512,768]{1,0:T(8,128)(2,1)S(1)} %get-tuple-element.43.dz, bf16[1536,768]{1,0:T(8,128)(2,1)S(1)} %copy-done.17), kind=kOutput, calls=%fused_computation | convolution fusion | flops 1208745984 | bytes 4718592 | tf_op jit(solution)/shard_map/dot_general | solution.py:36
  145.9 1.4 lay_out.1
  (38 shorter events, 0.1 us)
Async XLA Ops:
  0.6 1.4 copy-start
  2.0 1.7 %copy-start.16 = (bf16[1536,768]{1,0:T(8,128)(2,1)S(1)}, bf16[1536,768]{1,0:T(8,128)(2,1)}, u32[]{:S(2)}) copy-start(bf16[1536,768]{1,0:T(8,128)(2,1)} %head.1) | copy-start | bytes 7077892
  3.7 7.3 %copy-start.18 = (s32[512]{0:T(512)S(1)}, s32[512]{0:T(512)}, u32[]{:S(2)}) copy-start(s32[512]{0:T(512)} %param.5) | copy-start | bytes 6148
  3.7 7.5 %copy-start.1 = (bf16[512,1536]{1,0:T(8,128)(2,1)S(1)}, bf16[512,1536]{1,0:T(8,128)(2,1)}, u32[]{:S(2)}) copy-start(bf16[512,1536]{1,0:T(8,128)(2,1)} %frames.3) | copy-start | bytes 4718596
  5.9 1.1 copy-start.2
  7.1 0.7 copy-start.14
  7.8 5.7 %collective-permute-start = (bf16[512,768]{1,0:T(8,128)(2,1)S(1)}, bf16[512,768]{1,0:T(8,128)(2,1)}, u32[]{:S(2)}, u32[]{:S(2)}) collective-permute-start(bf16[512,768]{1,0:T(8,128)(2,1)S(1)} %get-tuple-element.24.emb.refs_0_), channel_id=1, source_target_pairs={{0,1},{1,0},{2,3},{3,2},{4,5},{5,4},{6,7},{7,6},{8,9},{9,8},{10,11... | collective-permute-start | bytes 2359304 | tf_op jit(solution)/shard_map/ppermute | solution.py:16
  11.0 17.9 %collective-permute-start.2 = (bf16[512,768]{1,0:T(8,128)(2,1)S(1)}, bf16[512,768]{1,0:T(8,128)(2,1)S(1)}, u32[]{:S(2)}, u32[]{:S(2)}) collective-permute-start(bf16[512,768]{1,0:T(8,128)(2,1)S(1)} %get-tuple-element.24.emb.refs_0_), channel_id=1, source_target_pairs={{0,254},{1,3},{2,0},{3,5},{4,2},{5,7},{6,4},{7,9},{8,6},{9,11},{10... | collective-permute-start | bytes 2359304 | tf_op jit(solution)/shard_map/ppermute | solution.py:16
  12.5 0.9 copy-start.12
  16.9 12.4 %copy-start.4 = (f32[512,512]{1,0:T(8,128)}, f32[512,512]{1,0:T(8,128)S(1)}, u32[]{:S(2)}) copy-start(f32[512,512]{1,0:T(8,128)S(1)} %get-tuple-element.38.e0) | copy-start | bytes 3145732
  16.9 12.4 %copy-start.6 = (f32[512,512]{1,0:T(8,128)}, f32[512,512]{1,0:T(8,128)S(1)}, u32[]{:S(2)}) copy-start(f32[512,512]{1,0:T(8,128)S(1)} %get-tuple-element.39.e1) | copy-start | bytes 3145732
  28.9 10.3 %collective-permute-start.3 = (bf16[512,768]{1,0:T(8,128)(2,1)S(1)}, bf16[512,768]{1,0:T(8,128)(2,1)S(1)}, u32[]{:S(2)}, u32[]{:S(2)}) collective-permute-start(bf16[512,768]{1,0:T(8,128)(2,1)S(1)} %after.3.block.b2), channel_id=1, source_target_pairs={{0,1},{1,0},{2,3},{3,2},{4,5},{5,4},{6,7},{7,6},{8,9},{9,8},{10,11... | collective-permute-start | bytes 2359304 | tf_op jit(solution)/shard_map/ppermute | solution.py:16
  29.3 42.2 %collective-permute-start.1 = (bf16[512,768]{1,0:T(8,128)(2,1)S(1)}, bf16[512,768]{1,0:T(8,128)(2,1)}, u32[]{:S(2)}, u32[]{:S(2)}) collective-permute-start(bf16[512,768]{1,0:T(8,128)(2,1)S(1)} %after.2.emb.b0), channel_id=1, source_target_pairs={{0,2},{1,255},{2,4},{3,1},{4,6},{5,3},{6,8},{7,5},{8,10},{9,7},{10... | collective-permute-start | bytes 2359304 | tf_op jit(solution)/shard_map/ppermute | solution.py:16
  38.2 1.0 copy-start.8
  39.2 6.7 %collective-permute-start.4 = (f32[1,512]{1,0:T(1,128)S(1)}, f32[1,512]{1,0:T(1,128)S(1)}, u32[]{:S(2)}, u32[]{:S(2)}) collective-permute-start(f32[1,512]{1,0:T(1,128)S(1)} %get-tuple-element.31), channel_id=1, source_target_pairs={{0,2},{1,255},{2,4},{3,1},{4,6},{5,3},{6,8},{7,5},{8,10},{9,7},{10... | collective-permute-start | bytes 6152 | tf_op jit(solution)/shard_map/ppermute | solution.py:16
  40.5 1.0 copy-start.10
  46.2 2.4 %collective-permute-start.5 = (f32[2,512]{1,0:T(2,128)S(1)}, f32[2,512]{1,0:T(2,128)S(1)}, u32[]{:S(2)}, u32[]{:S(2)}) collective-permute-start(f32[2,512]{1,0:T(2,128)S(1)} %get-tuple-element.33.own_note), channel_id=1, source_target_pairs={{0,1},{1,0},{2,3},{3,2},{4,5},{5,4},{6,7},{7,6},{8,9},{9,8},{10,11... | collective-permute-start | bytes 12296 | tf_op jit(solution)/shard_map/ppermute | solution.py:16
  47.7 28.5 %collective-permute-start.8 = (bf16[768,512]{1,0:T(8,128)(2,1)}, bf16[768,512]{1,0:T(8,128)(2,1)}, u32[]{:S(2)}, u32[]{:S(2)}) collective-permute-start(bf16[768,512]{1,0:T(8,128)(2,1)} %get-tuple-element.26.refs_2_), channel_id=1, source_target_pairs={{0,1},{1,0},{2,3},{3,2},{4,5},{5,4},{6,7},{7,6},{8,9},{9,8},{10,11... | collective-permute-start | bytes 2359304 | tf_op jit(solution)/shard_map/ppermute | solution.py:16
  48.6 7.1 %collective-permute-start.6 = (f32[4,512]{1,0:T(4,128)S(1)}, f32[4,512]{1,0:T(4,128)S(1)}, u32[]{:S(2)}, u32[]{:S(2)}) collective-permute-start(f32[4,512]{1,0:T(4,128)S(1)} %pad_maximum_fusion), channel_id=1, source_target_pairs={{0,2},{1,255},{2,4},{3,1},{4,6},{5,3},{6,8},{7,5},{8,10},{9,7},{10... | collective-permute-start | bytes 24584 | tf_op jit(solution)/shard_map/ppermute | solution.py:16
  55.0 8.1 %collective-permute-start.7 = (f32[2,512]{1,0:T(2,128)S(1)}, f32[2,512]{1,0:T(2,128)S(1)}, u32[]{:S(2)}, u32[]{:S(2)}) collective-permute-start(f32[2,512]{1,0:T(2,128)S(1)} %get-tuple-element.33.own_note), channel_id=1, source_target_pairs={{0,254},{1,3},{2,0},{3,5},{4,2},{5,7},{6,4},{7,9},{8,6},{9,11},{10... | collective-permute-start | bytes 12296 | tf_op jit(solution)/shard_map/ppermute | solution.py:16
  63.1 1.2 copy-start.5
  64.3 1.2 copy-start.7
  65.5 1.2 copy-start.9
  66.8 1.2 copy-start.11
  68.0 3.6 %copy-start.3 = (f32[512,768]{1,0:T(8,128)S(1)}, f32[512,768]{1,0:T(8,128)}, u32[]{:S(2)}) copy-start(f32[512,768]{1,0:T(8,128)} %copy-done.2) | copy-start | bytes 4718596
  68.0 3.6 %copy-start.15 = (f32[512,1]{1,0:T(8,128)S(1)}, f32[512,1]{1,0:T(8,128)}, u32[]{:S(2)}) copy-start(f32[512,1]{1,0:T(8,128)} %copy-done.14) | copy-start | bytes 6148
  71.6 3.9 %copy-start.13 = (bf16[768,512]{1,0:T(8,128)(2,1)S(1)}, bf16[768,512]{1,0:T(8,128)(2,1)}, u32[]{:S(2)}) copy-start(bf16[768,512]{1,0:T(8,128)(2,1)} %copy-done.12) | copy-start | bytes 2359300
  75.4 2.3 %collective-permute-start.9 = (bf16[512,768]{1,0:T(8,128)(2,1)S(1)}, bf16[512,768]{1,0:T(8,128)(2,1)S(1)}, u32[]{:S(2)}, u32[]{:S(2)}) collective-permute-start(bf16[512,768]{1,0:T(8,128)(2,1)S(1)} %get-tuple-element.43.dz), channel_id=1, source_target_pairs={{0,1},{1,0},{2,3},{3,2},{4,5},{5,4},{6,7},{7,6},{8,9},{9,8},{10,11... | collective-permute-start | bytes 2359304 | tf_op jit(solution)/shard_map/ppermute | solution.py:16
  120.4 22.9 %copy-start.17 = (bf16[1536,768]{1,0:T(8,128)(2,1)S(1)}, bf16[1536,768]{1,0:T(8,128)(2,1)}, u32[]{:S(2)}) copy-start(bf16[1536,768]{1,0:T(8,128)(2,1)} %head.1) | copy-start | bytes 7077892
  139.4 6.5 %collective-permute-start.10 = (bf16[768,768]{1,0:T(8,128)(2,1)S(1)}, bf16[768,768]{1,0:T(8,128)(2,1)S(1)}, u32[]{:S(2)}, u32[]{:S(2)}) collective-permute-start(bf16[768,768]{1,0:T(8,128)(2,1)S(1)} %bitcast.12), channel_id=1, source_target_pairs={{0,1},{1,0},{2,3},{3,2},{4,5},{5,4},{6,7},{7,6},{8,9},{9,8},{10,11... | collective-permute-start | bytes 3538952 | tf_op jit(solution)/shard_map/ppermute | solution.py:16

commit v2 on v1

v2 whole, which is shorter than its diff:
```python
import functools

import jax
import jax.numpy as jnp
from jax import lax
from jax.experimental import pallas as pl
from jax.experimental.pallas import tpu as pltpu
from jax.sharding import Mesh, PartitionSpec as P

SCALE = 50.0
ALL = ("z", "y", "x", "core")
SIZES = (8, 4, 4, 2)
F32, BF16 = jnp.float32, jnp.bfloat16
TILE, WIDE, PIECES = 128, 256, 4


def send(x, to):
    return lax.ppermute(x, ALL, [(i, to(i) % 256) for i in range(256)])


def in_chip(x):
    return send(x, lambda i: i ^ 1)


def inward(x):
    return send(x, lambda i: i - 2 if i % 2 == 0 else i + 2)


def outward(x):
    return send(x, lambda i: i + 2 if i % 2 == 0 else i - 2)


def dot(left, right):
    return jnp.dot(left, right, preferred_element_type=F32)


def dot_nt(left, right):
    return lax.dot_general(left, right, (((1,), (1,)), ((), ())), preferred_element_type=F32)


def to_row(column):
    return jnp.broadcast_to(column, (column.shape[0], 128)).T[:1]


def to_column(row):
    return jnp.broadcast_to(row, (128, row.shape[1])).T[:, :1]


def call(body, out, *arrays, scratch=(), flops=0, name=None, kept=()):
    vmem = pl.BlockSpec(memory_space=pltpu.VMEM)
    size = sum(a.size * a.dtype.itemsize for a in (*arrays, *out))
    return pl.pallas_call(
        body,
        out_shape=out,
        in_specs=[vmem] * len(arrays),
        out_specs=[vmem] * len(out),
        scratch_shapes=scratch,
        input_output_aliases=dict(kept),
        name=name,
        compiler_params=pltpu.CompilerParams(vmem_limit_bytes=16 * 2**20),
        cost_estimate=pl.CostEstimate(flops=flops, bytes_accessed=size, transcendentals=0),
    )(*arrays)


def after(x, *others):
    anywhere = pl.BlockSpec(memory_space=pl.ANY)
    return pl.pallas_call(
        lambda *refs: None,
        out_shape=jax.ShapeDtypeStruct(x.shape, x.dtype),
        in_specs=[anywhere] * (1 + len(others)),
        out_specs=anywhere,
        input_output_aliases={0: 0},
        name="after",
        compiler_params=pltpu.CompilerParams(vmem_limit_bytes=2**20),
    )(x, *others)


def embed(frames, head, offsets, emb, unit, rnorm, goal, goal_row, f, h, acc, sems):
    depth = head.shape[0]
    step = depth // PIECES
    copies = []
    for k in range(PIECES):
        cut = pl.ds(k * step, step)
        copies.append(pltpu.make_async_copy(frames.at[:, cut], f.at[:, cut], sems.at[0, k]))
        copies.append(pltpu.make_async_copy(head.at[cut, :], h.at[cut, :], sems.at[1, k]))
    for c in copies:
        c.start()
    row = offsets[...] + lax.broadcasted_iota(jnp.int32, offsets.shape, 1)
    goal_row[...] = row.astype(F32)
    goal[...] = to_column(row.astype(F32)).astype(jnp.int32)
    for k in range(PIECES):
        cut = pl.ds(k * step, step)
        copies[2 * k].wait()
        copies[2 * k + 1].wait()
        if k == 0:
            acc[...] = dot(f[:, cut], h[cut, :])
        elif k < PIECES - 1:
            acc[...] += dot(f[:, cut], h[cut, :])
    for r in range(0, acc.shape[0], WIDE):
        rows = pl.ds(r, WIDE)
        z = acc[rows, :] + dot(f[rows, cut], h[cut, :])
        norm = jnp.sqrt(jnp.sum(z * z, axis=1, keepdims=True) + 1e-06)
        inverse = 1.0 / norm
        u = z * inverse
        unit[rows, :] = u
        emb[rows, :] = u.astype(BF16)
        rnorm[rows, :] = inverse


def places():
    sign = 1 - 2 * lax.axis_index("core")
    return (0, sign, 2 * sign, -2 * sign, -sign)


def score_tile(at, emb, block, goal, rows):
    score = SCALE * dot_nt(emb[rows, :], block[...])
    cols = lax.broadcasted_iota(jnp.int32, score.shape, 1) + at * block.shape[0]
    hit = cols == goal[rows, :]
    return score, jnp.sum(jnp.where(hit, score, 0.0), axis=1, keepdims=True)


def near(emb, peer, goal, unit, rnorm, e_all, total, pos, *kept):
    at = places()
    for r in range(0, emb.shape[0], WIDE):
        rows = pl.ds(r, WIDE)
        score, p0 = score_tile(0, emb, emb, goal, rows)
        e = jnp.exp(score)
        i = lax.broadcasted_iota(jnp.int32, e.shape, 0) + r
        e = jnp.where(i == lax.broadcasted_iota(jnp.int32, e.shape, 1), 0.0, e)
        e_all[0, rows, :] = e
        total[rows, :] = jnp.sum(e, axis=1, keepdims=True)
        score, p1 = score_tile(at[1], emb, peer, goal, rows)
        e = jnp.exp(score)
        e_all[1, rows, :] = e
        total[rows, :] += jnp.sum(e, axis=1, keepdims=True)
        pos[rows, :] = p0 + p1


def add_block(slot, emb, block, goal, e_all, total, pos):
    at = places()[slot]
    for r in range(0, emb.shape[0], WIDE):
        rows = pl.ds(r, WIDE)
        score, p = score_tile(at, emb, block, goal, rows)
        e = jnp.exp(score)
        e_all[slot, rows, :] = e
        total[rows, :] += jnp.sum(e, axis=1, keepdims=True)
        pos[rows, :] += p


def far(emb, first, last, goal, e_in, total_in, pos_in, unit, rnorm, e_all, total, pos, *kept):
    add_block(2, emb, first, goal, e_all, total, pos)
    add_block(3, emb, last, goal, e_all, total, pos)


def seal(
    emb, relay, goal, goal_row, e_in, total_in, pos_in, unit, rnorm,
    e_all, total, pos, unit_out, rnorm_out, inverse, note, losses,
):
    add_block(4, emb, relay, goal, e_all, total, pos)
    whole = to_row(total[...])
    inv = 1.0 / whole
    note[0:1, :] = inv
    note[1:2, :] = goal_row[...]
    inverse[...] = to_column(inv)
    losses[...] = jnp.log(whole) - to_row(pos[...])


def slope(e, at, goal, inverse, their_inverse, their_goal, rows):
    width = e.shape[1]
    i = lax.broadcasted_iota(jnp.int32, e.shape, 0) + rows.start
    j = lax.broadcasted_iota(jnp.int32, e.shape, 1) + at * width
    ours = (j == goal[rows, :]).astype(F32)
    theirs = (i == their_goal + at * width).astype(F32)
    return e * (inverse[rows, :] + their_inverse) - ours - theirs


def finish(
    goal, inverse, own_note, peer_note, swap_a, swap_b, e_all, emb, peer, first, last, relay, unit, rnorm,
    dz, g, acc,
):
    at = places()
    matched = lax.rem(lax.axis_index("x") + lax.axis_index("core"), 2) == 0
    toward = jnp.where(matched, swap_a[...], swap_b[...])
    away = jnp.where(matched, swap_b[...], swap_a[...])
    notes = (own_note[...], peer_note[...], toward[:2], away[:2], away[2:])
    for k, (note, block) in enumerate(zip(notes, (emb, peer, first, last, relay))):
        their_inverse, their_goal = note[0:1], note[1:2].astype(jnp.int32)
        for r in range(0, g.shape[1], TILE):
            rows = pl.ds(r, TILE)
            g[k % 2, rows, :] = slope(e_all[k, rows, :], at[k], goal, inverse, their_inverse, their_goal, rows).astype(BF16)
        if k == 0:
            acc[...] = dot(g[0], block[...])
        else:
            acc[...] += dot(g[k % 2], block[...])
    for r in range(0, emb.shape[0], TILE):
        rows = pl.ds(r, TILE)
        demb = SCALE * acc[rows, :]
        u = unit[rows, :]
        along = jnp.sum(u * demb, axis=1, keepdims=True)
        dz[rows, :] = ((demb - u * along) * rnorm[rows, :]).astype(BF16)


def turn(frames, token, mine, theirs):
    half, core = mine.shape[0], lax.axis_index("core")
    for out, k in ((mine, core), (theirs, 1 - core)):
        for c in range(0, half, 256):
            columns = pl.ds(pl.multiple_of(k * half + c, 128), 256)
            out[pl.ds(c, 256), :] = frames[:, columns].T


def add_up(got, out):
    total = got[0].astype(F32)
    for k in range(1, got.shape[0]):
        total += got[k].astype(F32)
    total = total.astype(BF16)
    for k in range(out.shape[0]):
        out[k] = total


def head_own(left, dz, out):
    out[...] = dot(left[...], dz[...])


def head_both(part, left, dz, out):
    for r in range(0, out.shape[0], 256):
        rows = pl.ds(r, 256)
        out[rows, :] = (part[rows, :] + dot(left[rows, :], dz[...])).astype(BF16)


def lay_out(other, part, *rest):
    out, sem = rest[-2:]
    size, core = part.shape[0], lax.axis_index("core")
    start = pl.multiple_of((1 - core if other else core) * size, size)
    copy = pltpu.make_async_copy(part, out.at[pl.ds(start, size), :], sem)
    copy.start()
    copy.wait()


def place_half(part, *whole):
    anywhere = pl.BlockSpec(memory_space=pl.ANY)
    return pl.pallas_call(
        functools.partial(lay_out, bool(whole)),
        out_shape=jax.ShapeDtypeStruct((2 * part.shape[0], part.shape[1]), part.dtype),
        in_specs=[anywhere] * (1 + len(whole)),
        out_specs=anywhere,
        scratch_shapes=[pltpu.SemaphoreType.DMA],
        input_output_aliases={1: 0} if whole else {},
        name="lay_out",
        compiler_params=pltpu.CompilerParams(vmem_limit_bytes=2**20),
    )(part, *whole)


def on_device(frames, head, offsets):
    rows, depth = frames.shape
    width = head.shape[1]
    shape = jax.ShapeDtypeStruct
    col, row = shape((rows, 1), F32), shape((1, rows), F32)
    square, tall = shape((rows, rows), F32), shape((rows, width), F32)
    note = shape((2, rows), F32)
    block_flops = 2 * rows * rows * width
    half = depth // 2
    vmem, hbm = pl.BlockSpec(memory_space=pltpu.VMEM), pl.BlockSpec(memory_space=pltpu.HBM)
    emb, unit, rnorm, goal, goal_row = pl.pallas_call(
        embed,
        in_specs=[hbm, hbm, vmem],
        out_specs=[vmem] * 5,
        out_shape=[shape((rows, width), BF16), tall, col, shape((rows, 1), jnp.int32), row],
        scratch_shapes=[
            pltpu.VMEM((rows, depth), BF16),
            pltpu.VMEM((depth, width), BF16),
            pltpu.VMEM((rows, width), F32),
            pltpu.SemaphoreType.DMA((2, PIECES)),
        ],
        name="embed",
        compiler_params=pltpu.CompilerParams(vmem_limit_bytes=51 * 2**20),
        cost_estimate=pl.CostEstimate(flops=2 * rows * depth * width, bytes_accessed=2**22, transcendentals=0),
    )(frames, head, offsets.reshape(1, rows))

    peer = in_chip(emb)
    first = inward(emb)
    last = outward(emb)
    everything = shape((5, rows, rows), F32)
    e_all, total, pos, unit, rnorm = call(
        near, [everything, col, col, tall, col], emb, peer, goal, unit, rnorm,
        kept=((3, 3), (4, 4)), flops=2 * block_flops, name="near",
    )
    mine, theirs = call(turn, [shape((half, rows), BF16)] * 2, frames, pos, name="turn")
    first = after(first, total, theirs)
    relay = in_chip(first)
    theirs = in_chip(theirs)
    e_all, total, pos, unit, rnorm = call(
        far, [everything, col, col, tall, col], emb, first, last, goal, e_all, total, pos, unit, rnorm,
        kept=((4, 0), (5, 1), (6, 2), (7, 3), (8, 4)), flops=2 * block_flops, name="far",
    )
    e_all, total, pos, unit, rnorm, inverse, own_note, losses = call(
        seal, [everything, col, col, tall, col, col, note, row],
        emb, relay, goal, goal_row, e_all, total, pos, unit, rnorm,
        kept=((4, 0), (5, 1), (6, 2), (7, 3), (8, 4)), flops=block_flops, name="seal",
    )
    peer_note = in_chip(own_note)
    pair = jnp.concatenate([own_note, peer_note], axis=0)
    swap_a, swap_b = send(pair, lambda i: i ^ 2), send(pair, lambda i: ((i + 2) ^ 2) - 2)
    (dz,) = call(
        finish, [shape((rows, width), BF16)], goal, inverse, own_note, peer_note, swap_a, swap_b, e_all,
        emb, peer, first, last, relay, unit, rnorm,
        scratch=[pltpu.VMEM((2, rows, rows), BF16), pltpu.VMEM((rows, width), F32)],
        flops=5 * block_flops, name="finish",
    )
    dz_other = in_chip(dz)
    frame_grad = dot_nt(dz, head).astype(BF16)

    (partial,) = call(head_own, [shape((half, width), F32)], mine, dz, flops=2 * half * rows * width, name="head_own")
    (partial,) = call(
        head_both, [shape((half, width), BF16)], partial, theirs, dz_other, flops=2 * half * rows * width, name="head_both"
    )
    shares = partial.reshape(16, half // 16, width)
    got = lax.all_to_all(shares, ("y", "x"), split_axis=0, concat_axis=0)
    (copies,) = call(add_up, [shape((8, half // 16, width), BF16)], got, name="add_plane")
    got = lax.all_to_all(copies, "z", split_axis=0, concat_axis=0)
    (copies,) = call(add_up, [shape((16, half // 16, width), BF16)], got, name="add_z")
    own = lax.all_to_all(copies, ("y", "x"), split_axis=0, concat_axis=0).reshape(half, width)
    other = in_chip(own)
    head_grad = place_half(other, place_half(own))
    return (losses.reshape(rows), frame_grad, head_grad)


def solution(mesh):
    torus = Mesh(mesh.devices.reshape(SIZES), ALL)
    return jax.shard_map(
        on_device,
        mesh=torus,
        in_specs=(P(ALL, None), P(), P(ALL)),
        out_specs=(P(ALL), P(ALL, None), P()),
        check_vma=False,
    )
```

time: 148 us -> 129 us (0.87)
  waiting for transfers between devices: 26.4 us -> 12.9 us
  local copies, waits for them, and re-layouts: 12.9 us -> 0.78 us
  starting transfers between devices: 23.4 us -> 33.8 us
  Pallas kernels: 21.4 us -> 16.2 us
  blocking collectives: 59.4 us -> 61.8 us
    ppermute x11 -> x10, waiting for transfers between devices: 26.4 us -> 12.9 us  [send(): return lax.ppermute(x, ALL, [(i, to(i) % 256) for i in range(256)])]
    unnamed x38 -> x6, local copies, waits for them, and re-layouts: 12.7 us -> 0.78 us
    ppermute x11 -> x10, starting transfers between devices: 23.4 us -> 33.8 us  [send(): return lax.ppermute(x, ALL, [(i, to(i) % 256) for i in range(256)])]
    pallas_call x11 -> x12, Pallas kernels: 21.4 us -> 16.2 us  [the longest x9 9.86 us: call(): pl.pallas_call(body, out_shape=out, in_specs=[vmem] * len(arrays), out_sp...]
    all_to_all x1, blocking collectives: 19.3 us -> 21.2 us  [on_device(): got = lax.all_to_all(copies, 'z', split_axis=0, concat_axis=0)]
  transfers between devices with their start and end apart: 11 -> 10, of which waited for: 6 -> 6; matrix products, arithmetic and copies ran while one was open for 2% -> 2% of each run, Pallas kernels for 11% -> 6%
where the time goes in v2:
time: 129 us
  blocking collectives  61.8 us (48%)
  starting transfers between devices  33.8 us (26%)
  Pallas kernels  16.2 us (13%)
  waiting for transfers between devices  12.9 us (10%)
  matrix products  2.56 us (2%)
    ppermute x10, starting transfers between devices, send(): return lax.ppermute(x, ALL, [(i, to(i) % 256) for i in range(256)])  33.8 us
    all_to_all x1, blocking collectives, on_device(): got = lax.all_to_all(copies, 'z', split_axis=0, concat_axis=0)  21.2 us
    all_to_all x1, blocking collectives, on_device(): got = lax.all_to_all(shares, ('y', 'x'), split_axis=0, concat_axis=0)  20.9 us
    all_to_all x1, blocking collectives, on_device(): lax.all_to_all(copies, ('y', 'x'), split_axis=0, concat_axis=0)  19.7 us
    ppermute x10, waiting for transfers between devices, send(): return lax.ppermute(x, ALL, [(i, to(i) % 256) for i in range(256)])  12.9 us
    pallas_call x9, Pallas kernels, call(): pl.pallas_call(body, out_shape=out, in_specs=[vmem] * len(arrays), out_sp...  9.86 us
    pallas_call x1, Pallas kernels, on_device(): pl.pallas_call(embed, in_specs=[hbm, hbm, vmem], out_specs=[vmem] * 5, ou...  4.25 us
  transfers between devices with their start and end apart: 10, of which 6 were waited for; matrix products, arithmetic and copies ran while one was open for 2% of the time, Pallas kernels for 6%

profile of v2, /device:TPU:1, one launch (start us, length us, event | category | flops | bytes accessed | tf_op | source)
XLA Modules:
  0.0 128.9 jit_solution(12079519510718823125)
XLA Ops:
  0.6 0.0 copy-start.1
  0.6 0.7 copy-done.1
  1.3 4.3 %embed.1 = (bf16[512,768]{1,0:T(8,128)(2,1)S(1)}, f32[512,768]{1,0:T(8,128)S(1)}, f32[512,1]{1,0:T(8,128)S(1)}, s32[512,1]{1,0:T(8,128)S(1)}, f32[1,512]{1,0:T(1,128)S(1)}) custom-call(bf16[512,1536]{1,0:T(8,128)(2,1)} %frames.3, bf16[1536,768]{1,0:T(8,128)(2,1)} %head.1, s32[1,512]{1,0:T(1,128)S(1)} %bitcast.9), custom_call_target="tpu_custom_call" | custom-call | flops 1207959552 | bytes 4194304 | tf_op jit(solution)/shard_map/embed/pallas_call | solution.py:263
  5.6 3.3 %collective-permute-start.1 = (bf16[512,768]{1,0:T(8,128)(2,1)S(1)}, bf16[512,768]{1,0:T(8,128)(2,1)S(1)}, u32[]{:S(2)}, u32[]{:S(2)}) collective-permute-start(bf16[512,768]{1,0:T(8,128)(2,1)S(1)} %get-tuple-element.26.emb), channel_id=1, source_target_pairs={{0,1},{1,0},{2,3},{3,2},{4,5},{5,4},{6,7},{7,6},{8,9},{9,8},{10,11... | collective-permute-start | bytes 2359304 | tf_op jit(solution)/shard_map/ppermute | solution.py:18
  8.9 0.0 collective-permute-start
  8.9 8.5 %collective-permute-start.3 = (bf16[512,768]{1,0:T(8,128)(2,1)S(1)}, bf16[512,768]{1,0:T(8,128)(2,1)S(1)}, u32[]{:S(2)}, u32[]{:S(2)}) collective-permute-start(bf16[512,768]{1,0:T(8,128)(2,1)S(1)} %get-tuple-element.26.emb), channel_id=1, source_target_pairs={{0,2},{1,255},{2,4},{3,1},{4,6},{5,3},{6,8},{7,5},{8,10},{9,7},{10... | collective-permute-start | bytes 2359304 | tf_op jit(solution)/shard_map/ppermute | solution.py:18
  17.4 0.0 collective-permute-done.1.peer
  17.4 0.0 copy-start
  17.4 1.3 %near.1 = (f32[5,512,512]{2,1,0:T(8,128)S(1)}, f32[512,1]{1,0:T(8,128)S(1)}, f32[512,1]{1,0:T(8,128)S(1)}, f32[512,768]{1,0:T(8,128)S(1)}, f32[512,1]{1,0:T(8,128)S(1)}) custom-call(bf16[512,768]{1,0:T(8,128)(2,1)S(1)} %get-tuple-element.26.emb, bf16[512,768]{1,0:T(8,128)(2,1)S(1)} %collective-permute-done.1.peer, ...), custom_call_target="tpu_custom_call", output_to_operand_aliasing={{3}: (3, {}), {4}: (4, {})} | custom-call | flops 805306368 | bytes 9971712 | tf_op jit(solution)/shard_map/near/pallas_call | solution.py:52
  18.7 0.1 copy-done
  18.8 0.5 turn.1
  19.3 8.4 %collective-permute-done.refs_0_ = bf16[512,768]{1,0:T(8,128)(2,1)S(1)} collective-permute-done((bf16[512,768]{1,0:T(8,128)(2,1)S(1)}, bf16[512,768]{1,0:T(8,128)(2,1)S(1)}, u32[]{:S(2)}, u32[]{:S(2)}) %collective-permute-start) | collective-permute-done | bytes 786464 | tf_op jit(solution)/shard_map/ppermute | solution.py:18
  27.7 7.5 %collective-permute-start.2 = (bf16[512,768]{1,0:T(8,128)(2,1)S(1)}, bf16[512,768]{1,0:T(8,128)(2,1)S(1)}, u32[]{:S(2)}, u32[]{:S(2)}) collective-permute-start(bf16[512,768]{1,0:T(8,128)(2,1)S(1)} %after.1.first), channel_id=1, source_target_pairs={{0,1},{1,0},{2,3},{3,2},{4,5},{5,4},{6,7},{7,6},{8,9},{9,8},{10,11... | collective-permute-start | bytes 2359304 | tf_op jit(solution)/shard_map/ppermute | solution.py:18
  35.2 0.0 collective-permute-done.3.last
  35.2 1.3 far.1
  36.5 0.6 collective-permute-done.2.relay
  37.1 1.8 %seal.1 = (f32[5,512,512]{2,1,0:T(8,128)S(1)}, f32[512,1]{1,0:T(8,128)S(1)}, f32[512,1]{1,0:T(8,128)S(1)}, f32[512,768]{1,0:T(8,128)S(1)}, f32[512,1]{1,0:T(8,12...) custom-call(bf16[512,768]{1,0:T(8,128)(2,1)S(1)} %get-tuple-element., ...), custom_call_target="tpu_custom_call", output_to_operand_aliasing={{0}: (4, {}), {1}: (5, {}), {2}: (6, {}), {3}: (7, {}), {4}... | custom-call | flops 402653184 | bytes 15228928 | tf_op jit(solution)/shard_map/seal/pallas_call | solution.py:52
  38.9 0.4 collective-permute-start.4
  39.3 0.8 collective-permute-done.4.peer_note
  40.1 7.7 %collective-permute-start.6 = (f32[4,512]{1,0:T(4,128)S(1)}, f32[4,512]{1,0:T(4,128)S(1)}, u32[]{:S(2)}, u32[]{:S(2)}) collective-permute-start(f32[4,512]{1,0:T(4,128)S(1)} %pad_maximum_fusion), channel_id=1, source_target_pairs={{0,254},{1,255},{2,4},{3,5},{4,2},{5,3},{6,8},{7,9},{8,6},{9,7},{1... | collective-permute-start | bytes 24584 | tf_op jit(solution)/shard_map/ppermute | solution.py:18
  47.8 0.0 collective-permute-start.5
  47.8 0.6 collective-permute-start.7
  48.5 0.4 collective-permute-done.6.swap_b
  48.9 1.5 %collective-permute-done.5.swap_a = f32[4,512]{1,0:T(4,128)S(1)} collective-permute-done((f32[4,512]{1,0:T(4,128)S(1)}, f32[4,512]{1,0:T(4,128)S(1)}, u32[]{:S(2)}, u32[]{:S(2)}) %collective-permute-start.5) | collective-permute-done | bytes 8224 | tf_op jit(solution)/shard_map/ppermute | solution.py:18
  50.3 3.2 %finish.1.dz = bf16[512,768]{1,0:T(8,128)(2,1)S(1)} custom-call(s32[512,1]{1,0:T(8,128)S(1)} %get-tuple-element.27.goal, f32[512,1]{1,0:T(8,128)S(1)} %get-tuple-element.43.inverse, f32[2,512]{1,0:T(2,128)S(1)} %get-tuple-element.44.own_note, f32[2,512]{1,0:T(2,128)S(1)} %collective-permute-done.4.peer_note, f32[4,512]{1,0:T(4,128)S(1)} %collective-permute-done.5.swap_a, ...), custom_call_target="tpu_custom_call" | custom-call | flops 2013265920 | bytes 11565056 | tf_op jit(solution)/shard_map/finish/pallas_call | solution.py:52
  53.5 1.9 %collective-permute-start.8 = (bf16[512,768]{1,0:T(8,128)(2,1)S(1)}, bf16[512,768]{1,0:T(8,128)(2,1)S(1)}, u32[]{:S(2)}, u32[]{:S(2)}) collective-permute-start(bf16[512,768]{1,0:T(8,128)(2,1)S(1)} %finish.1.dz), channel_id=1, source_target_pairs={{0,1},{1,0},{2,3},{3,2},{4,5},{5,4},{6,7},{7,6},{8,9},{9,8},{10,11... | collective-permute-start | bytes 2359304 | tf_op jit(solution)/shard_map/ppermute | solution.py:18
  55.4 0.8 head_own.1.part
  56.2 0.0 collective-permute-done.7.left
  56.2 1.1 collective-permute-done.8.dz
  57.3 0.8 head_both.1
  58.1 20.9 %all_to_all.15.got = bf16[16,48,768]{2,1,0:T(8,128)(2,1)S(1)} all-to-all(bf16[16,48,768]{2,1,0:T(8,128)(2,1)S(1)} %bitcast.8), channel_id=1, replica_groups=mesh['z'=8,'y'=4,'x'=4,'core'=2] {'y','x'}, dimensions={0} | all-to-all | bytes 2359296 | tf_op jit(solution)/shard_map/all_to_all | solution.py:317
  79.0 0.2 add_plane.1
  79.2 21.2 %all_to_all.16.got = bf16[8,48,768]{2,1,0:T(8,128)(2,1)S(1)} all-to-all(bf16[8,48,768]{2,1,0:T(8,128)(2,1)S(1)} %add_plane.1), channel_id=1, replica_groups=mesh['z'=8,'y'=4,'x'=4,'core'=2] {'z'}, dimensions={0} | all-to-all | bytes 1179648 | tf_op jit(solution)/shard_map/all_to_all | solution.py:319
  100.4 0.1 add_z.1
  100.4 0.0 copy-start.2
  100.5 19.7 %all_to_all.17 = bf16[16,48,768]{2,1,0:T(8,128)(2,1)S(1)} all-to-all(bf16[16,48,768]{2,1,0:T(8,128)(2,1)S(1)} %add_z.1), channel_id=1, replica_groups=mesh['z'=8,'y'=4,'x'=4,'core'=2] {'y','x'}, dimensions={0} | all-to-all | bytes 2359296 | tf_op jit(solution)/shard_map/all_to_all | solution.py:321
  120.2 3.9 %collective-permute-start.9 = (bf16[768,768]{1,0:T(8,128)(2,1)S(1)}, bf16[768,768]{1,0:T(8,128)(2,1)S(1)}, u32[]{:S(2)}, u32[]{:S(2)}) collective-permute-start(bf16[768,768]{1,0:T(8,128)(2,1)S(1)} %bitcast.6), channel_id=1, source_target_pairs={{0,1},{1,0},{2,3},{3,2},{4,5},{5,4},{6,7},{7,6},{8,9},{9,8},{10,11... | collective-permute-start | bytes 3538952 | tf_op jit(solution)/shard_map/ppermute | solution.py:18
  124.1 0.0 copy-done.2
  124.1 2.6 %convolution_convert_fusion = bf16[512,1536]{1,0:T(8,128)(2,1)} fusion(bf16[512,768]{1,0:T(8,128)(2,1)S(1)} %finish.1.dz, bf16[1536,768]{1,0:T(8,128)(2,1)S(1)} %copy-done.2), kind=kOutput, calls=%fused_computation | convolution fusion | flops 1208745984 | bytes 4718592 | tf_op jit(solution)/shard_map/dot_general | solution.py:38
  126.7 1.0 lay_out.2.rest_0_
  127.7 0.0 collective-permute-done.9.part
  127.7 1.0 lay_out.3
  (2 shorter events, 0.0 us)
Async XLA Ops:
  0.6 0.7 copy-start.1
  5.6 11.8 %collective-permute-start.1 = (bf16[512,768]{1,0:T(8,128)(2,1)S(1)}, bf16[512,768]{1,0:T(8,128)(2,1)S(1)}, u32[]{:S(2)}, u32[]{:S(2)}) collective-permute-start(bf16[512,768]{1,0:T(8,128)(2,1)S(1)} %get-tuple-element.26.emb), channel_id=1, source_target_pairs={{0,1},{1,0},{2,3},{3,2},{4,5},{5,4},{6,7},{7,6},{8,9},{9,8},{10,11... | collective-permute-start | bytes 2359304 | tf_op jit(solution)/shard_map/ppermute | solution.py:18
  8.9 18.8 %collective-permute-start = (bf16[512,768]{1,0:T(8,128)(2,1)S(1)}, bf16[512,768]{1,0:T(8,128)(2,1)S(1)}, u32[]{:S(2)}, u32[]{:S(2)}) collective-permute-start(bf16[512,768]{1,0:T(8,128)(2,1)S(1)} %get-tuple-element.26.emb), channel_id=1, source_target_pairs={{0,254},{1,3},{2,0},{3,5},{4,2},{5,7},{6,4},{7,9},{8,6},{9,11},{10... | collective-permute-start | bytes 2359304 | tf_op jit(solution)/shard_map/ppermute | solution.py:18
  8.9 26.3 %collective-permute-start.3 = (bf16[512,768]{1,0:T(8,128)(2,1)S(1)}, bf16[512,768]{1,0:T(8,128)(2,1)S(1)}, u32[]{:S(2)}, u32[]{:S(2)}) collective-permute-start(bf16[512,768]{1,0:T(8,128)(2,1)S(1)} %get-tuple-element.26.emb), channel_id=1, source_target_pairs={{0,2},{1,255},{2,4},{3,1},{4,6},{5,3},{6,8},{7,5},{8,10},{9,7},{10... | collective-permute-start | bytes 2359304 | tf_op jit(solution)/shard_map/ppermute | solution.py:18
  17.4 1.4 %copy-start = (bf16[512,1536]{1,0:T(8,128)(2,1)S(1)}, bf16[512,1536]{1,0:T(8,128)(2,1)}, u32[]{:S(2)}) copy-start(bf16[512,1536]{1,0:T(8,128)(2,1)} %frames.3) | copy-start | bytes 4718596
  27.7 9.4 %collective-permute-start.2 = (bf16[512,768]{1,0:T(8,128)(2,1)S(1)}, bf16[512,768]{1,0:T(8,128)(2,1)S(1)}, u32[]{:S(2)}, u32[]{:S(2)}) collective-permute-start(bf16[512,768]{1,0:T(8,128)(2,1)S(1)} %after.1.first), channel_id=1, source_target_pairs={{0,1},{1,0},{2,3},{3,2},{4,5},{5,4},{6,7},{7,6},{8,9},{9,8},{10,11... | collective-permute-start | bytes 2359304 | tf_op jit(solution)/shard_map/ppermute | solution.py:18
  38.9 1.2 collective-permute-start.4
  40.1 8.7 %collective-permute-start.6 = (f32[4,512]{1,0:T(4,128)S(1)}, f32[4,512]{1,0:T(4,128)S(1)}, u32[]{:S(2)}, u32[]{:S(2)}) collective-permute-start(f32[4,512]{1,0:T(4,128)S(1)} %pad_maximum_fusion), channel_id=1, source_target_pairs={{0,254},{1,255},{2,4},{3,5},{4,2},{5,3},{6,8},{7,9},{8,6},{9,7},{1... | collective-permute-start | bytes 24584 | tf_op jit(solution)/shard_map/ppermute | solution.py:18
  47.8 2.5 %collective-permute-start.5 = (f32[4,512]{1,0:T(4,128)S(1)}, f32[4,512]{1,0:T(4,128)S(1)}, u32[]{:S(2)}, u32[]{:S(2)}) collective-permute-start(f32[4,512]{1,0:T(4,128)S(1)} %pad_maximum_fusion), channel_id=1, source_target_pairs={{0,2},{1,3},{2,0},{3,1},{4,6},{5,7},{6,4},{7,5},{8,10},{9,11},{10,... | collective-permute-start | bytes 24584 | tf_op jit(solution)/shard_map/ppermute | solution.py:18
  47.8 8.4 %collective-permute-start.7 = (bf16[768,512]{1,0:T(8,128)(2,1)S(1)}, bf16[768,512]{1,0:T(8,128)(2,1)S(1)}, u32[]{:S(2)}, u32[]{:S(2)}) collective-permute-start(bf16[768,512]{1,0:T(8,128)(2,1)S(1)} %get-tuple-element.32.refs_2_), channel_id=1, source_target_pairs={{0,1},{1,0},{2,3},{3,2},{4,5},{5,4},{6,7},{7,6},{8,9},{9,8},{10,11... | collective-permute-start | bytes 2359304 | tf_op jit(solution)/shard_map/ppermute | solution.py:18
  53.5 3.8 %collective-permute-start.8 = (bf16[512,768]{1,0:T(8,128)(2,1)S(1)}, bf16[512,768]{1,0:T(8,128)(2,1)S(1)}, u32[]{:S(2)}, u32[]{:S(2)}) collective-permute-start(bf16[512,768]{1,0:T(8,128)(2,1)S(1)} %finish.1.dz), channel_id=1, source_target_pairs={{0,1},{1,0},{2,3},{3,2},{4,5},{5,4},{6,7},{7,6},{8,9},{9,8},{10,11... | collective-permute-start | bytes 2359304 | tf_op jit(solution)/shard_map/ppermute | solution.py:18
  100.4 23.6 %copy-start.2 = (bf16[1536,768]{1,0:T(8,128)(2,1)S(1)}, bf16[1536,768]{1,0:T(8,128)(2,1)}, u32[]{:S(2)}) copy-start(bf16[1536,768]{1,0:T(8,128)(2,1)} %head.1) | copy-start | bytes 7077892
  120.2 7.5 %collective-permute-start.9 = (bf16[768,768]{1,0:T(8,128)(2,1)S(1)}, bf16[768,768]{1,0:T(8,128)(2,1)S(1)}, u32[]{:S(2)}, u32[]{:S(2)}) collective-permute-start(bf16[768,768]{1,0:T(8,128)(2,1)S(1)} %bitcast.6), channel_id=1, source_target_pairs={{0,1},{1,0},{2,3},{3,2},{4,5},{5,4},{6,7},{7,6},{8,9},{9,8},{10,11... | collective-permute-start | bytes 3538952 | tf_op jit(solution)/shard_map/ppermute | solution.py:18

commit v3 on v2

--- a/solution.py
+++ b/solution.py
@@ -8,8 +8,9 @@
 from jax.sharding import Mesh, PartitionSpec as P
 
 SCALE = 50.0
-ALL = ("z", "y", "x", "core")
-SIZES = (8, 4, 4, 2)
+ALL = ("zh", "zl", "y", "x", "core")
+SIZES = (4, 2, 4, 4, 2)
+NEAR = ("zl", "y", "x")
 F32, BF16 = jnp.float32, jnp.bfloat16
 TILE, WIDE, PIECES = 128, 256, 4
 
@@ -22,12 +23,12 @@
     return send(x, lambda i: i ^ 1)
 
 
-def inward(x):
-    return send(x, lambda i: i - 2 if i % 2 == 0 else i + 2)
-
-
-def outward(x):
-    return send(x, lambda i: i + 2 if i % 2 == 0 else i - 2)
+def swap_even(x):
+    return send(x, lambda i: i ^ 2)
+
+
+def swap_odd(x):
+    return send(x, lambda i: ((i + 2) ^ 2) - 2)
 
 
 def dot(left, right):
@@ -60,19 +61,6 @@
         compiler_params=pltpu.CompilerParams(vmem_limit_bytes=16 * 2**20),
         cost_estimate=pl.CostEstimate(flops=flops, bytes_accessed=size, transcendentals=0),
     )(*arrays)
-
-
-def after(x, *others):
-    anywhere = pl.BlockSpec(memory_space=pl.ANY)
-    return pl.pallas_call(
-        lambda *refs: None,
-        out_shape=jax.ShapeDtypeStruct(x.shape, x.dtype),
-        in_specs=[anywhere] * (1 + len(others)),
-        out_specs=anywhere,
-        input_output_aliases={0: 0},
-        name="after",
-        compiler_params=pltpu.CompilerParams(vmem_limit_bytes=2**20),
-    )(x, *others)
 
 
 def embed(frames, head, offsets, emb, unit, rnorm, goal, goal_row, f, h, acc, sems):
@@ -107,9 +95,25 @@
         rnorm[rows, :] = inverse
 
 
+def chip_sign():
+    return 1 - 2 * lax.rem(lax.axis_index("x"), 2)
+
+
+def crossed():
+    return lax.rem(lax.axis_index("x") + lax.axis_index("core"), 2) == 1
+
+
 def places():
-    sign = 1 - 2 * lax.axis_index("core")
-    return (0, sign, 2 * sign, -2 * sign, -sign)
+    core = 1 - 2 * lax.axis_index("core")
+    return (0, core, 2 * chip_sign(), -2 * chip_sign(), -core)
+
+
+def pick(odd, even, token, out):
+    out[...] = even[...]
+
+    @pl.when(crossed())
+    def _():
+        out[...] = odd[...]
 
 
 def score_tile(at, emb, block, goal, rows):
@@ -147,9 +151,9 @@
         pos[rows, :] += p
 
 
-def far(emb, first, last, goal, e_in, total_in, pos_in, unit, rnorm, e_all, total, pos, *kept):
-    add_block(2, emb, first, goal, e_all, total, pos)
-    add_block(3, emb, last, goal, e_all, total, pos)
+def far(emb, even, odd, goal, e_in, total_in, pos_in, unit, rnorm, e_all, total, pos, *kept):
+    add_block(2, emb, even, goal, e_all, total, pos)
+    add_block(3, emb, odd, goal, e_all, total, pos)
 
 
 def seal(
@@ -175,15 +179,14 @@
 
 
 def finish(
-    goal, inverse, own_note, peer_note, swap_a, swap_b, e_all, emb, peer, first, last, relay, unit, rnorm,
+    goal, inverse, own_note, peer_note, odd_note, even_note, e_all, emb, peer, even, odd, relay, unit, rnorm,
     dz, g, acc,
 ):
     at = places()
-    matched = lax.rem(lax.axis_index("x") + lax.axis_index("core"), 2) == 0
-    toward = jnp.where(matched, swap_a[...], swap_b[...])
-    away = jnp.where(matched, swap_b[...], swap_a[...])
-    notes = (own_note[...], peer_note[...], toward[:2], away[:2], away[2:])
-    for k, (note, block) in enumerate(zip(notes, (emb, peer, first, last, relay))):
+    even_note, odd_note = even_note[...], odd_note[...]
+    relay_note = jnp.where(crossed(), even_note, odd_note)[2:]
+    notes = (own_note[...], peer_note[...], even_note[:2], odd_note[:2], relay_note)
+    for k, (note, block) in enumerate(zip(notes, (emb, peer, even, odd, relay))):
         their_inverse, their_goal = note[0:1], note[1:2].astype(jnp.int32)
         for r in range(0, g.shape[1], TILE):
             rows = pl.ds(r, TILE)
@@ -222,28 +225,36 @@
 
 
 def head_both(part, left, dz, out):
-    for r in range(0, out.shape[0], 256):
-        rows = pl.ds(r, 256)
-        out[rows, :] = (part[rows, :] + dot(left[rows, :], dz[...])).astype(BF16)
+    cut = out.shape[2]
+    for r in range(0, out.shape[1], WIDE):
+        rows = pl.ds(r, WIDE)
+        whole = (part[rows, :] + dot(left[rows, :], dz[...])).astype(BF16)
+        for k in range(2):
+            out[k, rows, :] = whole[:, k * cut : (k + 1) * cut]
 
 
 def lay_out(other, part, *rest):
-    out, sem = rest[-2:]
-    size, core = part.shape[0], lax.axis_index("core")
+    out, sems = rest[-2:]
+    core = lax.axis_index("core")
+    _, size, cut = part.shape
     start = pl.multiple_of((1 - core if other else core) * size, size)
-    copy = pltpu.make_async_copy(part, out.at[pl.ds(start, size), :], sem)
-    copy.start()
-    copy.wait()
+    copies = [
+        pltpu.make_async_copy(part.at[k], out.at[pl.ds(start, size), pl.ds(k * cut, cut)], sems.at[k]) for k in range(2)
+    ]
+    for c in copies:
+        c.start()
+    for c in copies:
+        c.wait()
 
 
 def place_half(part, *whole):
     anywhere = pl.BlockSpec(memory_space=pl.ANY)
     return pl.pallas_call(
         functools.partial(lay_out, bool(whole)),
-        out_shape=jax.ShapeDtypeStruct((2 * part.shape[0], part.shape[1]), part.dtype),
+        out_shape=jax.ShapeDtypeStruct((2 * part.shape[1], 2 * part.shape[2]), part.dtype),
         in_specs=[anywhere] * (1 + len(whole)),
         out_specs=anywhere,
-        scratch_shapes=[pltpu.SemaphoreType.DMA],
+        scratch_shapes=[pltpu.SemaphoreType.DMA((2,))],
         input_output_aliases={1: 0} if whole else {},
         name="lay_out",
         compiler_params=pltpu.CompilerParams(vmem_limit_bytes=2**20),
@@ -277,19 +288,19 @@
     )(frames, head, offsets.reshape(1, rows))
 
     peer = in_chip(emb)
-    first = inward(emb)
-    last = outward(emb)
+    odd = swap_odd(emb)
+    even = swap_even(emb)
     everything = shape((5, rows, rows), F32)
     e_all, total, pos, unit, rnorm = call(
         near, [everything, col, col, tall, col], emb, peer, goal, unit, rnorm,
         kept=((3, 3), (4, 4)), flops=2 * block_flops, name="near",
     )
     mine, theirs = call(turn, [shape((half, rows), BF16)] * 2, frames, pos, name="turn")
-    first = after(first, total, theirs)
-    relay = in_chip(first)
+    (shared,) = call(pick, [shape((rows, width), BF16)], odd, even, theirs, name="pick")
+    relay = in_chip(shared)
     theirs = in_chip(theirs)
     e_all, total, pos, unit, rnorm = call(
-        far, [everything, col, col, tall, col], emb, first, last, goal, e_all, total, pos, unit, rnorm,
+        far, [everything, col, col, tall, col], emb, even, odd, goal, e_all, total, pos, unit, rnorm,
         kept=((4, 0), (5, 1), (6, 2), (7, 3), (8, 4)), flops=2 * block_flops, name="far",
     )
     e_all, total, pos, unit, rnorm, inverse, own_note, losses = call(
@@ -299,10 +310,11 @@
     )
     peer_note = in_chip(own_note)
     pair = jnp.concatenate([own_note, peer_note], axis=0)
-    swap_a, swap_b = send(pair, lambda i: i ^ 2), send(pair, lambda i: ((i + 2) ^ 2) - 2)
+    odd_note = swap_odd(pair)
+    even_note = swap_even(pair)
     (dz,) = call(
-        finish, [shape((rows, width), BF16)], goal, inverse, own_note, peer_note, swap_a, swap_b, e_all,
-        emb, peer, first, last, relay, unit, rnorm,
+        finish, [shape((rows, width), BF16)], goal, inverse, own_note, peer_note, odd_note, even_note, e_all,
+        emb, peer, even, odd, relay, unit, rnorm,
         scratch=[pltpu.VMEM((2, rows, rows), BF16), pltpu.VMEM((rows, width), F32)],
         flops=5 * block_flops, name="finish",
     )
@@ -311,14 +323,14 @@
 
     (partial,) = call(head_own, [shape((half, width), F32)], mine, dz, flops=2 * half * rows * width, name="head_own")
     (partial,) = call(
-        head_both, [shape((half, width), BF16)], partial, theirs, dz_other, flops=2 * half * rows * width, name="head_both"
-    )
-    shares = partial.reshape(16, half // 16, width)
-    got = lax.all_to_all(shares, ("y", "x"), split_axis=0, concat_axis=0)
-    (copies,) = call(add_up, [shape((8, half // 16, width), BF16)], got, name="add_plane")
-    got = lax.all_to_all(copies, "z", split_axis=0, concat_axis=0)
-    (copies,) = call(add_up, [shape((16, half // 16, width), BF16)], got, name="add_z")
-    own = lax.all_to_all(copies, ("y", "x"), split_axis=0, concat_axis=0).reshape(half, width)
+        head_both, [shape((2, half, width // 2), BF16)], partial, theirs, dz_other, flops=2 * half * rows * width, name="head_both"
+    )
+    share = (half // 16, width // 2)
+    got = lax.all_to_all(partial.reshape(32, *share), NEAR, split_axis=0, concat_axis=0)
+    (copies,) = call(add_up, [shape((4, *share), BF16)], got, name="add_near")
+    got = lax.all_to_all(copies, "zh", split_axis=0, concat_axis=0)
+    (copies,) = call(add_up, [shape((32, *share), BF16)], got, name="add_far")
+    own = lax.all_to_all(copies, NEAR, split_axis=0, concat_axis=0).reshape(2, half, width // 2)
     other = in_chip(own)
     head_grad = place_half(other, place_half(own))
     return (losses.reshape(rows), frame_grad, head_grad)

time: 129 us -> 123 us (0.953)
  starting transfers between devices: 33.8 us -> 27.4 us
  waiting for transfers between devices: 12.9 us -> 18.7 us
  blocking collectives: 61.8 us -> 56.1 us
    ppermute x10, starting transfers between devices: 33.8 us -> 27.4 us  [send(): return lax.ppermute(x, ALL, [(i, to(i) % 256) for i in range(256)])]
    ppermute x10, waiting for transfers between devices: 12.9 us -> 18.7 us  [send(): return lax.ppermute(x, ALL, [(i, to(i) % 256) for i in range(256)])]
    all_to_all x3, blocking collectives: 61.8 us -> 56.1 us  [the longest x1 21.4 us: on_device(): lax.all_to_all(partial.reshape(32, *share), NEAR, split_axis=0, concat_ax...]
    pallas_call x9 -> x10, Pallas kernels: 9.86 us -> 10 us  [call(): pl.pallas_call(body, out_shape=out, in_specs=[vmem] * len(arrays), out_sp...]
  transfers between devices with their start and end apart: 10 -> 10, of which waited for: 6 -> 6; matrix products, arithmetic and copies ran while one was open for 2% -> 2% of each run, Pallas kernels for 6% -> 7%
where the time goes in v3:
time: 123 us
  blocking collectives  56.1 us (46%)
  starting transfers between devices  27.4 us (22%)
  waiting for transfers between devices  18.7 us (15%)
  Pallas kernels  16.3 us (13%)
  matrix products  2.56 us (2%)
    ppermute x10, starting transfers between devices, send(): return lax.ppermute(x, ALL, [(i, to(i) % 256) for i in range(256)])  27.4 us
    all_to_all x1, blocking collectives, on_device(): lax.all_to_all(partial.reshape(32, *share), NEAR, split_axis=0, concat_ax...  21.4 us
    all_to_all x1, blocking collectives, on_device(): lax.all_to_all(copies, NEAR, split_axis=0, concat_axis=0)  19.5 us
    ppermute x10, waiting for transfers between devices, send(): return lax.ppermute(x, ALL, [(i, to(i) % 256) for i in range(256)])  18.7 us
    all_to_all x1, blocking collectives, on_device(): got = lax.all_to_all(copies, 'zh', split_axis=0, concat_axis=0)  15.3 us
    pallas_call x10, Pallas kernels, call(): pl.pallas_call(body, out_shape=out, in_specs=[vmem] * len(arrays), out_sp...  10 us
    pallas_call x1, Pallas kernels, on_device(): pl.pallas_call(embed, in_specs=[hbm, hbm, vmem], out_specs=[vmem] * 5, ou...  4.25 us
    dot_general x1, matrix products, dot_nt(): lax.dot_general(left, right, (((1,), (1,)), ((), ())), preferred_element_...  2.56 us
  transfers between devices with their start and end apart: 10, of which 6 were waited for; matrix products, arithmetic and copies ran while one was open for 2% of the time, Pallas kernels for 7%

profile of v3, /device:TPU:1, one launch (start us, length us, event | category | flops | bytes accessed | tf_op | source)
XLA Modules:
  0.0 122.9 jit_solution(16750636994307644913)
XLA Ops:
  0.6 0.0 copy-start.1
  0.6 0.7 copy-done.1
  1.3 4.3 %embed.1 = (bf16[512,768]{1,0:T(8,128)(2,1)S(1)}, f32[512,768]{1,0:T(8,128)S(1)}, f32[512,1]{1,0:T(8,128)S(1)}, s32[512,1]{1,0:T(8,128)S(1)}, f32[1,512]{1,0:T(1,128)S(1)}) custom-call(bf16[512,1536]{1,0:T(8,128)(2,1)} %frames.3, bf16[1536,768]{1,0:T(8,128)(2,1)} %head.1, s32[1,512]{1,0:T(1,128)S(1)} %bitcast.9), custom_call_target="tpu_custom_call" | custom-call | flops 1207959552 | bytes 4194304 | tf_op jit(solution)/shard_map/embed/pallas_call | solution.py:274
  5.6 3.3 %collective-permute-start.2 = (bf16[512,768]{1,0:T(8,128)(2,1)S(1)}, bf16[512,768]{1,0:T(8,128)(2,1)S(1)}, u32[]{:S(2)}, u32[]{:S(2)}) collective-permute-start(bf16[512,768]{1,0:T(8,128)(2,1)S(1)} %get-tuple-element.26.emb), channel_id=1, source_target_pairs={{0,1},{1,0},{2,3},{3,2},{4,5},{5,4},{6,7},{7,6},{8,9},{9,8},{10,11... | collective-permute-start | bytes 2359304 | tf_op jit(solution)/shard_map/ppermute | solution.py:19
  8.9 0.0 collective-permute-start.1
  8.9 9.0 %collective-permute-start = (bf16[512,768]{1,0:T(8,128)(2,1)S(1)}, bf16[512,768]{1,0:T(8,128)(2,1)S(1)}, u32[]{:S(2)}, u32[]{:S(2)}) collective-permute-start(bf16[512,768]{1,0:T(8,128)(2,1)S(1)} %get-tuple-element.26.emb), channel_id=1, source_target_pairs={{0,254},{1,255},{2,4},{3,5},{4,2},{5,3},{6,8},{7,9},{8,6},{9,7},{1... | collective-permute-start | bytes 2359304 | tf_op jit(solution)/shard_map/ppermute | solution.py:19
  18.0 0.0 collective-permute-done.2.peer
  18.0 0.0 copy-start
  18.0 1.3 %near.1 = (f32[5,512,512]{2,1,0:T(8,128)S(1)}, f32[512,1]{1,0:T(8,128)S(1)}, f32[512,1]{1,0:T(8,128)S(1)}, f32[512,768]{1,0:T(8,128)S(1)}, f32[512,1]{1,0:T(8,128)S(1)}) custom-call(bf16[512,768]{1,0:T(8,128)(2,1)S(1)} %get-tuple-element.26.emb, bf16[512,768]{1,0:T(8,128)(2,1)S(1)} %collective-permute-done.2.peer, ...), custom_call_target="tpu_custom_call", output_to_operand_aliasing={{3}: (3, {}), {4}: (4, {})} | custom-call | flops 805306368 | bytes 9971712 | tf_op jit(solution)/shard_map/near/pallas_call | solution.py:53
  19.3 0.1 copy-done
  19.4 0.5 turn.1
  19.8 8.2 %collective-permute-done.1.even = bf16[512,768]{1,0:T(8,128)(2,1)S(1)} collective-permute-done((bf16[512,768]{1,0:T(8,128)(2,1)S(1)}, bf16[512,768]{1,0:T(8,128)(2,1)S(1)}, u32[]{:S(2)}, u32[]{:S(2)}) %collective-permute-start.1) | collective-permute-done | bytes 786464 | tf_op jit(solution)/shard_map/ppermute | solution.py:19
  28.0 7.6 %collective-permute-done.odd = bf16[512,768]{1,0:T(8,128)(2,1)S(1)} collective-permute-done((bf16[512,768]{1,0:T(8,128)(2,1)S(1)}, bf16[512,768]{1,0:T(8,128)(2,1)S(1)}, u32[]{:S(2)}, u32[]{:S(2)}) %collective-permute-start) | collective-permute-done | bytes 786464 | tf_op jit(solution)/shard_map/ppermute | solution.py:19
  35.6 0.1 pick.1
  35.7 0.9 collective-permute-start.3
  36.6 1.3 %far.1 = (f32[5,512,512]{2,1,0:T(8,128)S(1)}, f32[512,1]{1,0:T(8,128)S(1)}, f32[512,1]{1,0:T(8,128)S(1)}, f32[512,768]{1,0:T(8,128)S(1)}, f32[512,1]{1,0:T(8,128)S(1)}) custom-call(bf16[512,768]{1,0:T(8,128)(2,1)S(1)} %get-tuple-element.26.emb, ...), custom_call_target="tpu_custom_call", output_to_operand_aliasing={{0}: (4, {}), {1}: (5, {}), {2}: (6, {}), {3}: (7, {}), {4}... | custom-call | flops 805306368 | bytes 16005120 | tf_op jit(solution)/shard_map/far/pallas_call | solution.py:53
  37.9 0.6 collective-permute-done.3.relay
  38.5 1.8 %seal.1 = (f32[5,512,512]{2,1,0:T(8,128)S(1)}, f32[512,1]{1,0:T(8,128)S(1)}, f32[512,1]{1,0:T(8,128)S(1)}, f32[512,768]{1,0:T(8,128)S(1)}, f32[512,1]{1,0:T(8,12...) custom-call(bf16[512,768]{1,0:T(8,128)(2,1)S(1)} %get-tuple-element., ...), custom_call_target="tpu_custom_call", output_to_operand_aliasing={{0}: (4, {}), {1}: (5, {}), {2}: (6, {}), {3}: (7, {}), {4}... | custom-call | flops 402653184 | bytes 15228928 | tf_op jit(solution)/shard_map/seal/pallas_call | solution.py:53
  40.3 0.4 collective-permute-start.4
  40.7 0.8 collective-permute-done.4.peer_note
  41.5 0.1 collective-permute-start.6
  41.6 7.0 %collective-permute-start.5 = (f32[4,512]{1,0:T(4,128)S(1)}, f32[4,512]{1,0:T(4,128)S(1)}, u32[]{:S(2)}, u32[]{:S(2)}) collective-permute-start(f32[4,512]{1,0:T(4,128)S(1)} %pad_maximum_fusion), channel_id=1, source_target_pairs={{0,254},{1,255},{2,4},{3,5},{4,2},{5,3},{6,8},{7,9},{8,6},{9,7},{1... | collective-permute-start | bytes 24584 | tf_op jit(solution)/shard_map/ppermute | solution.py:19
  48.7 0.6 collective-permute-start.7
  49.3 0.0 collective-permute-done.6.even_note
  49.3 0.4 collective-permute-done.5.odd_note
  49.7 3.2 %finish.1.dz = bf16[512,768]{1,0:T(8,128)(2,1)S(1)} custom-call(s32[512,1]{1,0:T(8,128)S(1)} %get-tuple-element.27.goal, f32[512,1]{1,0:T(8,128)S(1)} %get-tuple-element.43.inverse, f32[2,512]{1,0:T(2,128)S(1)} %get-tuple-element.44.own_note, f32[2,512]{1,0:T(2,128)S(1)} %collective-permute-done.4.peer_note, f32[4,512]{1,0:T(4,128)S(1)} %collective-permute-done.5.odd_note, ...), custom_call_target="tpu_custom_call" | custom-call | flops 2013265920 | bytes 11565056 | tf_op jit(solution)/shard_map/finish/pallas_call | solution.py:53
  52.9 1.5 %collective-permute-start.8 = (bf16[512,768]{1,0:T(8,128)(2,1)S(1)}, bf16[512,768]{1,0:T(8,128)(2,1)S(1)}, u32[]{:S(2)}, u32[]{:S(2)}) collective-permute-start(bf16[512,768]{1,0:T(8,128)(2,1)S(1)} %finish.1.dz), channel_id=1, source_target_pairs={{0,1},{1,0},{2,3},{3,2},{4,5},{5,4},{6,7},{7,6},{8,9},{9,8},{10,11... | collective-permute-start | bytes 2359304 | tf_op jit(solution)/shard_map/ppermute | solution.py:19
  54.5 0.8 head_own.1.part
  55.3 0.0 collective-permute-done.7.left
  55.3 1.1 collective-permute-done.8.dz
  56.4 0.8 head_both.1
  57.2 21.4 %all_to_all.15.got = bf16[32,48,384]{2,1,0:T(8,128)(2,1)S(1)} all-to-all(bf16[32,48,384]{2,1,0:T(8,128)(2,1)S(1)} %bitcast.8), channel_id=1, replica_groups=mesh['zh'=4,'zl'=2,'y'=4,'x'=4,'core'=2] {'zl','y','x'}, dimensions={0} | all-to-all | bytes 2359296 | tf_op jit(solution)/shard_map/all_to_all | solution.py:329
  78.5 0.2 add_near.1
  78.7 15.3 %all_to_all.16.got = bf16[4,48,384]{2,1,0:T(8,128)(2,1)S(1)} all-to-all(bf16[4,48,384]{2,1,0:T(8,128)(2,1)S(1)} %add_near.1), channel_id=1, replica_groups=mesh['zh'=4,'zl'=2,'y'=4,'x'=4,'core'=2] {'zh'}, dimensions={0} | all-to-all | bytes 294912 | tf_op jit(solution)/shard_map/all_to_all | solution.py:331
  94.0 0.0 copy-start.2
  94.0 0.1 add_far.1
  94.1 19.5 %all_to_all.17 = bf16[32,48,384]{2,1,0:T(8,128)(2,1)S(1)} all-to-all(bf16[32,48,384]{2,1,0:T(8,128)(2,1)S(1)} %add_far.1), channel_id=1, replica_groups=mesh['zh'=4,'zl'=2,'y'=4,'x'=4,'core'=2] {'zl','y','x'}, dimensions={0} | all-to-all | bytes 2359296 | tf_op jit(solution)/shard_map/all_to_all | solution.py:333
  113.6 4.5 %collective-permute-start.9 = (bf16[2,768,384]{2,1,0:T(8,128)(2,1)S(1)}, bf16[2,768,384]{2,1,0:T(8,128)(2,1)S(1)}, u32[]{:S(2)}, u32[]{:S(2)}) collective-permute-start(bf16[2,768,384]{2,1,0:T(8,128)(2,1)S(1)} %bitcast.6), channel_id=1, source_target_pairs={{0,1},{1,0},{2,3},{3,2},{4,5},{5,4},{6,7},{7,6},{8,9},{9,8},{10,11... | collective-permute-start | bytes 3538952 | tf_op jit(solution)/shard_map/ppermute | solution.py:19
  118.1 0.0 copy-done.2
  118.1 2.6 %convolution_convert_fusion = bf16[512,1536]{1,0:T(8,128)(2,1)} fusion(bf16[512,768]{1,0:T(8,128)(2,1)S(1)} %finish.1.dz, bf16[1536,768]{1,0:T(8,128)(2,1)S(1)} %copy-done.2), kind=kOutput, calls=%fused_computation | convolution fusion | flops 1208745984 | bytes 4718592 | tf_op jit(solution)/shard_map/dot_general | solution.py:39
  120.6 1.0 lay_out.2.rest_0_
  121.7 0.0 collective-permute-done.9.part
  121.7 1.0 lay_out.3
  (1 shorter events, 0.0 us)
Async XLA Ops:
  0.6 0.7 copy-start.1
  5.6 12.4 %collective-permute-start.2 = (bf16[512,768]{1,0:T(8,128)(2,1)S(1)}, bf16[512,768]{1,0:T(8,128)(2,1)S(1)}, u32[]{:S(2)}, u32[]{:S(2)}) collective-permute-start(bf16[512,768]{1,0:T(8,128)(2,1)S(1)} %get-tuple-element.26.emb), channel_id=1, source_target_pairs={{0,1},{1,0},{2,3},{3,2},{4,5},{5,4},{6,7},{7,6},{8,9},{9,8},{10,11... | collective-permute-start | bytes 2359304 | tf_op jit(solution)/shard_map/ppermute | solution.py:19
  8.9 19.1 %collective-permute-start.1 = (bf16[512,768]{1,0:T(8,128)(2,1)S(1)}, bf16[512,768]{1,0:T(8,128)(2,1)S(1)}, u32[]{:S(2)}, u32[]{:S(2)}) collective-permute-start(bf16[512,768]{1,0:T(8,128)(2,1)S(1)} %get-tuple-element.26.emb), channel_id=1, source_target_pairs={{0,2},{1,3},{2,0},{3,1},{4,6},{5,7},{6,4},{7,5},{8,10},{9,11},{10,... | collective-permute-start | bytes 2359304 | tf_op jit(solution)/shard_map/ppermute | solution.py:19
  8.9 26.7 %collective-permute-start = (bf16[512,768]{1,0:T(8,128)(2,1)S(1)}, bf16[512,768]{1,0:T(8,128)(2,1)S(1)}, u32[]{:S(2)}, u32[]{:S(2)}) collective-permute-start(bf16[512,768]{1,0:T(8,128)(2,1)S(1)} %get-tuple-element.26.emb), channel_id=1, source_target_pairs={{0,254},{1,255},{2,4},{3,5},{4,2},{5,3},{6,8},{7,9},{8,6},{9,7},{1... | collective-permute-start | bytes 2359304 | tf_op jit(solution)/shard_map/ppermute | solution.py:19
  18.0 1.4 %copy-start = (bf16[512,1536]{1,0:T(8,128)(2,1)S(1)}, bf16[512,1536]{1,0:T(8,128)(2,1)}, u32[]{:S(2)}) copy-start(bf16[512,1536]{1,0:T(8,128)(2,1)} %frames.3) | copy-start | bytes 4718596
  35.7 2.8 %collective-permute-start.3 = (bf16[512,768]{1,0:T(8,128)(2,1)S(1)}, bf16[512,768]{1,0:T(8,128)(2,1)S(1)}, u32[]{:S(2)}, u32[]{:S(2)}) collective-permute-start(bf16[512,768]{1,0:T(8,128)(2,1)S(1)} %pick.1), channel_id=1, source_target_pairs={{0,1},{1,0},{2,3},{3,2},{4,5},{5,4},{6,7},{7,6},{8,9},{9,8},{10,11... | collective-permute-start | bytes 2359304 | tf_op jit(solution)/shard_map/ppermute | solution.py:19
  40.3 1.2 collective-permute-start.4
  41.5 7.8 %collective-permute-start.6 = (f32[4,512]{1,0:T(4,128)S(1)}, f32[4,512]{1,0:T(4,128)S(1)}, u32[]{:S(2)}, u32[]{:S(2)}) collective-permute-start(f32[4,512]{1,0:T(4,128)S(1)} %pad_maximum_fusion), channel_id=1, source_target_pairs={{0,2},{1,3},{2,0},{3,1},{4,6},{5,7},{6,4},{7,5},{8,10},{9,11},{10,... | collective-permute-start | bytes 24584 | tf_op jit(solution)/shard_map/ppermute | solution.py:19
  41.6 8.1 %collective-permute-start.5 = (f32[4,512]{1,0:T(4,128)S(1)}, f32[4,512]{1,0:T(4,128)S(1)}, u32[]{:S(2)}, u32[]{:S(2)}) collective-permute-start(f32[4,512]{1,0:T(4,128)S(1)} %pad_maximum_fusion), channel_id=1, source_target_pairs={{0,254},{1,255},{2,4},{3,5},{4,2},{5,3},{6,8},{7,9},{8,6},{9,7},{1... | collective-permute-start | bytes 24584 | tf_op jit(solution)/shard_map/ppermute | solution.py:19
  48.7 6.6 %collective-permute-start.7 = (bf16[768,512]{1,0:T(8,128)(2,1)S(1)}, bf16[768,512]{1,0:T(8,128)(2,1)S(1)}, u32[]{:S(2)}, u32[]{:S(2)}) collective-permute-start(bf16[768,512]{1,0:T(8,128)(2,1)S(1)} %get-tuple-element.31.token), channel_id=1, source_target_pairs={{0,1},{1,0},{2,3},{3,2},{4,5},{5,4},{6,7},{7,6},{8,9},{9,8},{10,11... | collective-permute-start | bytes 2359304 | tf_op jit(solution)/shard_map/ppermute | solution.py:19
  52.9 3.5 %collective-permute-start.8 = (bf16[512,768]{1,0:T(8,128)(2,1)S(1)}, bf16[512,768]{1,0:T(8,128)(2,1)S(1)}, u32[]{:S(2)}, u32[]{:S(2)}) collective-permute-start(bf16[512,768]{1,0:T(8,128)(2,1)S(1)} %finish.1.dz), channel_id=1, source_target_pairs={{0,1},{1,0},{2,3},{3,2},{4,5},{5,4},{6,7},{7,6},{8,9},{9,8},{10,11... | collective-permute-start | bytes 2359304 | tf_op jit(solution)/shard_map/ppermute | solution.py:19
  94.0 24.1 %copy-start.2 = (bf16[1536,768]{1,0:T(8,128)(2,1)S(1)}, bf16[1536,768]{1,0:T(8,128)(2,1)}, u32[]{:S(2)}) copy-start(bf16[1536,768]{1,0:T(8,128)(2,1)} %head.1) | copy-start | bytes 7077892
  113.6 8.1 %collective-permute-start.9 = (bf16[2,768,384]{2,1,0:T(8,128)(2,1)S(1)}, bf16[2,768,384]{2,1,0:T(8,128)(2,1)S(1)}, u32[]{:S(2)}, u32[]{:S(2)}) collective-permute-start(bf16[2,768,384]{2,1,0:T(8,128)(2,1)S(1)} %bitcast.6), channel_id=1, source_target_pairs={{0,1},{1,0},{2,3},{3,2},{4,5},{5,4},{6,7},{7,6},{8,9},{9,8},{10,11... | collective-permute-start | bytes 3538952 | tf_op jit(solution)/shard_map/ppermute | solution.py:19

commit v4 on v3

--- a/solution.py
+++ b/solution.py
@@ -12,7 +12,7 @@
 SIZES = (4, 2, 4, 4, 2)
 NEAR = ("zl", "y", "x")
 F32, BF16 = jnp.float32, jnp.bfloat16
-TILE, WIDE, PIECES = 128, 256, 4
+TILE, WIDE, PIECES = 128, 256, 2
 
 
 def send(x, to):
@@ -63,7 +63,7 @@
     )(*arrays)
 
 
-def embed(frames, head, offsets, emb, unit, rnorm, goal, goal_row, f, h, acc, sems):
+def embed(frames, head, emb, unit, rnorm, f, h, acc, sems):
     depth = head.shape[0]
     step = depth // PIECES
     copies = []
@@ -73,9 +73,6 @@
         copies.append(pltpu.make_async_copy(head.at[cut, :], h.at[cut, :], sems.at[1, k]))
     for c in copies:
         c.start()
-    row = offsets[...] + lax.broadcasted_iota(jnp.int32, offsets.shape, 1)
-    goal_row[...] = row.astype(F32)
-    goal[...] = to_column(row.astype(F32)).astype(jnp.int32)
     for k in range(PIECES):
         cut = pl.ds(k * step, step)
         copies[2 * k].wait()
@@ -123,8 +120,11 @@
     return score, jnp.sum(jnp.where(hit, score, 0.0), axis=1, keepdims=True)
 
 
-def near(emb, peer, goal, unit, rnorm, e_all, total, pos, *kept):
+def near(emb, peer, offsets, unit, rnorm, e_all, total, pos, unit_out, rnorm_out, goal, goal_row):
     at = places()
+    positives = (offsets[...] + lax.broadcasted_iota(jnp.int32, offsets.shape, 1)).astype(F32)
+    goal_row[...] = positives
+    goal[...] = to_column(positives).astype(jnp.int32)
     for r in range(0, emb.shape[0], WIDE):
         rows = pl.ds(r, WIDE)
         score, p0 = score_tile(0, emb, emb, goal, rows)
@@ -158,15 +158,17 @@
 
 def seal(
     emb, relay, goal, goal_row, e_in, total_in, pos_in, unit, rnorm,
-    e_all, total, pos, unit_out, rnorm_out, inverse, note, losses,
+    e_all, total, pos, unit_out, rnorm_out, inverse, note,
 ):
     add_block(4, emb, relay, goal, e_all, total, pos)
-    whole = to_row(total[...])
-    inv = 1.0 / whole
-    note[0:1, :] = inv
+    inverse[...] = 1.0 / total[...]
+    note[0:1, :] = to_row(inverse[...])
     note[1:2, :] = goal_row[...]
-    inverse[...] = to_column(inv)
-    losses[...] = jnp.log(whole) - to_row(pos[...])
+
+
+def lose(total, pos, losses, token):
+    losses[...] = to_row(jnp.log(total[...]) - pos[...])
+    token[...] = jnp.zeros_like(token)
 
 
 def slope(e, at, goal, inverse, their_inverse, their_goal, rows):
@@ -179,7 +181,7 @@
 
 
 def finish(
-    goal, inverse, own_note, peer_note, odd_note, even_note, e_all, emb, peer, even, odd, relay, unit, rnorm,
+    goal, inverse, own_note, peer_note, odd_note, even_note, e_all, emb, peer, even, odd, relay, unit, rnorm, token,
     dz, g, acc,
 ):
     at = places()
@@ -233,32 +235,41 @@
             out[k, rows, :] = whole[:, k * cut : (k + 1) * cut]
 
 
-def lay_out(other, part, *rest):
-    out, sems = rest[-2:]
-    core = lax.axis_index("core")
+def half_copies(part, out, sems, core):
     _, size, cut = part.shape
-    start = pl.multiple_of((1 - core if other else core) * size, size)
-    copies = [
-        pltpu.make_async_copy(part.at[k], out.at[pl.ds(start, size), pl.ds(k * cut, cut)], sems.at[k]) for k in range(2)
+    step = size // 2
+    start = pl.multiple_of(core * size, size)
+    return [
+        pltpu.make_async_copy(
+            part.at[k, pl.ds(r * step, step), :],
+            out.at[pl.ds(start + r * step, step), pl.ds(k * cut, cut)],
+            sems.at[k, r],
+        )
+        for k in range(2)
+        for r in range(2)
     ]
+
+
+def ends(dz, head, own, frame_grad, out, held, sems, out_sems):
+    copies = half_copies(own, out, sems, lax.axis_index("core"))
     for c in copies:
         c.start()
+    step = head.shape[0] // out_sems.shape[0]
+    for k in range(out_sems.shape[0]):
+        cut = pl.ds(k * step, step)
+        held[:, cut] = dot_nt(dz[...], head[cut, :]).astype(BF16)
+        copies.append(pltpu.make_async_copy(held.at[:, cut], frame_grad.at[:, cut], out_sems.at[k]))
+        copies[-1].start()
     for c in copies:
         c.wait()
 
 
-def place_half(part, *whole):
-    anywhere = pl.BlockSpec(memory_space=pl.ANY)
-    return pl.pallas_call(
-        functools.partial(lay_out, bool(whole)),
-        out_shape=jax.ShapeDtypeStruct((2 * part.shape[1], 2 * part.shape[2]), part.dtype),
-        in_specs=[anywhere] * (1 + len(whole)),
-        out_specs=anywhere,
-        scratch_shapes=[pltpu.SemaphoreType.DMA((2,))],
-        input_output_aliases={1: 0} if whole else {},
-        name="lay_out",
-        compiler_params=pltpu.CompilerParams(vmem_limit_bytes=2**20),
-    )(part, *whole)
+def last_half(other, whole, out, sems):
+    copies = half_copies(other, out, sems, 1 - lax.axis_index("core"))
+    for c in copies:
+        c.start()
+    for c in copies:
+        c.wait()
 
 
 def on_device(frames, head, offsets):
@@ -271,11 +282,11 @@
     block_flops = 2 * rows * rows * width
     half = depth // 2
     vmem, hbm = pl.BlockSpec(memory_space=pltpu.VMEM), pl.BlockSpec(memory_space=pltpu.HBM)
-    emb, unit, rnorm, goal, goal_row = pl.pallas_call(
+    emb, unit, rnorm = pl.pallas_call(
         embed,
-        in_specs=[hbm, hbm, vmem],
-        out_specs=[vmem] * 5,
-        out_shape=[shape((rows, width), BF16), tall, col, shape((rows, 1), jnp.int32), row],
+        in_specs=[hbm, hbm],
+        out_specs=[vmem] * 3,
+        out_shape=[shape((rows, width), BF16), tall, col],
         scratch_shapes=[
             pltpu.VMEM((rows, depth), BF16),
             pltpu.VMEM((depth, width), BF16),
@@ -285,14 +296,15 @@
         name="embed",
         compiler_params=pltpu.CompilerParams(vmem_limit_bytes=51 * 2**20),
         cost_estimate=pl.CostEstimate(flops=2 * rows * depth * width, bytes_accessed=2**22, transcendentals=0),
-    )(frames, head, offsets.reshape(1, rows))
+    )(frames, head)
 
     peer = in_chip(emb)
     odd = swap_odd(emb)
     even = swap_even(emb)
     everything = shape((5, rows, rows), F32)
-    e_all, total, pos, unit, rnorm = call(
-        near, [everything, col, col, tall, col], emb, peer, goal, unit, rnorm,
+    e_all, total, pos, unit, rnorm, goal, goal_row = call(
+        near, [everything, col, col, tall, col, shape((rows, 1), jnp.int32), row],
+        emb, peer, offsets.reshape(1, rows), unit, rnorm,
         kept=((3, 3), (4, 4)), flops=2 * block_flops, name="near",
     )
     mine, theirs = call(turn, [shape((half, rows), BF16)] * 2, frames, pos, name="turn")
@@ -303,23 +315,23 @@
         far, [everything, col, col, tall, col], emb, even, odd, goal, e_all, total, pos, unit, rnorm,
         kept=((4, 0), (5, 1), (6, 2), (7, 3), (8, 4)), flops=2 * block_flops, name="far",
     )
-    e_all, total, pos, unit, rnorm, inverse, own_note, losses = call(
-        seal, [everything, col, col, tall, col, col, note, row],
+    e_all, total, pos, unit, rnorm, inverse, own_note = call(
+        seal, [everything, col, col, tall, col, col, note],
         emb, relay, goal, goal_row, e_all, total, pos, unit, rnorm,
         kept=((4, 0), (5, 1), (6, 2), (7, 3), (8, 4)), flops=block_flops, name="seal",
     )
     peer_note = in_chip(own_note)
+    losses, token = call(lose, [row, shape((8, 128), F32)], total, pos, name="lose")
     pair = jnp.concatenate([own_note, peer_note], axis=0)
     odd_note = swap_odd(pair)
     even_note = swap_even(pair)
     (dz,) = call(
         finish, [shape((rows, width), BF16)], goal, inverse, own_note, peer_note, odd_note, even_note, e_all,
-        emb, peer, even, odd, relay, unit, rnorm,
+        emb, peer, even, odd, relay, unit, rnorm, token,
         scratch=[pltpu.VMEM((2, rows, rows), BF16), pltpu.VMEM((rows, width), F32)],
         flops=5 * block_flops, name="finish",
     )
     dz_other = in_chip(dz)
-    frame_grad = dot_nt(dz, head).astype(BF16)
 
     (partial,) = call(head_own, [shape((half, width), F32)], mine, dz, flops=2 * half * rows * width, name="head_own")
     (partial,) = call(
@@ -332,7 +344,29 @@
     (copies,) = call(add_up, [shape((32, *share), BF16)], got, name="add_far")
     own = lax.all_to_all(copies, NEAR, split_axis=0, concat_axis=0).reshape(2, half, width // 2)
     other = in_chip(own)
-    head_grad = place_half(other, place_half(own))
+    anywhere = pl.BlockSpec(memory_space=pl.ANY)
+    frame_grad, head_grad = pl.pallas_call(
+        ends,
+        in_specs=[vmem, vmem, anywhere],
+        out_specs=[anywhere] * 2,
+        out_shape=[shape((rows, depth), BF16), shape((depth, width), BF16)],
+        scratch_shapes=[
+            pltpu.VMEM((rows, depth), BF16), pltpu.SemaphoreType.DMA((2, 2)), pltpu.SemaphoreType.DMA((3,))
+        ],
+        name="ends",
+        compiler_params=pltpu.CompilerParams(vmem_limit_bytes=16 * 2**20),
+        cost_estimate=pl.CostEstimate(flops=2 * rows * depth * width, bytes_accessed=2**22, transcendentals=0),
+    )(dz, head, own)
+    head_grad = pl.pallas_call(
+        last_half,
+        in_specs=[anywhere] * 2,
+        out_specs=anywhere,
+        out_shape=shape((depth, width), BF16),
+        scratch_shapes=[pltpu.SemaphoreType.DMA((2, 2))],
+        input_output_aliases={1: 0},
+        name="last_half",
+        compiler_params=pltpu.CompilerParams(vmem_limit_bytes=2**20),
+    )(other, head_grad)
     return (losses.reshape(rows), frame_grad, head_grad)
 
 

time: 123 us -> 120 us (0.976)
  matrix products: 2.56 us -> 0 us
    dot_general x1 -> x0, matrix products: 2.56 us -> none  [dot_nt(): lax.dot_general(left, right, (((1,), (1,)), ((), ())), preferred_element_...]
    pallas_call x10 -> x11, Pallas kernels: 10 us -> 9.89 us  [call(): pl.pallas_call(body, out_shape=out, in_specs=[vmem] * len(arrays), out_sp...]
  transfers between devices with their start and end apart: 10 -> 10, of which waited for: 6 -> 5; matrix products, arithmetic and copies ran while one was open for 2% -> 0% of each run, Pallas kernels for 7% -> 9%
where the time goes in v4:
time: 120 us
  blocking collectives  56.1 us (47%)
  starting transfers between devices  27.1 us (23%)
  waiting for transfers between devices  18.3 us (15%)
  Pallas kernels  17 us (14%)
    ppermute x10, starting transfers between devices, send(): return lax.ppermute(x, ALL, [(i, to(i) % 256) for i in range(256)])  27.1 us
    all_to_all x1, blocking collectives, on_device(): lax.all_to_all(partial.reshape(32, *share), NEAR, split_axis=0, concat_ax...  21.4 us
    all_to_all x1, blocking collectives, on_device(): lax.all_to_all(copies, NEAR, split_axis=0, concat_axis=0)  19.5 us
    ppermute x10, waiting for transfers between devices, send(): return lax.ppermute(x, ALL, [(i, to(i) % 256) for i in range(256)])  18.3 us
    all_to_all x1, blocking collectives, on_device(): got = lax.all_to_all(copies, 'zh', split_axis=0, concat_axis=0)  15.3 us
    pallas_call x11, Pallas kernels, call(): pl.pallas_call(body, out_shape=out, in_specs=[vmem] * len(arrays), out_sp...  9.89 us
    pallas_call x1, Pallas kernels, on_device(): pl.pallas_call(embed, in_specs=[hbm, hbm], out_specs=[vmem] * 3, out_shap...  3.52 us
    pallas_call x1, Pallas kernels, on_device(): pl.pallas_call(ends, in_specs=[vmem, vmem, anywhere], out_specs=[anywhere...  2.53 us
  transfers between devices with their start and end apart: 10, of which 5 were waited for; matrix products, arithmetic and copies ran while one was open for 0% of the time, Pallas kernels for 9%

profile of v4, /device:TPU:1, one launch (start us, length us, event | category | flops | bytes accessed | tf_op | source)
XLA Modules:
  0.0 119.6 jit_solution(6772946643216890331)
XLA Ops:
  0.6 0.0 copy-start.1
  0.6 3.5 %embed.1 = (bf16[512,768]{1,0:T(8,128)(2,1)S(1)}, f32[512,768]{1,0:T(8,128)S(1)}, f32[512,1]{1,0:T(8,128)S(1)}) custom-call(bf16[512,1536]{1,0:T(8,128)(2,1)} %frames.3, bf16[1536,768]{1,0:T(8,128)(2,1)} %head.3), custom_call_target="tpu_custom_call" | custom-call | flops 1207959552 | bytes 4194304 | tf_op jit(solution)/shard_map/embed/pallas_call | solution.py:285
  4.2 3.3 %collective-permute-start.2 = (bf16[512,768]{1,0:T(8,128)(2,1)S(1)}, bf16[512,768]{1,0:T(8,128)(2,1)S(1)}, u32[]{:S(2)}, u32[]{:S(2)}) collective-permute-start(bf16[512,768]{1,0:T(8,128)(2,1)S(1)} %get-tuple-element.31.emb), channel_id=1, source_target_pairs={{0,1},{1,0},{2,3},{3,2},{4,5},{5,4},{6,7},{7,6},{8,9},{9,8},{10,11... | collective-permute-start | bytes 2359304 | tf_op jit(solution)/shard_map/ppermute | solution.py:19
  7.5 0.0 collective-permute-start.1
  7.5 9.0 %collective-permute-start = (bf16[512,768]{1,0:T(8,128)(2,1)S(1)}, bf16[512,768]{1,0:T(8,128)(2,1)S(1)}, u32[]{:S(2)}, u32[]{:S(2)}) collective-permute-start(bf16[512,768]{1,0:T(8,128)(2,1)S(1)} %get-tuple-element.31.emb), channel_id=1, source_target_pairs={{0,254},{1,255},{2,4},{3,5},{4,2},{5,3},{6,8},{7,9},{8,6},{9,7},{1... | collective-permute-start | bytes 2359304 | tf_op jit(solution)/shard_map/ppermute | solution.py:19
  16.6 0.0 collective-permute-done.2.peer
  16.6 0.0 copy-done.1
  16.6 0.0 copy-start
  16.6 1.3 %near.1 = (f32[5,512,512]{2,1,0:T(8,128)S(1)}, f32[512,1]{1,0:T(8,128)S(1)}, f32[512,1]{1,0:T(8,128)S(1)}, f32[512,768]{1,0:T(8,128)S(1)}, f32[512,1]{1,0:T(8,12...) custom-call(bf16[512,768]{1,0:T(8,128)(2,1)S(1)} %get-tuple-element.31.emb, ...), custom_call_target="tpu_custom_call", output_to_operand_aliasing={{3}: (3, {}), {4}: (4, {})} | custom-call | flops 805306368 | bytes 9975808 | tf_op jit(solution)/shard_map/near/pallas_call | solution.py:53
  17.9 0.1 copy-done
  18.0 0.5 turn.1
  18.4 8.2 %collective-permute-done.1.even = bf16[512,768]{1,0:T(8,128)(2,1)S(1)} collective-permute-done((bf16[512,768]{1,0:T(8,128)(2,1)S(1)}, bf16[512,768]{1,0:T(8,128)(2,1)S(1)}, u32[]{:S(2)}, u32[]{:S(2)}) %collective-permute-start.1) | collective-permute-done | bytes 786464 | tf_op jit(solution)/shard_map/ppermute | solution.py:19
  26.6 7.6 %collective-permute-done.odd = bf16[512,768]{1,0:T(8,128)(2,1)S(1)} collective-permute-done((bf16[512,768]{1,0:T(8,128)(2,1)S(1)}, bf16[512,768]{1,0:T(8,128)(2,1)S(1)}, u32[]{:S(2)}, u32[]{:S(2)}) %collective-permute-start) | collective-permute-done | bytes 786464 | tf_op jit(solution)/shard_map/ppermute | solution.py:19
  34.2 0.1 pick.1
  34.3 0.9 collective-permute-start.3
  35.2 1.3 %far.1 = (f32[5,512,512]{2,1,0:T(8,128)S(1)}, f32[512,1]{1,0:T(8,128)S(1)}, f32[512,1]{1,0:T(8,128)S(1)}, f32[512,768]{1,0:T(8,128)S(1)}, f32[512,1]{1,0:T(8,128)S(1)}) custom-call(bf16[512,768]{1,0:T(8,128)(2,1)S(1)} %get-tuple-element.31.emb, ...), custom_call_target="tpu_custom_call", output_to_operand_aliasing={{0}: (4, {}), {1}: (5, {}), {2}: (6, {}), {3}: (7, {}), {4}... | custom-call | flops 805306368 | bytes 16005120 | tf_op jit(solution)/shard_map/far/pallas_call | solution.py:53
  36.5 0.6 collective-permute-done.3.relay
  37.1 1.0 seal.1
  38.1 0.4 collective-permute-start.4
  38.5 0.8 collective-permute-done.4.peer_note
  39.4 0.1 collective-permute-start.6
  39.5 7.0 %collective-permute-start.5 = (f32[4,512]{1,0:T(4,128)S(1)}, f32[4,512]{1,0:T(4,128)S(1)}, u32[]{:S(2)}, u32[]{:S(2)}) collective-permute-start(f32[4,512]{1,0:T(4,128)S(1)} %pad_maximum_fusion), channel_id=1, source_target_pairs={{0,254},{1,255},{2,4},{3,5},{4,2},{5,3},{6,8},{7,9},{8,6},{9,7},{1... | collective-permute-start | bytes 24584 | tf_op jit(solution)/shard_map/ppermute | solution.py:19
  46.5 0.6 collective-permute-start.7
  47.1 0.8 lose.1
  47.9 0.0 collective-permute-done.6.even_note
  47.9 0.0 collective-permute-done.5.odd_note
  47.9 3.1 %finish.1.dz = bf16[512,768]{1,0:T(8,128)(2,1)S(1)} custom-call(s32[512,1]{1,0:T(8,128)S(1)} %get-tuple-element.36.goal, f32[512,1]{1,0:T(8,128)S(1)} %get-tuple-element.50.inverse, f32[2,512]{1,0:T(2,128)S(1)} %get-tuple-element.51.own_note, f32[2,512]{1,0:T(2,128)S(1)} %collective-permute-done.4.peer_note, f32[4,512]{1,0:T(4,128)S(1)} %collective-permute-done.5.odd_note, ...), custom_call_target="tpu_custom_call" | custom-call | flops 2013265920 | bytes 11569152 | tf_op jit(solution)/shard_map/finish/pallas_call | solution.py:53
  51.1 1.2 collective-permute-start.8
  52.2 0.8 head_own.1.part
  53.0 0.0 collective-permute-done.7.left
  53.0 1.1 collective-permute-done.8.dz
  54.1 0.8 head_both.1
  54.9 21.4 %all_to_all.15.got = bf16[32,48,384]{2,1,0:T(8,128)(2,1)S(1)} all-to-all(bf16[32,48,384]{2,1,0:T(8,128)(2,1)S(1)} %bitcast.4), channel_id=1, replica_groups=mesh['zh'=4,'zl'=2,'y'=4,'x'=4,'core'=2] {'zl','y','x'}, dimensions={0} | all-to-all | bytes 2359296 | tf_op jit(solution)/shard_map/all_to_all | solution.py:341
  76.3 0.2 add_near.1
  76.5 15.3 %all_to_all.16.got = bf16[4,48,384]{2,1,0:T(8,128)(2,1)S(1)} all-to-all(bf16[4,48,384]{2,1,0:T(8,128)(2,1)S(1)} %add_near.1), channel_id=1, replica_groups=mesh['zh'=4,'zl'=2,'y'=4,'x'=4,'core'=2] {'zh'}, dimensions={0} | all-to-all | bytes 294912 | tf_op jit(solution)/shard_map/all_to_all | solution.py:343
  91.7 0.0 copy-start.2
  91.7 0.1 add_far.1
  91.8 19.5 %all_to_all.17 = bf16[32,48,384]{2,1,0:T(8,128)(2,1)S(1)} all-to-all(bf16[32,48,384]{2,1,0:T(8,128)(2,1)S(1)} %add_far.1), channel_id=1, replica_groups=mesh['zh'=4,'zl'=2,'y'=4,'x'=4,'core'=2] {'zl','y','x'}, dimensions={0} | all-to-all | bytes 2359296 | tf_op jit(solution)/shard_map/all_to_all | solution.py:345
  111.3 4.5 %collective-permute-start.9 = (bf16[2,768,384]{2,1,0:T(8,128)(2,1)S(1)}, bf16[2,768,384]{2,1,0:T(8,128)(2,1)S(1)}, u32[]{:S(2)}, u32[]{:S(2)}) collective-permute-start(bf16[2,768,384]{2,1,0:T(8,128)(2,1)S(1)} %bitcast.5), channel_id=1, source_target_pairs={{0,1},{1,0},{2,3},{3,2},{4,5},{5,4},{6,7},{7,6},{8,9},{9,8},{10,11... | collective-permute-start | bytes 3538952 | tf_op jit(solution)/shard_map/ppermute | solution.py:19
  115.8 0.0 copy-done.2
  115.8 2.5 %ends.1 = (bf16[512,1536]{1,0:T(8,128)(2,1)}, bf16[1536,768]{1,0:T(8,128)(2,1)}) custom-call(bf16[512,768]{1,0:T(8,128)(2,1)S(1)} %finish.1.dz, bf16[1536,768]{1,0:T(8,128)(2,1)S(1)} %copy-done.2, bf16[2,768,384]{2,1,0:T(8,128)(2,1)S(1)} %bitcast.6), custom_call_target="tpu_custom_call" | custom-call | flops 1207959552 | bytes 4194304 | tf_op jit(solution)/shard_map/ends/pallas_call | solution.py:348
  118.4 0.0 collective-permute-done.9.other
  118.4 1.1 last_half.1
  (1 shorter events, 0.0 us)
Async XLA Ops:
  0.6 15.9 %copy-start.1 = (s32[512]{0:T(512)S(1)}, s32[512]{0:T(512)}, u32[]{:S(2)}) copy-start(s32[512]{0:T(512)} %param.5) | copy-start | bytes 6148
  4.2 12.4 %collective-permute-start.2 = (bf16[512,768]{1,0:T(8,128)(2,1)S(1)}, bf16[512,768]{1,0:T(8,128)(2,1)S(1)}, u32[]{:S(2)}, u32[]{:S(2)}) collective-permute-start(bf16[512,768]{1,0:T(8,128)(2,1)S(1)} %get-tuple-element.31.emb), channel_id=1, source_target_pairs={{0,1},{1,0},{2,3},{3,2},{4,5},{5,4},{6,7},{7,6},{8,9},{9,8},{10,11... | collective-permute-start | bytes 2359304 | tf_op jit(solution)/shard_map/ppermute | solution.py:19
  7.5 19.1 %collective-permute-start.1 = (bf16[512,768]{1,0:T(8,128)(2,1)S(1)}, bf16[512,768]{1,0:T(8,128)(2,1)S(1)}, u32[]{:S(2)}, u32[]{:S(2)}) collective-permute-start(bf16[512,768]{1,0:T(8,128)(2,1)S(1)} %get-tuple-element.31.emb), channel_id=1, source_target_pairs={{0,2},{1,3},{2,0},{3,1},{4,6},{5,7},{6,4},{7,5},{8,10},{9,11},{10,... | collective-permute-start | bytes 2359304 | tf_op jit(solution)/shard_map/ppermute | solution.py:19
  7.5 26.7 %collective-permute-start = (bf16[512,768]{1,0:T(8,128)(2,1)S(1)}, bf16[512,768]{1,0:T(8,128)(2,1)S(1)}, u32[]{:S(2)}, u32[]{:S(2)}) collective-permute-start(bf16[512,768]{1,0:T(8,128)(2,1)S(1)} %get-tuple-element.31.emb), channel_id=1, source_target_pairs={{0,254},{1,255},{2,4},{3,5},{4,2},{5,3},{6,8},{7,9},{8,6},{9,7},{1... | collective-permute-start | bytes 2359304 | tf_op jit(solution)/shard_map/ppermute | solution.py:19
  16.6 1.4 %copy-start = (bf16[512,1536]{1,0:T(8,128)(2,1)S(1)}, bf16[512,1536]{1,0:T(8,128)(2,1)}, u32[]{:S(2)}) copy-start(bf16[512,1536]{1,0:T(8,128)(2,1)} %frames.3) | copy-start | bytes 4718596
  34.3 2.8 %collective-permute-start.3 = (bf16[512,768]{1,0:T(8,128)(2,1)S(1)}, bf16[512,768]{1,0:T(8,128)(2,1)S(1)}, u32[]{:S(2)}, u32[]{:S(2)}) collective-permute-start(bf16[512,768]{1,0:T(8,128)(2,1)S(1)} %pick.1), channel_id=1, source_target_pairs={{0,1},{1,0},{2,3},{3,2},{4,5},{5,4},{6,7},{7,6},{8,9},{9,8},{10,11... | collective-permute-start | bytes 2359304 | tf_op jit(solution)/shard_map/ppermute | solution.py:19
  38.1 1.3 %collective-permute-start.4 = (f32[2,512]{1,0:T(2,128)S(1)}, f32[2,512]{1,0:T(2,128)S(1)}, u32[]{:S(2)}, u32[]{:S(2)}) collective-permute-start(f32[2,512]{1,0:T(2,128)S(1)} %get-tuple-element.51.own_note), channel_id=1, source_target_pairs={{0,1},{1,0},{2,3},{3,2},{4,5},{5,4},{6,7},{7,6},{8,9},{9,8},{10,11... | collective-permute-start | bytes 12296 | tf_op jit(solution)/shard_map/ppermute | solution.py:19
  39.4 8.5 %collective-permute-start.6 = (f32[4,512]{1,0:T(4,128)S(1)}, f32[4,512]{1,0:T(4,128)S(1)}, u32[]{:S(2)}, u32[]{:S(2)}) collective-permute-start(f32[4,512]{1,0:T(4,128)S(1)} %pad_maximum_fusion), channel_id=1, source_target_pairs={{0,2},{1,3},{2,0},{3,1},{4,6},{5,7},{6,4},{7,5},{8,10},{9,11},{10,... | collective-permute-start | bytes 24584 | tf_op jit(solution)/shard_map/ppermute | solution.py:19
  39.5 8.4 %collective-permute-start.5 = (f32[4,512]{1,0:T(4,128)S(1)}, f32[4,512]{1,0:T(4,128)S(1)}, u32[]{:S(2)}, u32[]{:S(2)}) collective-permute-start(f32[4,512]{1,0:T(4,128)S(1)} %pad_maximum_fusion), channel_id=1, source_target_pairs={{0,254},{1,255},{2,4},{3,5},{4,2},{5,3},{6,8},{7,9},{8,6},{9,7},{1... | collective-permute-start | bytes 24584 | tf_op jit(solution)/shard_map/ppermute | solution.py:19
  46.5 6.5 %collective-permute-start.7 = (bf16[768,512]{1,0:T(8,128)(2,1)S(1)}, bf16[768,512]{1,0:T(8,128)(2,1)S(1)}, u32[]{:S(2)}, u32[]{:S(2)}) collective-permute-start(bf16[768,512]{1,0:T(8,128)(2,1)S(1)} %get-tuple-element.35.token), channel_id=1, source_target_pairs={{0,1},{1,0},{2,3},{3,2},{4,5},{5,4},{6,7},{7,6},{8,9},{9,8},{10,11... | collective-permute-start | bytes 2359304 | tf_op jit(solution)/shard_map/ppermute | solution.py:19
  51.1 3.1 %collective-permute-start.8 = (bf16[512,768]{1,0:T(8,128)(2,1)S(1)}, bf16[512,768]{1,0:T(8,128)(2,1)S(1)}, u32[]{:S(2)}, u32[]{:S(2)}) collective-permute-start(bf16[512,768]{1,0:T(8,128)(2,1)S(1)} %finish.1.dz), channel_id=1, source_target_pairs={{0,1},{1,0},{2,3},{3,2},{4,5},{5,4},{6,7},{7,6},{8,9},{9,8},{10,11... | collective-permute-start | bytes 2359304 | tf_op jit(solution)/shard_map/ppermute | solution.py:19
  91.7 24.1 %copy-start.2 = (bf16[1536,768]{1,0:T(8,128)(2,1)S(1)}, bf16[1536,768]{1,0:T(8,128)(2,1)}, u32[]{:S(2)}) copy-start(bf16[1536,768]{1,0:T(8,128)(2,1)} %head.3) | copy-start | bytes 7077892
  111.3 7.0 %collective-permute-start.9 = (bf16[2,768,384]{2,1,0:T(8,128)(2,1)S(1)}, bf16[2,768,384]{2,1,0:T(8,128)(2,1)S(1)}, u32[]{:S(2)}, u32[]{:S(2)}) collective-permute-start(bf16[2,768,384]{2,1,0:T(8,128)(2,1)S(1)} %bitcast.5), channel_id=1, source_target_pairs={{0,1},{1,0},{2,3},{3,2},{4,5},{5,4},{6,7},{7,6},{8,9},{9,8},{10,11... | collective-permute-start | bytes 3538952 | tf_op jit(solution)/shard_map/ppermute | solution.py:19

commit v5 on v4

--- a/solution.py
+++ b/solution.py
@@ -12,7 +12,7 @@
 SIZES = (4, 2, 4, 4, 2)
 NEAR = ("zl", "y", "x")
 F32, BF16 = jnp.float32, jnp.bfloat16
-TILE, WIDE, PIECES = 128, 256, 2
+TILE, WIDE = 128, 256
 
 
 def send(x, to):
@@ -65,22 +65,19 @@
 
 def embed(frames, head, emb, unit, rnorm, f, h, acc, sems):
     depth = head.shape[0]
-    step = depth // PIECES
+    cuts = (pl.ds(0, 2 * depth // 3), pl.ds(2 * depth // 3, depth // 3))
     copies = []
-    for k in range(PIECES):
-        cut = pl.ds(k * step, step)
+    for k, cut in enumerate(cuts):
         copies.append(pltpu.make_async_copy(frames.at[:, cut], f.at[:, cut], sems.at[0, k]))
         copies.append(pltpu.make_async_copy(head.at[cut, :], h.at[cut, :], sems.at[1, k]))
     for c in copies:
         c.start()
-    for k in range(PIECES):
-        cut = pl.ds(k * step, step)
-        copies[2 * k].wait()
-        copies[2 * k + 1].wait()
-        if k == 0:
-            acc[...] = dot(f[:, cut], h[cut, :])
-        elif k < PIECES - 1:
-            acc[...] += dot(f[:, cut], h[cut, :])
+    copies[0].wait()
+    copies[1].wait()
+    acc[...] = dot(f[:, cuts[0]], h[cuts[0], :])
+    copies[2].wait()
+    copies[3].wait()
+    cut = cuts[1]
     for r in range(0, acc.shape[0], WIDE):
         rows = pl.ds(r, WIDE)
         z = acc[rows, :] + dot(f[rows, cut], h[cut, :])
@@ -105,7 +102,7 @@
     return (0, core, 2 * chip_sign(), -2 * chip_sign(), -core)
 
 
-def pick(odd, even, token, out):
+def pick(even, odd, token, out):
     out[...] = even[...]
 
     @pl.when(crossed())
@@ -171,13 +168,9 @@
     token[...] = jnp.zeros_like(token)
 
 
-def slope(e, at, goal, inverse, their_inverse, their_goal, rows):
-    width = e.shape[1]
-    i = lax.broadcasted_iota(jnp.int32, e.shape, 0) + rows.start
-    j = lax.broadcasted_iota(jnp.int32, e.shape, 1) + at * width
-    ours = (j == goal[rows, :]).astype(F32)
-    theirs = (i == their_goal + at * width).astype(F32)
-    return e * (inverse[rows, :] + their_inverse) - ours - theirs
+def slope(e, inverse, their_inverse, left, right):
+    weight = e * (inverse + their_inverse)
+    return jnp.where(left == right, weight - 1.0, weight)
 
 
 def finish(
@@ -188,11 +181,21 @@
     even_note, odd_note = even_note[...], odd_note[...]
     relay_note = jnp.where(crossed(), even_note, odd_note)[2:]
     notes = (own_note[...], peer_note[...], even_note[:2], odd_note[:2], relay_note)
+    size = g.shape[1]
+    ids = lax.broadcasted_iota(jnp.int32, (1, size), 1)
     for k, (note, block) in enumerate(zip(notes, (emb, peer, even, odd, relay))):
         their_inverse, their_goal = note[0:1], note[1:2].astype(jnp.int32)
-        for r in range(0, g.shape[1], TILE):
+        shift = at[k] * size
+        ahead = at[k] >= 0
+        right = jnp.where(ahead, ids + shift, their_goal + shift)
+        for r in range(0, size, TILE):
             rows = pl.ds(r, TILE)
-            g[k % 2, rows, :] = slope(e_all[k, rows, :], at[k], goal, inverse, their_inverse, their_goal, rows).astype(BF16)
+            mine = lax.broadcasted_iota(jnp.int32, (TILE, 1), 0) + r
+            left = jnp.where(ahead, goal[rows, :], mine)
+            weight = slope(e_all[k, rows, :], inverse[rows, :], their_inverse, left, right)
+            if k == 0:
+                weight = jnp.where(mine == their_goal, weight - 1.0, weight)
+            g[k % 2, rows, :] = weight.astype(BF16)
         if k == 0:
             acc[...] = dot(g[0], block[...])
         else:
@@ -291,7 +294,7 @@
             pltpu.VMEM((rows, depth), BF16),
             pltpu.VMEM((depth, width), BF16),
             pltpu.VMEM((rows, width), F32),
-            pltpu.SemaphoreType.DMA((2, PIECES)),
+            pltpu.SemaphoreType.DMA((2, 2)),
         ],
         name="embed",
         compiler_params=pltpu.CompilerParams(vmem_limit_bytes=51 * 2**20),
@@ -308,7 +311,7 @@
         kept=((3, 3), (4, 4)), flops=2 * block_flops, name="near",
     )
     mine, theirs = call(turn, [shape((half, rows), BF16)] * 2, frames, pos, name="turn")
-    (shared,) = call(pick, [shape((rows, width), BF16)], odd, even, theirs, name="pick")
+    (shared,) = call(pick, [shape((rows, width), BF16)], even, odd, theirs, name="pick")
     relay = in_chip(shared)
     theirs = in_chip(theirs)
     e_all, total, pos, unit, rnorm = call(

time: 120 us -> 119 us (level)
  waiting for transfers between devices: 18.3 us -> 20.5 us
  blocking collectives: 56.1 us -> 54.4 us
    ppermute x10, waiting for transfers between devices: 18.3 us -> 20.5 us  [send(): return lax.ppermute(x, ALL, [(i, to(i) % 256) for i in range(256)])]
    all_to_all x1, blocking collectives: 15.3 us -> 13.6 us  [on_device(): got = lax.all_to_all(copies, 'zh', split_axis=0, concat_axis=0)]
  transfers between devices with their start and end apart: 10 -> 10, of which waited for: 5 -> 6; matrix products, arithmetic and copies ran while one was open for 0% -> 0% of each run, Pallas kernels for 9% -> 9%
where the time goes in v5:
time: 119 us
  blocking collectives  54.4 us (46%)
  starting transfers between devices  26.1 us (22%)
  waiting for transfers between devices  20.5 us (17%)
  Pallas kernels  17 us (14%)
    ppermute x10, starting transfers between devices, send(): return lax.ppermute(x, ALL, [(i, to(i) % 256) for i in range(256)])  26.1 us
    all_to_all x1, blocking collectives, on_device(): lax.all_to_all(partial.reshape(32, *share), NEAR, split_axis=0, concat_ax...  21.4 us
    ppermute x10, waiting for transfers between devices, send(): return lax.ppermute(x, ALL, [(i, to(i) % 256) for i in range(256)])  20.5 us
    all_to_all x1, blocking collectives, on_device(): lax.all_to_all(copies, NEAR, split_axis=0, concat_axis=0)  19.5 us
    all_to_all x1, blocking collectives, on_device(): got = lax.all_to_all(copies, 'zh', split_axis=0, concat_axis=0)  13.6 us
    pallas_call x11, Pallas kernels, call(): pl.pallas_call(body, out_shape=out, in_specs=[vmem] * len(arrays), out_sp...  9.77 us
    pallas_call x1, Pallas kernels, on_device(): pl.pallas_call(embed, in_specs=[hbm, hbm], out_specs=[vmem] * 3, out_shap...  3.62 us
    pallas_call x1, Pallas kernels, on_device(): pl.pallas_call(ends, in_specs=[vmem, vmem, anywhere], out_specs=[anywhere...  2.53 us
  transfers between devices with their start and end apart: 10, of which 6 were waited for; matrix products, arithmetic and copies ran while one was open for 0% of the time, Pallas kernels for 9%

profile of v5, /device:TPU:1, one launch (start us, length us, event | category | flops | bytes accessed | tf_op | source)
XLA Modules:
  0.0 119.0 jit_solution(12677409749699942833)
XLA Ops:
  0.6 0.0 copy-start.1
  0.6 3.6 %embed.1 = (bf16[512,768]{1,0:T(8,128)(2,1)S(1)}, f32[512,768]{1,0:T(8,128)S(1)}, f32[512,1]{1,0:T(8,128)S(1)}) custom-call(bf16[512,1536]{1,0:T(8,128)(2,1)} %frames.3, bf16[1536,768]{1,0:T(8,128)(2,1)} %head.3), custom_call_target="tpu_custom_call" | custom-call | flops 1207959552 | bytes 4194304 | tf_op jit(solution)/shard_map/embed/pallas_call | solution.py:288
  4.3 3.3 %collective-permute-start.2 = (bf16[512,768]{1,0:T(8,128)(2,1)S(1)}, bf16[512,768]{1,0:T(8,128)(2,1)S(1)}, u32[]{:S(2)}, u32[]{:S(2)}) collective-permute-start(bf16[512,768]{1,0:T(8,128)(2,1)S(1)} %get-tuple-element.31.emb), channel_id=1, source_target_pairs={{0,1},{1,0},{2,3},{3,2},{4,5},{5,4},{6,7},{7,6},{8,9},{9,8},{10,11... | collective-permute-start | bytes 2359304 | tf_op jit(solution)/shard_map/ppermute | solution.py:19
  7.6 8.5 %collective-permute-start.1 = (bf16[512,768]{1,0:T(8,128)(2,1)S(1)}, bf16[512,768]{1,0:T(8,128)(2,1)S(1)}, u32[]{:S(2)}, u32[]{:S(2)}) collective-permute-start(bf16[512,768]{1,0:T(8,128)(2,1)S(1)} %get-tuple-element.31.emb), channel_id=1, source_target_pairs={{0,254},{1,255},{2,4},{3,5},{4,2},{5,3},{6,8},{7,9},{8,6},{9,7},{1... | collective-permute-start | bytes 2359304 | tf_op jit(solution)/shard_map/ppermute | solution.py:19
  16.1 0.0 collective-permute-start
  16.1 0.0 collective-permute-done.2.peer
  16.1 0.0 copy-done.1
  16.1 0.0 copy-start
  16.1 1.3 %near.1 = (f32[5,512,512]{2,1,0:T(8,128)S(1)}, f32[512,1]{1,0:T(8,128)S(1)}, f32[512,1]{1,0:T(8,128)S(1)}, f32[512,768]{1,0:T(8,128)S(1)}, f32[512,1]{1,0:T(8,12...) custom-call(bf16[512,768]{1,0:T(8,128)(2,1)S(1)} %get-tuple-element.31.emb, ...), custom_call_target="tpu_custom_call", output_to_operand_aliasing={{3}: (3, {}), {4}: (4, {})} | custom-call | flops 805306368 | bytes 9975808 | tf_op jit(solution)/shard_map/near/pallas_call | solution.py:53
  17.4 0.1 copy-done
  17.5 0.5 turn.1
  18.0 15.9 %collective-permute-done.1.odd = bf16[512,768]{1,0:T(8,128)(2,1)S(1)} collective-permute-done((bf16[512,768]{1,0:T(8,128)(2,1)S(1)}, bf16[512,768]{1,0:T(8,128)(2,1)S(1)}, u32[]{:S(2)}, u32[]{:S(2)}) %collective-permute-start.1) | collective-permute-done | bytes 786464 | tf_op jit(solution)/shard_map/ppermute | solution.py:19
  33.9 1.0 collective-permute-done.even
  34.9 0.1 pick.1
  35.0 1.2 %collective-permute-start.3 = (bf16[512,768]{1,0:T(8,128)(2,1)S(1)}, bf16[512,768]{1,0:T(8,128)(2,1)S(1)}, u32[]{:S(2)}, u32[]{:S(2)}) collective-permute-start(bf16[512,768]{1,0:T(8,128)(2,1)S(1)} %pick.1), channel_id=1, source_target_pairs={{0,1},{1,0},{2,3},{3,2},{4,5},{5,4},{6,7},{7,6},{8,9},{9,8},{10,11... | collective-permute-start | bytes 2359304 | tf_op jit(solution)/shard_map/ppermute | solution.py:19
  36.2 1.3 %far.1 = (f32[5,512,512]{2,1,0:T(8,128)S(1)}, f32[512,1]{1,0:T(8,128)S(1)}, f32[512,1]{1,0:T(8,128)S(1)}, f32[512,768]{1,0:T(8,128)S(1)}, f32[512,1]{1,0:T(8,128)S(1)}) custom-call(bf16[512,768]{1,0:T(8,128)(2,1)S(1)} %get-tuple-element.31.emb, ...), custom_call_target="tpu_custom_call", output_to_operand_aliasing={{0}: (4, {}), {1}: (5, {}), {2}: (6, {}), {3}: (7, {}), {4}... | custom-call | flops 805306368 | bytes 16005120 | tf_op jit(solution)/shard_map/far/pallas_call | solution.py:53
  37.5 0.6 collective-permute-done.3.relay
  38.1 1.0 seal.1
  39.1 0.4 collective-permute-start.4
  39.6 0.8 collective-permute-done.4.peer_note
  40.4 0.1 collective-permute-start.6
  40.5 5.5 %collective-permute-start.5 = (f32[4,512]{1,0:T(4,128)S(1)}, f32[4,512]{1,0:T(4,128)S(1)}, u32[]{:S(2)}, u32[]{:S(2)}) collective-permute-start(f32[4,512]{1,0:T(4,128)S(1)} %pad_maximum_fusion), channel_id=1, source_target_pairs={{0,254},{1,255},{2,4},{3,5},{4,2},{5,3},{6,8},{7,9},{8,6},{9,7},{1... | collective-permute-start | bytes 24584 | tf_op jit(solution)/shard_map/ppermute | solution.py:19
  46.0 0.6 collective-permute-start.7
  46.7 0.8 lose.1
  47.5 0.0 collective-permute-done.6.even_note
  47.5 1.0 collective-permute-done.5.odd_note
  48.5 3.0 %finish.1.dz = bf16[512,768]{1,0:T(8,128)(2,1)S(1)} custom-call(s32[512,1]{1,0:T(8,128)S(1)} %get-tuple-element.36.goal, f32[512,1]{1,0:T(8,128)S(1)} %get-tuple-element.50.inverse, f32[2,512]{1,0:T(2,128)S(1)} %get-tuple-element.51.own_note, f32[2,512]{1,0:T(2,128)S(1)} %collective-permute-done.4.peer_note, f32[4,512]{1,0:T(4,128)S(1)} %collective-permute-done.5.odd_note, ...), custom_call_target="tpu_custom_call" | custom-call | flops 2013265920 | bytes 11569152 | tf_op jit(solution)/shard_map/finish/pallas_call | solution.py:53
  51.5 1.8 %collective-permute-start.8 = (bf16[512,768]{1,0:T(8,128)(2,1)S(1)}, bf16[512,768]{1,0:T(8,128)(2,1)S(1)}, u32[]{:S(2)}, u32[]{:S(2)}) collective-permute-start(bf16[512,768]{1,0:T(8,128)(2,1)S(1)} %finish.1.dz), channel_id=1, source_target_pairs={{0,1},{1,0},{2,3},{3,2},{4,5},{5,4},{6,7},{7,6},{8,9},{9,8},{10,11... | collective-permute-start | bytes 2359304 | tf_op jit(solution)/shard_map/ppermute | solution.py:19
  53.3 0.8 head_own.1.part
  54.1 0.0 collective-permute-done.7.left
  54.1 1.1 collective-permute-done.8.dz
  55.3 0.8 head_both.1
  56.0 21.4 %all_to_all.15.got = bf16[32,48,384]{2,1,0:T(8,128)(2,1)S(1)} all-to-all(bf16[32,48,384]{2,1,0:T(8,128)(2,1)S(1)} %bitcast.4), channel_id=1, replica_groups=mesh['zh'=4,'zl'=2,'y'=4,'x'=4,'core'=2] {'zl','y','x'}, dimensions={0} | all-to-all | bytes 2359296 | tf_op jit(solution)/shard_map/all_to_all | solution.py:344
  77.4 0.2 add_near.1
  77.6 13.6 %all_to_all.16.got = bf16[4,48,384]{2,1,0:T(8,128)(2,1)S(1)} all-to-all(bf16[4,48,384]{2,1,0:T(8,128)(2,1)S(1)} %add_near.1), channel_id=1, replica_groups=mesh['zh'=4,'zl'=2,'y'=4,'x'=4,'core'=2] {'zh'}, dimensions={0} | all-to-all | bytes 294912 | tf_op jit(solution)/shard_map/all_to_all | solution.py:346
  91.2 0.0 copy-start.2
  91.2 0.1 add_far.1
  91.3 19.5 %all_to_all.17 = bf16[32,48,384]{2,1,0:T(8,128)(2,1)S(1)} all-to-all(bf16[32,48,384]{2,1,0:T(8,128)(2,1)S(1)} %add_far.1), channel_id=1, replica_groups=mesh['zh'=4,'zl'=2,'y'=4,'x'=4,'core'=2] {'zl','y','x'}, dimensions={0} | all-to-all | bytes 2359296 | tf_op jit(solution)/shard_map/all_to_all | solution.py:348
  110.7 4.5 %collective-permute-start.9 = (bf16[2,768,384]{2,1,0:T(8,128)(2,1)S(1)}, bf16[2,768,384]{2,1,0:T(8,128)(2,1)S(1)}, u32[]{:S(2)}, u32[]{:S(2)}) collective-permute-start(bf16[2,768,384]{2,1,0:T(8,128)(2,1)S(1)} %bitcast.5), channel_id=1, source_target_pairs={{0,1},{1,0},{2,3},{3,2},{4,5},{5,4},{6,7},{7,6},{8,9},{9,8},{10,11... | collective-permute-start | bytes 3538952 | tf_op jit(solution)/shard_map/ppermute | solution.py:19
  115.2 0.0 copy-done.2
  115.2 2.5 %ends.1 = (bf16[512,1536]{1,0:T(8,128)(2,1)}, bf16[1536,768]{1,0:T(8,128)(2,1)}) custom-call(bf16[512,768]{1,0:T(8,128)(2,1)S(1)} %finish.1.dz, bf16[1536,768]{1,0:T(8,128)(2,1)S(1)} %copy-done.2, bf16[2,768,384]{2,1,0:T(8,128)(2,1)S(1)} %bitcast.6), custom_call_target="tpu_custom_call" | custom-call | flops 1207959552 | bytes 4194304 | tf_op jit(solution)/shard_map/ends/pallas_call | solution.py:351
  117.8 0.0 collective-permute-done.9.other
  117.8 1.1 last_half.1
  (1 shorter events, 0.0 us)
Async XLA Ops:
  0.6 15.5 %copy-start.1 = (s32[512]{0:T(512)S(1)}, s32[512]{0:T(512)}, u32[]{:S(2)}) copy-start(s32[512]{0:T(512)} %param.5) | copy-start | bytes 6148
  4.3 11.8 %collective-permute-start.2 = (bf16[512,768]{1,0:T(8,128)(2,1)S(1)}, bf16[512,768]{1,0:T(8,128)(2,1)S(1)}, u32[]{:S(2)}, u32[]{:S(2)}) collective-permute-start(bf16[512,768]{1,0:T(8,128)(2,1)S(1)} %get-tuple-element.31.emb), channel_id=1, source_target_pairs={{0,1},{1,0},{2,3},{3,2},{4,5},{5,4},{6,7},{7,6},{8,9},{9,8},{10,11... | collective-permute-start | bytes 2359304 | tf_op jit(solution)/shard_map/ppermute | solution.py:19
  7.6 26.3 %collective-permute-start.1 = (bf16[512,768]{1,0:T(8,128)(2,1)S(1)}, bf16[512,768]{1,0:T(8,128)(2,1)S(1)}, u32[]{:S(2)}, u32[]{:S(2)}) collective-permute-start(bf16[512,768]{1,0:T(8,128)(2,1)S(1)} %get-tuple-element.31.emb), channel_id=1, source_target_pairs={{0,254},{1,255},{2,4},{3,5},{4,2},{5,3},{6,8},{7,9},{8,6},{9,7},{1... | collective-permute-start | bytes 2359304 | tf_op jit(solution)/shard_map/ppermute | solution.py:19
  16.1 18.8 %collective-permute-start = (bf16[512,768]{1,0:T(8,128)(2,1)S(1)}, bf16[512,768]{1,0:T(8,128)(2,1)S(1)}, u32[]{:S(2)}, u32[]{:S(2)}) collective-permute-start(bf16[512,768]{1,0:T(8,128)(2,1)S(1)} %get-tuple-element.31.emb), channel_id=1, source_target_pairs={{0,2},{1,3},{2,0},{3,1},{4,6},{5,7},{6,4},{7,5},{8,10},{9,11},{10,... | collective-permute-start | bytes 2359304 | tf_op jit(solution)/shard_map/ppermute | solution.py:19
  16.1 1.4 %copy-start = (bf16[512,1536]{1,0:T(8,128)(2,1)S(1)}, bf16[512,1536]{1,0:T(8,128)(2,1)}, u32[]{:S(2)}) copy-start(bf16[512,1536]{1,0:T(8,128)(2,1)} %frames.3) | copy-start | bytes 4718596
  35.0 3.1 %collective-permute-start.3 = (bf16[512,768]{1,0:T(8,128)(2,1)S(1)}, bf16[512,768]{1,0:T(8,128)(2,1)S(1)}, u32[]{:S(2)}, u32[]{:S(2)}) collective-permute-start(bf16[512,768]{1,0:T(8,128)(2,1)S(1)} %pick.1), channel_id=1, source_target_pairs={{0,1},{1,0},{2,3},{3,2},{4,5},{5,4},{6,7},{7,6},{8,9},{9,8},{10,11... | collective-permute-start | bytes 2359304 | tf_op jit(solution)/shard_map/ppermute | solution.py:19
  39.1 1.3 %collective-permute-start.4 = (f32[2,512]{1,0:T(2,128)S(1)}, f32[2,512]{1,0:T(2,128)S(1)}, u32[]{:S(2)}, u32[]{:S(2)}) collective-permute-start(f32[2,512]{1,0:T(2,128)S(1)} %get-tuple-element.51.own_note), channel_id=1, source_target_pairs={{0,1},{1,0},{2,3},{3,2},{4,5},{5,4},{6,7},{7,6},{8,9},{9,8},{10,11... | collective-permute-start | bytes 12296 | tf_op jit(solution)/shard_map/ppermute | solution.py:19
  40.4 7.1 %collective-permute-start.6 = (f32[4,512]{1,0:T(4,128)S(1)}, f32[4,512]{1,0:T(4,128)S(1)}, u32[]{:S(2)}, u32[]{:S(2)}) collective-permute-start(f32[4,512]{1,0:T(4,128)S(1)} %pad_maximum_fusion), channel_id=1, source_target_pairs={{0,2},{1,3},{2,0},{3,1},{4,6},{5,7},{6,4},{7,5},{8,10},{9,11},{10,... | collective-permute-start | bytes 24584 | tf_op jit(solution)/shard_map/ppermute | solution.py:19
  40.5 8.0 %collective-permute-start.5 = (f32[4,512]{1,0:T(4,128)S(1)}, f32[4,512]{1,0:T(4,128)S(1)}, u32[]{:S(2)}, u32[]{:S(2)}) collective-permute-start(f32[4,512]{1,0:T(4,128)S(1)} %pad_maximum_fusion), channel_id=1, source_target_pairs={{0,254},{1,255},{2,4},{3,5},{4,2},{5,3},{6,8},{7,9},{8,6},{9,7},{1... | collective-permute-start | bytes 24584 | tf_op jit(solution)/shard_map/ppermute | solution.py:19
  46.0 8.1 %collective-permute-start.7 = (bf16[768,512]{1,0:T(8,128)(2,1)S(1)}, bf16[768,512]{1,0:T(8,128)(2,1)S(1)}, u32[]{:S(2)}, u32[]{:S(2)}) collective-permute-start(bf16[768,512]{1,0:T(8,128)(2,1)S(1)} %get-tuple-element.35.token), channel_id=1, source_target_pairs={{0,1},{1,0},{2,3},{3,2},{4,5},{5,4},{6,7},{7,6},{8,9},{9,8},{10,11... | collective-permute-start | bytes 2359304 | tf_op jit(solution)/shard_map/ppermute | solution.py:19
  51.5 3.7 %collective-permute-start.8 = (bf16[512,768]{1,0:T(8,128)(2,1)S(1)}, bf16[512,768]{1,0:T(8,128)(2,1)S(1)}, u32[]{:S(2)}, u32[]{:S(2)}) collective-permute-start(bf16[512,768]{1,0:T(8,128)(2,1)S(1)} %finish.1.dz), channel_id=1, source_target_pairs={{0,1},{1,0},{2,3},{3,2},{4,5},{5,4},{6,7},{7,6},{8,9},{9,8},{10,11... | collective-permute-start | bytes 2359304 | tf_op jit(solution)/shard_map/ppermute | solution.py:19
  91.2 24.1 %copy-start.2 = (bf16[1536,768]{1,0:T(8,128)(2,1)S(1)}, bf16[1536,768]{1,0:T(8,128)(2,1)}, u32[]{:S(2)}) copy-start(bf16[1536,768]{1,0:T(8,128)(2,1)} %head.3) | copy-start | bytes 7077892
  110.7 7.0 %collective-permute-start.9 = (bf16[2,768,384]{2,1,0:T(8,128)(2,1)S(1)}, bf16[2,768,384]{2,1,0:T(8,128)(2,1)S(1)}, u32[]{:S(2)}, u32[]{:S(2)}) collective-permute-start(bf16[2,768,384]{2,1,0:T(8,128)(2,1)S(1)} %bitcast.5), channel_id=1, source_target_pairs={{0,1},{1,0},{2,3},{3,2},{4,5},{5,4},{6,7},{7,6},{8,9},{9,8},{10,11... | collective-permute-start | bytes 3538952 | tf_op jit(solution)/shard_map/ppermute | solution.py:19

commit v6 on v5

--- a/solution.py
+++ b/solution.py
@@ -65,7 +65,7 @@
 
 def embed(frames, head, emb, unit, rnorm, f, h, acc, sems):
     depth = head.shape[0]
-    cuts = (pl.ds(0, 2 * depth // 3), pl.ds(2 * depth // 3, depth // 3))
+    cuts = (pl.ds(0, depth // 2), pl.ds(depth // 2, depth // 2))
     copies = []
     for k, cut in enumerate(cuts):
         copies.append(pltpu.make_async_copy(frames.at[:, cut], f.at[:, cut], sems.at[0, k]))
@@ -148,19 +148,37 @@
         pos[rows, :] += p
 
 
-def far(emb, even, odd, goal, e_in, total_in, pos_in, unit, rnorm, e_all, total, pos, *kept):
+def far(
+    emb, even, odd, peer, goal, goal_row, token, e_in, total_in, pos_in, unit, rnorm,
+    e_all, total, pos, unit_out, rnorm_out, note, part,
+):
+    def for_peer(block):
+        for r in range(0, peer.shape[0], WIDE):
+            rows = pl.ds(r, WIDE)
+            e = jnp.exp(SCALE * dot_nt(peer[rows, :], block[...]))
+            part[rows, :] = jnp.sum(e, axis=1, keepdims=True)
+
+    pl.when(crossed())(lambda: for_peer(odd))
+    pl.when(jnp.logical_not(crossed()))(lambda: for_peer(even))
     add_block(2, emb, even, goal, e_all, total, pos)
     add_block(3, emb, odd, goal, e_all, total, pos)
-
-
-def seal(
-    emb, relay, goal, goal_row, e_in, total_in, pos_in, unit, rnorm,
-    e_all, total, pos, unit_out, rnorm_out, inverse, note,
-):
+    note[0:1, :] = to_row(total[...])
+    note[1:2, :] = to_row(part[...])
+    note[2:3, :] = goal_row[...]
+    note[3:4, :] = jnp.zeros_like(goal_row)
+
+
+def combine(own, peer, pair, inverse):
+    inv = 1.0 / (own[0:1, :] + peer[1:2, :])
+    inverse[...] = to_column(inv)
+    pair[0:1, :] = inv
+    pair[1:2, :] = own[2:3, :]
+    pair[2:3, :] = 1.0 / (peer[0:1, :] + own[1:2, :])
+    pair[3:4, :] = peer[2:3, :]
+
+
+def seal(emb, relay, goal, e_in, total_in, pos_in, unit, rnorm, e_all, total, pos, *kept):
     add_block(4, emb, relay, goal, e_all, total, pos)
-    inverse[...] = 1.0 / total[...]
-    note[0:1, :] = to_row(inverse[...])
-    note[1:2, :] = goal_row[...]
 
 
 def lose(total, pos, losses, token):
@@ -174,32 +192,42 @@
 
 
 def finish(
-    goal, inverse, own_note, peer_note, odd_note, even_note, e_all, emb, peer, even, odd, relay, unit, rnorm, token,
+    goal, inverse, pair, even_note, odd_note, e_all, emb, peer, even, odd, relay, unit, rnorm, token,
     dz, g, acc,
 ):
     at = places()
-    even_note, odd_note = even_note[...], odd_note[...]
+    pair, even_note, odd_note = pair[...], even_note[...], odd_note[...]
     relay_note = jnp.where(crossed(), even_note, odd_note)[2:]
-    notes = (own_note[...], peer_note[...], even_note[:2], odd_note[:2], relay_note)
+    notes = (pair[:2], pair[2:], even_note[:2], odd_note[:2], relay_note)
+    blocks = (emb, peer, even, odd, relay)
     size = g.shape[1]
     ids = lax.broadcasted_iota(jnp.int32, (1, size), 1)
-    for k, (note, block) in enumerate(zip(notes, (emb, peer, even, odd, relay))):
+
+    def slopes(k, rows):
+        note = notes[k]
         their_inverse, their_goal = note[0:1], note[1:2].astype(jnp.int32)
         shift = at[k] * size
         ahead = at[k] >= 0
         right = jnp.where(ahead, ids + shift, their_goal + shift)
-        for r in range(0, size, TILE):
-            rows = pl.ds(r, TILE)
-            mine = lax.broadcasted_iota(jnp.int32, (TILE, 1), 0) + r
-            left = jnp.where(ahead, goal[rows, :], mine)
-            weight = slope(e_all[k, rows, :], inverse[rows, :], their_inverse, left, right)
+        mine = lax.broadcasted_iota(jnp.int32, (rows.size, 1), 0) + rows.start
+        left = jnp.where(ahead, goal[rows, :], mine)
+        weight = slope(e_all[k, rows, :], inverse[rows, :], their_inverse, left, right)
+        if k == 0:
+            weight = jnp.where(mine == their_goal, weight - 1.0, weight)
+        g[k % 2, rows, :] = weight.astype(BF16)
+
+    tiles = [pl.ds(r, WIDE) for r in range(0, size, WIDE)]
+    for rows in tiles:
+        slopes(0, rows)
+    for k, block in enumerate(blocks):
+        for rows in tiles:
+            product = dot(g[k % 2, rows, :], block[...])
+            if k + 1 < len(blocks):
+                slopes(k + 1, rows)
             if k == 0:
-                weight = jnp.where(mine == their_goal, weight - 1.0, weight)
-            g[k % 2, rows, :] = weight.astype(BF16)
-        if k == 0:
-            acc[...] = dot(g[0], block[...])
-        else:
-            acc[...] += dot(g[k % 2], block[...])
+                acc[rows, :] = product
+            else:
+                acc[rows, :] += product
     for r in range(0, emb.shape[0], TILE):
         rows = pl.ds(r, TILE)
         demb = SCALE * acc[rows, :]
@@ -311,25 +339,25 @@
         kept=((3, 3), (4, 4)), flops=2 * block_flops, name="near",
     )
     mine, theirs = call(turn, [shape((half, rows), BF16)] * 2, frames, pos, name="turn")
-    (shared,) = call(pick, [shape((rows, width), BF16)], even, odd, theirs, name="pick")
-    relay = in_chip(shared)
     theirs = in_chip(theirs)
-    e_all, total, pos, unit, rnorm = call(
-        far, [everything, col, col, tall, col], emb, even, odd, goal, e_all, total, pos, unit, rnorm,
-        kept=((4, 0), (5, 1), (6, 2), (7, 3), (8, 4)), flops=2 * block_flops, name="far",
-    )
-    e_all, total, pos, unit, rnorm, inverse, own_note = call(
-        seal, [everything, col, col, tall, col, col, note],
-        emb, relay, goal, goal_row, e_all, total, pos, unit, rnorm,
-        kept=((4, 0), (5, 1), (6, 2), (7, 3), (8, 4)), flops=block_flops, name="seal",
+    state, keep = [everything, col, col, tall, col], lambda k: tuple((k + j, j) for j in range(5))
+    note = shape((4, rows), F32)
+    e_all, total, pos, unit, rnorm, own_note = call(
+        far, state + [note], emb, even, odd, peer, goal, goal_row, theirs, e_all, total, pos, unit, rnorm,
+        kept=keep(7), scratch=[pltpu.VMEM((rows, 1), F32)], flops=3 * block_flops, name="far",
     )
     peer_note = in_chip(own_note)
-    losses, token = call(lose, [row, shape((8, 128), F32)], total, pos, name="lose")
-    pair = jnp.concatenate([own_note, peer_note], axis=0)
+    pair, inverse = call(combine, [note, col], own_note, peer_note, name="combine")
     odd_note = swap_odd(pair)
     even_note = swap_even(pair)
+    (shared,) = call(pick, [shape((rows, width), BF16)], even, odd, pair, name="pick")
+    relay = in_chip(shared)
+    e_all, total, pos, unit, rnorm = call(
+        seal, state, emb, relay, goal, e_all, total, pos, unit, rnorm, kept=keep(3), flops=block_flops, name="seal",
+    )
+    losses, token = call(lose, [row, shape((8, 128), F32)], total, pos, name="lose")
     (dz,) = call(
-        finish, [shape((rows, width), BF16)], goal, inverse, own_note, peer_note, odd_note, even_note, e_all,
+        finish, [shape((rows, width), BF16)], goal, inverse, pair, even_note, odd_note, e_all,
         emb, peer, even, odd, relay, unit, rnorm, token,
         scratch=[pltpu.VMEM((2, rows, rows), BF16), pltpu.VMEM((rows, width), F32)],
         flops=5 * block_flops, name="finish",

time: 119 us -> 119 us (level)
  waiting for transfers between devices: 20.5 us -> 17 us
  blocking collectives: 54.4 us -> 56.1 us
    ppermute x10, waiting for transfers between devices: 20.5 us -> 17 us  [send(): return lax.ppermute(x, ALL, [(i, to(i) % 256) for i in range(256)])]
    all_to_all x1, blocking collectives: 13.6 us -> 15.3 us  [on_device(): got = lax.all_to_all(copies, 'zh', split_axis=0, concat_axis=0)]
    pallas_call x11 -> x12, Pallas kernels: 9.77 us -> 10.6 us  [call(): pl.pallas_call(body, out_shape=out, in_specs=[vmem] * len(arrays), out_sp...]
  transfers between devices with their start and end apart: 10 -> 10, of which waited for: 6 -> 4; matrix products, arithmetic and copies ran while one was open for 0% -> 0% of each run, Pallas kernels for 9% -> 6%
where the time goes in v6:
time: 119 us
  blocking collectives  56.1 us (47%)
  starting transfers between devices  26.9 us (23%)
  Pallas kernels  17.7 us (15%)
  waiting for transfers between devices  17 us (14%)
    ppermute x10, starting transfers between devices, send(): return lax.ppermute(x, ALL, [(i, to(i) % 256) for i in range(256)])  26.9 us
    all_to_all x1, blocking collectives, on_device(): lax.all_to_all(partial.reshape(32, *share), NEAR, split_axis=0, concat_ax...  21.4 us
    all_to_all x1, blocking collectives, on_device(): lax.all_to_all(copies, NEAR, split_axis=0, concat_axis=0)  19.5 us
    ppermute x10, waiting for transfers between devices, send(): return lax.ppermute(x, ALL, [(i, to(i) % 256) for i in range(256)])  17 us
    all_to_all x1, blocking collectives, on_device(): got = lax.all_to_all(copies, 'zh', split_axis=0, concat_axis=0)  15.3 us
    pallas_call x12, Pallas kernels, call(): pl.pallas_call(body, out_shape=out, in_specs=[vmem] * len(arrays), out_sp...  10.6 us
    pallas_call x1, Pallas kernels, on_device(): pl.pallas_call(embed, in_specs=[hbm, hbm], out_specs=[vmem] * 3, out_shap...  3.52 us
    pallas_call x1, Pallas kernels, on_device(): pl.pallas_call(ends, in_specs=[vmem, vmem, anywhere], out_specs=[anywhere...  2.54 us
  transfers between devices with their start and end apart: 10, of which 4 were waited for; matrix products, arithmetic and copies ran while one was open for 0% of the time, Pallas kernels for 6%

profile of v6, /device:TPU:1, one launch (start us, length us, event | category | flops | bytes accessed | tf_op | source)
XLA Modules:
  0.0 118.7 jit_solution(5027629506841087479)
XLA Ops:
  0.6 0.0 copy-start.1
  0.6 3.5 %embed.1 = (bf16[512,768]{1,0:T(8,128)(2,1)S(1)}, f32[512,768]{1,0:T(8,128)S(1)}, f32[512,1]{1,0:T(8,128)S(1)}) custom-call(bf16[512,1536]{1,0:T(8,128)(2,1)} %frames.3, bf16[1536,768]{1,0:T(8,128)(2,1)} %head.3), custom_call_target="tpu_custom_call" | custom-call | flops 1207959552 | bytes 4194304 | tf_op jit(solution)/shard_map/embed/pallas_call | solution.py:316
  4.2 3.3 %collective-permute-start.2 = (bf16[512,768]{1,0:T(8,128)(2,1)S(1)}, bf16[512,768]{1,0:T(8,128)(2,1)S(1)}, u32[]{:S(2)}, u32[]{:S(2)}) collective-permute-start(bf16[512,768]{1,0:T(8,128)(2,1)S(1)} %get-tuple-element.32.emb), channel_id=1, source_target_pairs={{0,1},{1,0},{2,3},{3,2},{4,5},{5,4},{6,7},{7,6},{8,9},{9,8},{10,11... | collective-permute-start | bytes 2359304 | tf_op jit(solution)/shard_map/ppermute | solution.py:19
  7.5 0.0 collective-permute-start
  7.5 9.0 %collective-permute-start.1 = (bf16[512,768]{1,0:T(8,128)(2,1)S(1)}, bf16[512,768]{1,0:T(8,128)(2,1)S(1)}, u32[]{:S(2)}, u32[]{:S(2)}) collective-permute-start(bf16[512,768]{1,0:T(8,128)(2,1)S(1)} %get-tuple-element.32.emb), channel_id=1, source_target_pairs={{0,254},{1,255},{2,4},{3,5},{4,2},{5,3},{6,8},{7,9},{8,6},{9,7},{1... | collective-permute-start | bytes 2359304 | tf_op jit(solution)/shard_map/ppermute | solution.py:19
  16.6 0.0 collective-permute-done.2.peer
  16.6 0.0 copy-done.1
  16.6 0.0 copy-start
  16.6 1.3 %near.1 = (f32[5,512,512]{2,1,0:T(8,128)S(1)}, f32[512,1]{1,0:T(8,128)S(1)}, f32[512,1]{1,0:T(8,128)S(1)}, f32[512,768]{1,0:T(8,128)S(1)}, f32[512,1]{1,0:T(8,12...) custom-call(bf16[512,768]{1,0:T(8,128)(2,1)S(1)} %get-tuple-element.32.emb, ...), custom_call_target="tpu_custom_call", output_to_operand_aliasing={{3}: (3, {}), {4}: (4, {})} | custom-call | flops 805306368 | bytes 9975808 | tf_op jit(solution)/shard_map/near/pallas_call | solution.py:53
  17.9 0.1 copy-done
  18.0 0.5 turn.1
  18.4 0.7 collective-permute-start.3
  19.2 7.4 %collective-permute-done.even = bf16[512,768]{1,0:T(8,128)(2,1)S(1)} collective-permute-done((bf16[512,768]{1,0:T(8,128)(2,1)S(1)}, bf16[512,768]{1,0:T(8,128)(2,1)S(1)}, u32[]{:S(2)}, u32[]{:S(2)}) %collective-permute-start) | collective-permute-done | bytes 786464 | tf_op jit(solution)/shard_map/ppermute | solution.py:19
  26.6 7.6 %collective-permute-done.1.odd = bf16[512,768]{1,0:T(8,128)(2,1)S(1)} collective-permute-done((bf16[512,768]{1,0:T(8,128)(2,1)S(1)}, bf16[512,768]{1,0:T(8,128)(2,1)S(1)}, u32[]{:S(2)}, u32[]{:S(2)}) %collective-permute-start.1) | collective-permute-done | bytes 786464 | tf_op jit(solution)/shard_map/ppermute | solution.py:19
  34.2 0.0 collective-permute-done.3.token.left
  34.2 2.2 %far.1 = (f32[5,512,512]{2,1,0:T(8,128)S(1)}, f32[512,1]{1,0:T(8,128)S(1)}, f32[512,1]{1,0:T(8,128)S(1)}, f32[512,768]{1,0:T(8,128)S(1)}, f32[512,1]{1,0:T(8,128)S(1)}, /*index=5*/f32[4,512]{1,0:T(4,128)S(1)}) custom-call(bf16[512,768]{1,0:T(8,128)(2,1)S(1)} %get-tuple-element.32.emb, ...), custom_call_target="tpu_custom_call", output_to_operand_aliasing={{0}: (7, {}), {1}: (8, {}), {2}: (9, {}), {3}: (10, {}), {4... | custom-call | flops 1207959552 | bytes 17588224 | tf_op jit(solution)/shard_map/far/pallas_call | solution.py:53
  36.4 0.9 collective-permute-start.4
  37.4 0.8 collective-permute-done.4.peer
  38.2 0.1 combine.1
  38.3 0.1 pick.1
  38.4 0.4 collective-permute-start.5
  38.8 0.0 collective-permute-start.6
  38.8 6.9 %collective-permute-start.7 = (f32[4,512]{1,0:T(4,128)S(1)}, f32[4,512]{1,0:T(4,128)S(1)}, u32[]{:S(2)}, u32[]{:S(2)}) collective-permute-start(f32[4,512]{1,0:T(4,128)S(1)} %get-tuple-element.44.token.pair), channel_id=1, source_target_pairs={{0,254},{1,255},{2,4},{3,5},{4,2},{5,3},{6,8},{7,9},{8,6},{9,7},{1... | collective-permute-start | bytes 24584 | tf_op jit(solution)/shard_map/ppermute | solution.py:19
  45.8 0.0 collective-permute-done.5.relay
  45.8 0.8 seal.1
  46.6 0.8 lose.1
  47.3 0.0 collective-permute-done.6.even_note
  47.3 0.0 collective-permute-done.7.odd_note
  47.4 2.9 %finish.1.dz = bf16[512,768]{1,0:T(8,128)(2,1)S(1)} custom-call(s32[512,1]{1,0:T(8,128)S(1)} %get-tuple-element.35.goal, f32[512,1]{1,0:T(8,128)S(1)} %get-tuple-element.53.inverse, f32[4,512]{1,0:T(4,128)S(1)} %get-tuple-element.44.token.pair, f32[4,512]{1,0:T(4,128)S(1)} %collective-permute-done.6.even_note, f32[4,512]{1,0:T(4,128)S(1)} %collective-permute-done.7.odd_note, ...), custom_call_target="tpu_custom_call" | custom-call | flops 2013265920 | bytes 11569152 | tf_op jit(solution)/shard_map/finish/pallas_call | solution.py:53
  50.3 1.0 collective-permute-start.8
  51.3 0.8 head_own.1.part
  52.1 1.1 collective-permute-done.8.dz
  53.2 0.8 head_both.1
  54.0 21.4 %all_to_all.15.got = bf16[32,48,384]{2,1,0:T(8,128)(2,1)S(1)} all-to-all(bf16[32,48,384]{2,1,0:T(8,128)(2,1)S(1)} %bitcast.4), channel_id=1, replica_groups=mesh['zh'=4,'zl'=2,'y'=4,'x'=4,'core'=2] {'zl','y','x'}, dimensions={0} | all-to-all | bytes 2359296 | tf_op jit(solution)/shard_map/all_to_all | solution.py:372
  75.4 0.2 add_near.1
  75.5 15.3 %all_to_all.16.got = bf16[4,48,384]{2,1,0:T(8,128)(2,1)S(1)} all-to-all(bf16[4,48,384]{2,1,0:T(8,128)(2,1)S(1)} %add_near.1), channel_id=1, replica_groups=mesh['zh'=4,'zl'=2,'y'=4,'x'=4,'core'=2] {'zh'}, dimensions={0} | all-to-all | bytes 294912 | tf_op jit(solution)/shard_map/all_to_all | solution.py:374
  90.8 0.0 copy-start.2
  90.8 0.1 add_far.1
  90.9 19.5 %all_to_all.17 = bf16[32,48,384]{2,1,0:T(8,128)(2,1)S(1)} all-to-all(bf16[32,48,384]{2,1,0:T(8,128)(2,1)S(1)} %add_far.1), channel_id=1, replica_groups=mesh['zh'=4,'zl'=2,'y'=4,'x'=4,'core'=2] {'zl','y','x'}, dimensions={0} | all-to-all | bytes 2359296 | tf_op jit(solution)/shard_map/all_to_all | solution.py:376
  110.4 4.5 %collective-permute-start.9 = (bf16[2,768,384]{2,1,0:T(8,128)(2,1)S(1)}, bf16[2,768,384]{2,1,0:T(8,128)(2,1)S(1)}, u32[]{:S(2)}, u32[]{:S(2)}) collective-permute-start(bf16[2,768,384]{2,1,0:T(8,128)(2,1)S(1)} %bitcast.5), channel_id=1, source_target_pairs={{0,1},{1,0},{2,3},{3,2},{4,5},{5,4},{6,7},{7,6},{8,9},{9,8},{10,11... | collective-permute-start | bytes 3538952 | tf_op jit(solution)/shard_map/ppermute | solution.py:19
  114.9 0.0 copy-done.2
  114.9 2.5 %ends.1 = (bf16[512,1536]{1,0:T(8,128)(2,1)}, bf16[1536,768]{1,0:T(8,128)(2,1)}) custom-call(bf16[512,768]{1,0:T(8,128)(2,1)S(1)} %finish.1.dz, bf16[1536,768]{1,0:T(8,128)(2,1)S(1)} %copy-done.2, bf16[2,768,384]{2,1,0:T(8,128)(2,1)S(1)} %bitcast.6), custom_call_target="tpu_custom_call" | custom-call | flops 1207959552 | bytes 4194304 | tf_op jit(solution)/shard_map/ends/pallas_call | solution.py:379
  117.4 0.0 collective-permute-done.9.other
  117.4 1.1 last_half.1
Async XLA Ops:
  0.6 15.9 %copy-start.1 = (s32[512]{0:T(512)S(1)}, s32[512]{0:T(512)}, u32[]{:S(2)}) copy-start(s32[512]{0:T(512)} %param.5) | copy-start | bytes 6148
  4.2 12.4 %collective-permute-start.2 = (bf16[512,768]{1,0:T(8,128)(2,1)S(1)}, bf16[512,768]{1,0:T(8,128)(2,1)S(1)}, u32[]{:S(2)}, u32[]{:S(2)}) collective-permute-start(bf16[512,768]{1,0:T(8,128)(2,1)S(1)} %get-tuple-element.32.emb), channel_id=1, source_target_pairs={{0,1},{1,0},{2,3},{3,2},{4,5},{5,4},{6,7},{7,6},{8,9},{9,8},{10,11... | collective-permute-start | bytes 2359304 | tf_op jit(solution)/shard_map/ppermute | solution.py:19
  7.5 19.1 %collective-permute-start = (bf16[512,768]{1,0:T(8,128)(2,1)S(1)}, bf16[512,768]{1,0:T(8,128)(2,1)S(1)}, u32[]{:S(2)}, u32[]{:S(2)}) collective-permute-start(bf16[512,768]{1,0:T(8,128)(2,1)S(1)} %get-tuple-element.32.emb), channel_id=1, source_target_pairs={{0,2},{1,3},{2,0},{3,1},{4,6},{5,7},{6,4},{7,5},{8,10},{9,11},{10,... | collective-permute-start | bytes 2359304 | tf_op jit(solution)/shard_map/ppermute | solution.py:19
  7.5 26.7 %collective-permute-start.1 = (bf16[512,768]{1,0:T(8,128)(2,1)S(1)}, bf16[512,768]{1,0:T(8,128)(2,1)S(1)}, u32[]{:S(2)}, u32[]{:S(2)}) collective-permute-start(bf16[512,768]{1,0:T(8,128)(2,1)S(1)} %get-tuple-element.32.emb), channel_id=1, source_target_pairs={{0,254},{1,255},{2,4},{3,5},{4,2},{5,3},{6,8},{7,9},{8,6},{9,7},{1... | collective-permute-start | bytes 2359304 | tf_op jit(solution)/shard_map/ppermute | solution.py:19
  16.6 1.4 %copy-start = (bf16[512,1536]{1,0:T(8,128)(2,1)S(1)}, bf16[512,1536]{1,0:T(8,128)(2,1)}, u32[]{:S(2)}) copy-start(bf16[512,1536]{1,0:T(8,128)(2,1)} %frames.3) | copy-start | bytes 4718596
  18.4 15.7 %collective-permute-start.3 = (bf16[768,512]{1,0:T(8,128)(2,1)S(1)}, bf16[768,512]{1,0:T(8,128)(2,1)S(1)}, u32[]{:S(2)}, u32[]{:S(2)}) collective-permute-start(bf16[768,512]{1,0:T(8,128)(2,1)S(1)} %get-tuple-element.38), channel_id=1, source_target_pairs={{0,1},{1,0},{2,3},{3,2},{4,5},{5,4},{6,7},{7,6},{8,9},{9,8},{10,11... | collective-permute-start | bytes 2359304 | tf_op jit(solution)/shard_map/ppermute | solution.py:19
  36.4 1.8 %collective-permute-start.4 = (f32[4,512]{1,0:T(4,128)S(1)}, f32[4,512]{1,0:T(4,128)S(1)}, u32[]{:S(2)}, u32[]{:S(2)}) collective-permute-start(f32[4,512]{1,0:T(4,128)S(1)} %get-tuple-element.43.own), channel_id=1, source_target_pairs={{0,1},{1,0},{2,3},{3,2},{4,5},{5,4},{6,7},{7,6},{8,9},{9,8},{10,11... | collective-permute-start | bytes 24584 | tf_op jit(solution)/shard_map/ppermute | solution.py:19
  38.4 7.3 %collective-permute-start.5 = (bf16[512,768]{1,0:T(8,128)(2,1)S(1)}, bf16[512,768]{1,0:T(8,128)(2,1)S(1)}, u32[]{:S(2)}, u32[]{:S(2)}) collective-permute-start(bf16[512,768]{1,0:T(8,128)(2,1)S(1)} %pick.1), channel_id=1, source_target_pairs={{0,1},{1,0},{2,3},{3,2},{4,5},{5,4},{6,7},{7,6},{8,9},{9,8},{10,11... | collective-permute-start | bytes 2359304 | tf_op jit(solution)/shard_map/ppermute | solution.py:19
  38.8 8.5 %collective-permute-start.6 = (f32[4,512]{1,0:T(4,128)S(1)}, f32[4,512]{1,0:T(4,128)S(1)}, u32[]{:S(2)}, u32[]{:S(2)}) collective-permute-start(f32[4,512]{1,0:T(4,128)S(1)} %get-tuple-element.44.token.pair), channel_id=1, source_target_pairs={{0,2},{1,3},{2,0},{3,1},{4,6},{5,7},{6,4},{7,5},{8,10},{9,11},{10,... | collective-permute-start | bytes 24584 | tf_op jit(solution)/shard_map/ppermute | solution.py:19
  38.8 8.5 %collective-permute-start.7 = (f32[4,512]{1,0:T(4,128)S(1)}, f32[4,512]{1,0:T(4,128)S(1)}, u32[]{:S(2)}, u32[]{:S(2)}) collective-permute-start(f32[4,512]{1,0:T(4,128)S(1)} %get-tuple-element.44.token.pair), channel_id=1, source_target_pairs={{0,254},{1,255},{2,4},{3,5},{4,2},{5,3},{6,8},{7,9},{8,6},{9,7},{1... | collective-permute-start | bytes 24584 | tf_op jit(solution)/shard_map/ppermute | solution.py:19
  50.3 2.9 %collective-permute-start.8 = (bf16[512,768]{1,0:T(8,128)(2,1)S(1)}, bf16[512,768]{1,0:T(8,128)(2,1)S(1)}, u32[]{:S(2)}, u32[]{:S(2)}) collective-permute-start(bf16[512,768]{1,0:T(8,128)(2,1)S(1)} %finish.1.dz), channel_id=1, source_target_pairs={{0,1},{1,0},{2,3},{3,2},{4,5},{5,4},{6,7},{7,6},{8,9},{9,8},{10,11... | collective-permute-start | bytes 2359304 | tf_op jit(solution)/shard_map/ppermute | solution.py:19
  90.8 24.1 %copy-start.2 = (bf16[1536,768]{1,0:T(8,128)(2,1)S(1)}, bf16[1536,768]{1,0:T(8,128)(2,1)}, u32[]{:S(2)}) copy-start(bf16[1536,768]{1,0:T(8,128)(2,1)} %head.3) | copy-start | bytes 7077892
  110.4 7.0 %collective-permute-start.9 = (bf16[2,768,384]{2,1,0:T(8,128)(2,1)S(1)}, bf16[2,768,384]{2,1,0:T(8,128)(2,1)S(1)}, u32[]{:S(2)}, u32[]{:S(2)}) collective-permute-start(bf16[2,768,384]{2,1,0:T(8,128)(2,1)S(1)} %bitcast.5), channel_id=1, source_target_pairs={{0,1},{1,0},{2,3},{3,2},{4,5},{5,4},{6,7},{7,6},{8,9},{9,8},{10,11... | collective-permute-start | bytes 3538952 | tf_op jit(solution)/shard_map/ppermute | solution.py:19

commit v7 on v6

--- a/solution.py
+++ b/solution.py
@@ -192,7 +192,7 @@
 
 
 def finish(
-    goal, inverse, pair, even_note, odd_note, e_all, emb, peer, even, odd, relay, unit, rnorm, token,
+    base, goal, inverse, pair, even_note, odd_note, e_all, emb, peer, even, odd, relay, unit, rnorm, token,
     dz, g, acc,
 ):
     at = places()
@@ -200,7 +200,7 @@
     relay_note = jnp.where(crossed(), even_note, odd_note)[2:]
     notes = (pair[:2], pair[2:], even_note[:2], odd_note[:2], relay_note)
     blocks = (emb, peer, even, odd, relay)
-    size = g.shape[1]
+    half, size = g.shape[1:]
     ids = lax.broadcasted_iota(jnp.int32, (1, size), 1)
 
     def slopes(k, rows):
@@ -214,26 +214,28 @@
         weight = slope(e_all[k, rows, :], inverse[rows, :], their_inverse, left, right)
         if k == 0:
             weight = jnp.where(mine == their_goal, weight - 1.0, weight)
-        g[k % 2, rows, :] = weight.astype(BF16)
-
-    tiles = [pl.ds(r, WIDE) for r in range(0, size, WIDE)]
+        g[k % 2, here(rows), :] = weight.astype(BF16)
+
+    def here(rows):
+        return pl.ds(rows.start - base, rows.size)
+
+    tiles = [pl.ds(base + r, TILE) for r in range(0, half, TILE)]
     for rows in tiles:
         slopes(0, rows)
     for k, block in enumerate(blocks):
-        for rows in tiles:
-            product = dot(g[k % 2, rows, :], block[...])
-            if k + 1 < len(blocks):
+        product = dot(g[k % 2], block[...])
+        if k + 1 < len(blocks):
+            for rows in tiles:
                 slopes(k + 1, rows)
-            if k == 0:
-                acc[rows, :] = product
-            else:
-                acc[rows, :] += product
-    for r in range(0, emb.shape[0], TILE):
-        rows = pl.ds(r, TILE)
-        demb = SCALE * acc[rows, :]
+        if k == 0:
+            acc[...] = product
+        else:
+            acc[...] += product
+    for rows in tiles:
+        demb = SCALE * acc[here(rows), :]
         u = unit[rows, :]
         along = jnp.sum(u * demb, axis=1, keepdims=True)
-        dz[rows, :] = ((demb - u * along) * rnorm[rows, :]).astype(BF16)
+        dz[here(rows), :] = ((demb - u * along) * rnorm[rows, :]).astype(BF16)
 
 
 def turn(frames, token, mine, theirs):
@@ -253,17 +255,18 @@
         out[k] = total
 
 
-def head_own(left, dz, out):
-    out[...] = dot(left[...], dz[...])
-
-
-def head_both(part, left, dz, out):
-    cut = out.shape[2]
+def head_first(mine, theirs, dz_a, dz_b, other_a, out):
+    n = dz_a.shape[0]
+    out[...] = dot(mine[:, :n], dz_a[...]) + dot(theirs[:, :n], other_a[...]) + dot(mine[:, n:], dz_b[...])
+
+
+def head_last(part, theirs, other_b, out):
+    cut, n = out.shape[2], other_b.shape[0]
     for r in range(0, out.shape[1], WIDE):
         rows = pl.ds(r, WIDE)
-        whole = (part[rows, :] + dot(left[rows, :], dz[...])).astype(BF16)
+        whole = part[rows, :] + dot(theirs[rows, n:], other_b[...])
         for k in range(2):
-            out[k, rows, :] = whole[:, k * cut : (k + 1) * cut]
+            out[k, rows, :] = whole[:, k * cut : (k + 1) * cut].astype(BF16)
 
 
 def half_copies(part, out, sems, core):
@@ -281,14 +284,16 @@
     ]
 
 
-def ends(dz, head, own, frame_grad, out, held, sems, out_sems):
+def ends(dz_a, dz_b, head, own, frame_grad, out, held, sems, out_sems):
     copies = half_copies(own, out, sems, lax.axis_index("core"))
     for c in copies:
         c.start()
     step = head.shape[0] // out_sems.shape[0]
     for k in range(out_sems.shape[0]):
         cut = pl.ds(k * step, step)
-        held[:, cut] = dot_nt(dz[...], head[cut, :]).astype(BF16)
+        n = dz_a.shape[0]
+        held[:n, cut] = dot_nt(dz_a[...], head[cut, :]).astype(BF16)
+        held[n:, cut] = dot_nt(dz_b[...], head[cut, :]).astype(BF16)
         copies.append(pltpu.make_async_copy(held.at[:, cut], frame_grad.at[:, cut], out_sems.at[k]))
         copies[-1].start()
     for c in copies:
@@ -356,17 +361,24 @@
         seal, state, emb, relay, goal, e_all, total, pos, unit, rnorm, kept=keep(3), flops=block_flops, name="seal",
     )
     losses, token = call(lose, [row, shape((8, 128), F32)], total, pos, name="lose")
-    (dz,) = call(
-        finish, [shape((rows, width), BF16)], goal, inverse, pair, even_note, odd_note, e_all,
-        emb, peer, even, odd, relay, unit, rnorm, token,
-        scratch=[pltpu.VMEM((2, rows, rows), BF16), pltpu.VMEM((rows, width), F32)],
-        flops=5 * block_flops, name="finish",
-    )
-    dz_other = in_chip(dz)
-
-    (partial,) = call(head_own, [shape((half, width), F32)], mine, dz, flops=2 * half * rows * width, name="head_own")
+    parts = []
+    for base in (0, rows // 2):
+        (dz,) = call(
+            functools.partial(finish, base), [shape((rows // 2, width), BF16)], goal, inverse, pair, even_note, odd_note,
+            e_all, emb, peer, even, odd, relay, unit, rnorm, token,
+            scratch=[pltpu.VMEM((2, rows // 2, rows), BF16), pltpu.VMEM((rows // 2, width), F32)],
+            flops=5 * block_flops // 2, name="finish",
+        )
+        parts.append(dz)
+        token = dz
+    others = [in_chip(dz) for dz in parts]
+
+    flops = 2 * half * rows * width
     (partial,) = call(
-        head_both, [shape((2, half, width // 2), BF16)], partial, theirs, dz_other, flops=2 * half * rows * width, name="head_both"
+        head_first, [shape((half, width), F32)], mine, theirs, *parts, others[0], flops=flops, name="head_first"
+    )
+    (partial,) = call(
+        head_last, [shape((2, half, width // 2), BF16)], partial, theirs, others[1], flops=flops, name="head_last"
     )
     share = (half // 16, width // 2)
     got = lax.all_to_all(partial.reshape(32, *share), NEAR, split_axis=0, concat_axis=0)
@@ -378,7 +390,7 @@
     anywhere = pl.BlockSpec(memory_space=pl.ANY)
     frame_grad, head_grad = pl.pallas_call(
         ends,
-        in_specs=[vmem, vmem, anywhere],
+        in_specs=[vmem, vmem, vmem, anywhere],
         out_specs=[anywhere] * 2,
         out_shape=[shape((rows, depth), BF16), shape((depth, width), BF16)],
         scratch_shapes=[
@@ -387,7 +399,7 @@
         name="ends",
         compiler_params=pltpu.CompilerParams(vmem_limit_bytes=16 * 2**20),
         cost_estimate=pl.CostEstimate(flops=2 * rows * depth * width, bytes_accessed=2**22, transcendentals=0),
-    )(dz, head, own)
+    )(*parts, head, own)
     head_grad = pl.pallas_call(
         last_half,
         in_specs=[anywhere] * 2,

time: 119 us -> 119 us (level)
    ppermute x10 -> x11, waiting for transfers between devices: 17 us -> 16.5 us  [send(): return lax.ppermute(x, ALL, [(i, to(i) % 256) for i in range(256)])]
    pallas_call x12 -> x13, Pallas kernels: 10.6 us -> 10.9 us  [call(): pl.pallas_call(body, out_shape=out, in_specs=[vmem] * len(arrays), out_sp...]
    ppermute x10 -> x11, starting transfers between devices: 26.9 us -> 26.8 us  [send(): return lax.ppermute(x, ALL, [(i, to(i) % 256) for i in range(256)])]
  transfers between devices with their start and end apart: 10 -> 11, of which waited for: 4 -> 4; matrix products, arithmetic and copies ran while one was open for 0% -> 0% of each run, Pallas kernels for 6% -> 7%
where the time goes in v7:
time: 119 us; the launch traced here: 118 us
  blocking collectives  56.2 us (47%)
  starting transfers between devices  26.8 us (23%)
  Pallas kernels  17.9 us (15%)
  waiting for transfers between devices  16.5 us (14%)
    ppermute x11, starting transfers between devices, send(): return lax.ppermute(x, ALL, [(i, to(i) % 256) for i in range(256)])  26.8 us
    all_to_all x1, blocking collectives, on_device(): lax.all_to_all(partial.reshape(32, *share), NEAR, split_axis=0, concat_ax...  21.6 us
    all_to_all x1, blocking collectives, on_device(): lax.all_to_all(copies, NEAR, split_axis=0, concat_axis=0)  19.8 us
    ppermute x11, waiting for transfers between devices, send(): return lax.ppermute(x, ALL, [(i, to(i) % 256) for i in range(256)])  16.5 us
    all_to_all x1, blocking collectives, on_device(): got = lax.all_to_all(copies, 'zh', split_axis=0, concat_axis=0)  14.8 us
    pallas_call x13, Pallas kernels, call(): pl.pallas_call(body, out_shape=out, in_specs=[vmem] * len(arrays), out_sp...  10.9 us
    pallas_call x1, Pallas kernels, on_device(): pl.pallas_call(embed, in_specs=[hbm, hbm], out_specs=[vmem] * 3, out_shap...  3.52 us
    pallas_call x1, Pallas kernels, on_device(): pl.pallas_call(ends, in_specs=[vmem, vmem, vmem, anywhere], out_specs=[an...  2.47 us
  transfers between devices with their start and end apart: 11, of which 4 were waited for; matrix products, arithmetic and copies ran while one was open for 0% of the time, Pallas kernels for 7%

profile of v7, /device:TPU:1, one launch (start us, length us, event | category | flops | bytes accessed | tf_op | source)
XLA Modules:
  0.0 118.4 jit_solution(17723279839303530503)
XLA Ops:
  0.6 0.0 copy-start.1
  0.6 3.5 %embed.1 = (bf16[512,768]{1,0:T(8,128)(2,1)S(1)}, f32[512,768]{1,0:T(8,128)S(1)}, f32[512,1]{1,0:T(8,128)S(1)}) custom-call(bf16[512,1536]{1,0:T(8,128)(2,1)} %frames.3, bf16[1536,768]{1,0:T(8,128)(2,1)} %head.3), custom_call_target="tpu_custom_call" | custom-call | flops 1207959552 | bytes 4194304 | tf_op jit(solution)/shard_map/embed/pallas_call | solution.py:321
  4.2 3.3 %collective-permute-start.2 = (bf16[512,768]{1,0:T(8,128)(2,1)S(1)}, bf16[512,768]{1,0:T(8,128)(2,1)S(1)}, u32[]{:S(2)}, u32[]{:S(2)}) collective-permute-start(bf16[512,768]{1,0:T(8,128)(2,1)S(1)} %get-tuple-element.32.emb), channel_id=1, source_target_pairs={{0,1},{1,0},{2,3},{3,2},{4,5},{5,4},{6,7},{7,6},{8,9},{9,8},{10,11... | collective-permute-start | bytes 2359304 | tf_op jit(solution)/shard_map/ppermute | solution.py:19
  7.5 0.0 collective-permute-start
  7.5 9.0 %collective-permute-start.1 = (bf16[512,768]{1,0:T(8,128)(2,1)S(1)}, bf16[512,768]{1,0:T(8,128)(2,1)S(1)}, u32[]{:S(2)}, u32[]{:S(2)}) collective-permute-start(bf16[512,768]{1,0:T(8,128)(2,1)S(1)} %get-tuple-element.32.emb), channel_id=1, source_target_pairs={{0,254},{1,255},{2,4},{3,5},{4,2},{5,3},{6,8},{7,9},{8,6},{9,7},{1... | collective-permute-start | bytes 2359304 | tf_op jit(solution)/shard_map/ppermute | solution.py:19
  16.6 0.0 collective-permute-done.2.peer
  16.6 0.0 copy-done.1
  16.6 0.0 copy-start
  16.6 1.3 %near.1 = (f32[5,512,512]{2,1,0:T(8,128)S(1)}, f32[512,1]{1,0:T(8,128)S(1)}, f32[512,1]{1,0:T(8,128)S(1)}, f32[512,768]{1,0:T(8,128)S(1)}, f32[512,1]{1,0:T(8,12...) custom-call(bf16[512,768]{1,0:T(8,128)(2,1)S(1)} %get-tuple-element.32.emb, ...), custom_call_target="tpu_custom_call", output_to_operand_aliasing={{3}: (3, {}), {4}: (4, {})} | custom-call | flops 805306368 | bytes 9975808 | tf_op jit(solution)/shard_map/near/pallas_call | solution.py:53
  17.9 0.1 copy-done
  18.0 0.5 turn.1
  18.4 0.7 collective-permute-start.3
  19.2 7.4 %collective-permute-done.even = bf16[512,768]{1,0:T(8,128)(2,1)S(1)} collective-permute-done((bf16[512,768]{1,0:T(8,128)(2,1)S(1)}, bf16[512,768]{1,0:T(8,128)(2,1)S(1)}, u32[]{:S(2)}, u32[]{:S(2)}) %collective-permute-start) | collective-permute-done | bytes 786464 | tf_op jit(solution)/shard_map/ppermute | solution.py:19
  26.6 7.6 %collective-permute-done.1.odd = bf16[512,768]{1,0:T(8,128)(2,1)S(1)} collective-permute-done((bf16[512,768]{1,0:T(8,128)(2,1)S(1)}, bf16[512,768]{1,0:T(8,128)(2,1)S(1)}, u32[]{:S(2)}, u32[]{:S(2)}) %collective-permute-start.1) | collective-permute-done | bytes 786464 | tf_op jit(solution)/shard_map/ppermute | solution.py:19
  34.2 0.0 collective-permute-done.3.token.theirs
  34.2 2.2 %far.1 = (f32[5,512,512]{2,1,0:T(8,128)S(1)}, f32[512,1]{1,0:T(8,128)S(1)}, f32[512,1]{1,0:T(8,128)S(1)}, f32[512,768]{1,0:T(8,128)S(1)}, f32[512,1]{1,0:T(8,128)S(1)}, /*index=5*/f32[4,512]{1,0:T(4,128)S(1)}) custom-call(bf16[512,768]{1,0:T(8,128)(2,1)S(1)} %get-tuple-element.32.emb, ...), custom_call_target="tpu_custom_call", output_to_operand_aliasing={{0}: (7, {}), {1}: (8, {}), {2}: (9, {}), {3}: (10, {}), {4... | custom-call | flops 1207959552 | bytes 17588224 | tf_op jit(solution)/shard_map/far/pallas_call | solution.py:53
  36.4 1.0 collective-permute-start.4
  37.4 0.8 collective-permute-done.4.peer
  38.2 0.1 combine.1
  38.3 0.1 pick.1
  38.4 0.4 collective-permute-start.5
  38.8 0.0 collective-permute-start.6
  38.8 6.9 %collective-permute-start.7 = (f32[4,512]{1,0:T(4,128)S(1)}, f32[4,512]{1,0:T(4,128)S(1)}, u32[]{:S(2)}, u32[]{:S(2)}) collective-permute-start(f32[4,512]{1,0:T(4,128)S(1)} %get-tuple-element.44.token.pair), channel_id=1, source_target_pairs={{0,254},{1,255},{2,4},{3,5},{4,2},{5,3},{6,8},{7,9},{8,6},{9,7},{1... | collective-permute-start | bytes 24584 | tf_op jit(solution)/shard_map/ppermute | solution.py:19
  45.8 0.0 collective-permute-done.5.relay
  45.8 0.8 seal.1
  46.5 0.8 lose.1
  47.3 0.0 collective-permute-done.6.even_note
  47.3 0.0 collective-permute-done.7.odd_note
  47.3 1.6 %finish.2.token.dz_a = bf16[256,768]{1,0:T(8,128)(2,1)S(1)} custom-call(s32[512,1]{1,0:T(8,128)S(1)} %get-tuple-element.35.goal, f32[512,1]{1,0:T(8,128)S(1)} %get-tuple-element.53.inverse, f32[4,512]{1,0:T(4,128)S(1)} %get-tuple-element.44.token.pair, f32[4,512]{1,0:T(4,128)S(1)} %collective-permute-done.6.even_note, ...), custom_call_target="tpu_custom_call" | custom-call | flops 1006632960 | bytes 11175936 | tf_op jit(solution)/shard_map/finish/pallas_call | solution.py:53
  48.9 1.1 collective-permute-start.8
  50.0 1.6 %finish.3.dz_b = bf16[256,768]{1,0:T(8,128)(2,1)S(1)} custom-call(s32[512,1]{1,0:T(8,128)S(1)} %get-tuple-element.35.goal, f32[512,1]{1,0:T(8,128)S(1)} %get-tuple-element.53.inverse, f32[4,512]{1,0:T(4,128)S(1)} %get-tuple-element.44.token.pair, f32[4,512]{1,0:T(4,128)S(1)} %collective-permute-done.6.even_note, ...), custom_call_target="tpu_custom_call" | custom-call | flops 1006632960 | bytes 11565056 | tf_op jit(solution)/shard_map/finish/pallas_call | solution.py:53
  51.6 0.1 collective-permute-start.9
  51.7 0.0 collective-permute-done.8.other_a
  51.7 1.1 head_first.1.part
  52.8 0.6 collective-permute-done.9.other_b
  53.4 0.5 head_last.1
  53.9 21.6 %all_to_all.15.got = bf16[32,48,384]{2,1,0:T(8,128)(2,1)S(1)} all-to-all(bf16[32,48,384]{2,1,0:T(8,128)(2,1)S(1)} %bitcast.4), channel_id=1, replica_groups=mesh['zh'=4,'zl'=2,'y'=4,'x'=4,'core'=2] {'zl','y','x'}, dimensions={0} | all-to-all | bytes 2359296 | tf_op jit(solution)/shard_map/all_to_all | solution.py:384
  75.5 0.2 add_near.1
  75.7 14.8 %all_to_all.16.got = bf16[4,48,384]{2,1,0:T(8,128)(2,1)S(1)} all-to-all(bf16[4,48,384]{2,1,0:T(8,128)(2,1)S(1)} %add_near.1), channel_id=1, replica_groups=mesh['zh'=4,'zl'=2,'y'=4,'x'=4,'core'=2] {'zh'}, dimensions={0} | all-to-all | bytes 294912 | tf_op jit(solution)/shard_map/all_to_all | solution.py:386
  90.5 0.0 copy-start.2
  90.5 0.1 add_far.1
  90.6 19.8 %all_to_all.17 = bf16[32,48,384]{2,1,0:T(8,128)(2,1)S(1)} all-to-all(bf16[32,48,384]{2,1,0:T(8,128)(2,1)S(1)} %add_far.1), channel_id=1, replica_groups=mesh['zh'=4,'zl'=2,'y'=4,'x'=4,'core'=2] {'zl','y','x'}, dimensions={0} | all-to-all | bytes 2359296 | tf_op jit(solution)/shard_map/all_to_all | solution.py:388
  110.4 4.3 %collective-permute-start.10 = (bf16[2,768,384]{2,1,0:T(8,128)(2,1)S(1)}, bf16[2,768,384]{2,1,0:T(8,128)(2,1)S(1)}, u32[]{:S(2)}, u32[]{:S(2)}) collective-permute-start(bf16[2,768,384]{2,1,0:T(8,128)(2,1)S(1)} %bitcast.5), channel_id=1, source_target_pairs={{0,1},{1,0},{2,3},{3,2},{4,5},{5,4},{6,7},{7,6},{8,9},{9,8},{10,11... | collective-permute-start | bytes 3538952 | tf_op jit(solution)/shard_map/ppermute | solution.py:19
  114.7 0.0 copy-done.2
  114.7 2.5 %ends.1 = (bf16[512,1536]{1,0:T(8,128)(2,1)}, bf16[1536,768]{1,0:T(8,128)(2,1)}) custom-call(bf16[256,768]{1,0:T(8,128)(2,1)S(1)} %finish.2.token.dz_a, bf16[256,768]{1,0:T(8,128)(2,1)S(1)} %finish.3.dz_b, bf16[1536,768]{1,0:T(8,128)(2,1)S(1)} %copy-done.2, bf16[2,768,384]{2,1,0:T(8,128)(2,1)S(1)} %bitcast.6), custom_call_target="tpu_custom_call" | custom-call | flops 1207959552 | bytes 4194304 | tf_op jit(solution)/shard_map/ends/pallas_call | solution.py:391
  117.2 0.0 collective-permute-done.10.other
  117.2 1.1 last_half.1
Async XLA Ops:
  0.6 15.9 %copy-start.1 = (s32[512]{0:T(512)S(1)}, s32[512]{0:T(512)}, u32[]{:S(2)}) copy-start(s32[512]{0:T(512)} %param.5) | copy-start | bytes 6148
  4.2 12.4 %collective-permute-start.2 = (bf16[512,768]{1,0:T(8,128)(2,1)S(1)}, bf16[512,768]{1,0:T(8,128)(2,1)S(1)}, u32[]{:S(2)}, u32[]{:S(2)}) collective-permute-start(bf16[512,768]{1,0:T(8,128)(2,1)S(1)} %get-tuple-element.32.emb), channel_id=1, source_target_pairs={{0,1},{1,0},{2,3},{3,2},{4,5},{5,4},{6,7},{7,6},{8,9},{9,8},{10,11... | collective-permute-start | bytes 2359304 | tf_op jit(solution)/shard_map/ppermute | solution.py:19
  7.5 19.1 %collective-permute-start = (bf16[512,768]{1,0:T(8,128)(2,1)S(1)}, bf16[512,768]{1,0:T(8,128)(2,1)S(1)}, u32[]{:S(2)}, u32[]{:S(2)}) collective-permute-start(bf16[512,768]{1,0:T(8,128)(2,1)S(1)} %get-tuple-element.32.emb), channel_id=1, source_target_pairs={{0,2},{1,3},{2,0},{3,1},{4,6},{5,7},{6,4},{7,5},{8,10},{9,11},{10,... | collective-permute-start | bytes 2359304 | tf_op jit(solution)/shard_map/ppermute | solution.py:19
  7.5 26.7 %collective-permute-start.1 = (bf16[512,768]{1,0:T(8,128)(2,1)S(1)}, bf16[512,768]{1,0:T(8,128)(2,1)S(1)}, u32[]{:S(2)}, u32[]{:S(2)}) collective-permute-start(bf16[512,768]{1,0:T(8,128)(2,1)S(1)} %get-tuple-element.32.emb), channel_id=1, source_target_pairs={{0,254},{1,255},{2,4},{3,5},{4,2},{5,3},{6,8},{7,9},{8,6},{9,7},{1... | collective-permute-start | bytes 2359304 | tf_op jit(solution)/shard_map/ppermute | solution.py:19
  16.6 1.4 %copy-start = (bf16[512,1536]{1,0:T(8,128)(2,1)S(1)}, bf16[512,1536]{1,0:T(8,128)(2,1)}, u32[]{:S(2)}) copy-start(bf16[512,1536]{1,0:T(8,128)(2,1)} %frames.3) | copy-start | bytes 4718596
  18.4 15.7 %collective-permute-start.3 = (bf16[768,512]{1,0:T(8,128)(2,1)S(1)}, bf16[768,512]{1,0:T(8,128)(2,1)S(1)}, u32[]{:S(2)}, u32[]{:S(2)}) collective-permute-start(bf16[768,512]{1,0:T(8,128)(2,1)S(1)} %get-tuple-element.38), channel_id=1, source_target_pairs={{0,1},{1,0},{2,3},{3,2},{4,5},{5,4},{6,7},{7,6},{8,9},{9,8},{10,11... | collective-permute-start | bytes 2359304 | tf_op jit(solution)/shard_map/ppermute | solution.py:19
  36.4 1.8 %collective-permute-start.4 = (f32[4,512]{1,0:T(4,128)S(1)}, f32[4,512]{1,0:T(4,128)S(1)}, u32[]{:S(2)}, u32[]{:S(2)}) collective-permute-start(f32[4,512]{1,0:T(4,128)S(1)} %get-tuple-element.43.own), channel_id=1, source_target_pairs={{0,1},{1,0},{2,3},{3,2},{4,5},{5,4},{6,7},{7,6},{8,9},{9,8},{10,11... | collective-permute-start | bytes 24584 | tf_op jit(solution)/shard_map/ppermute | solution.py:19
  38.4 7.3 %collective-permute-start.5 = (bf16[512,768]{1,0:T(8,128)(2,1)S(1)}, bf16[512,768]{1,0:T(8,128)(2,1)S(1)}, u32[]{:S(2)}, u32[]{:S(2)}) collective-permute-start(bf16[512,768]{1,0:T(8,128)(2,1)S(1)} %pick.1), channel_id=1, source_target_pairs={{0,1},{1,0},{2,3},{3,2},{4,5},{5,4},{6,7},{7,6},{8,9},{9,8},{10,11... | collective-permute-start | bytes 2359304 | tf_op jit(solution)/shard_map/ppermute | solution.py:19
  38.8 8.5 %collective-permute-start.6 = (f32[4,512]{1,0:T(4,128)S(1)}, f32[4,512]{1,0:T(4,128)S(1)}, u32[]{:S(2)}, u32[]{:S(2)}) collective-permute-start(f32[4,512]{1,0:T(4,128)S(1)} %get-tuple-element.44.token.pair), channel_id=1, source_target_pairs={{0,2},{1,3},{2,0},{3,1},{4,6},{5,7},{6,4},{7,5},{8,10},{9,11},{10,... | collective-permute-start | bytes 24584 | tf_op jit(solution)/shard_map/ppermute | solution.py:19
  38.8 8.5 %collective-permute-start.7 = (f32[4,512]{1,0:T(4,128)S(1)}, f32[4,512]{1,0:T(4,128)S(1)}, u32[]{:S(2)}, u32[]{:S(2)}) collective-permute-start(f32[4,512]{1,0:T(4,128)S(1)} %get-tuple-element.44.token.pair), channel_id=1, source_target_pairs={{0,254},{1,255},{2,4},{3,5},{4,2},{5,3},{6,8},{7,9},{8,6},{9,7},{1... | collective-permute-start | bytes 24584 | tf_op jit(solution)/shard_map/ppermute | solution.py:19
  48.9 2.8 %collective-permute-start.8 = (bf16[256,768]{1,0:T(8,128)(2,1)S(1)}, bf16[256,768]{1,0:T(8,128)(2,1)S(1)}, u32[]{:S(2)}, u32[]{:S(2)}) collective-permute-start(bf16[256,768]{1,0:T(8,128)(2,1)S(1)} %finish.2.token.dz_a), channel_id=1, source_target_pairs={{0,1},{1,0},{2,3},{3,2},{4,5},{5,4},{6,7},{7,6},{8,9},{9,8},{10,11... | collective-permute-start | bytes 1179656 | tf_op jit(solution)/shard_map/ppermute | solution.py:19
  51.6 1.8 %collective-permute-start.9 = (bf16[256,768]{1,0:T(8,128)(2,1)S(1)}, bf16[256,768]{1,0:T(8,128)(2,1)S(1)}, u32[]{:S(2)}, u32[]{:S(2)}) collective-permute-start(bf16[256,768]{1,0:T(8,128)(2,1)S(1)} %finish.3.dz_b), channel_id=1, source_target_pairs={{0,1},{1,0},{2,3},{3,2},{4,5},{5,4},{6,7},{7,6},{8,9},{9,8},{10,11... | collective-permute-start | bytes 1179656 | tf_op jit(solution)/shard_map/ppermute | solution.py:19
  90.5 24.2 %copy-start.2 = (bf16[1536,768]{1,0:T(8,128)(2,1)S(1)}, bf16[1536,768]{1,0:T(8,128)(2,1)}, u32[]{:S(2)}) copy-start(bf16[1536,768]{1,0:T(8,128)(2,1)} %head.3) | copy-start | bytes 7077892
  110.4 6.8 %collective-permute-start.10 = (bf16[2,768,384]{2,1,0:T(8,128)(2,1)S(1)}, bf16[2,768,384]{2,1,0:T(8,128)(2,1)S(1)}, u32[]{:S(2)}, u32[]{:S(2)}) collective-permute-start(bf16[2,768,384]{2,1,0:T(8,128)(2,1)S(1)} %bitcast.5), channel_id=1, source_target_pairs={{0,1},{1,0},{2,3},{3,2},{4,5},{5,4},{6,7},{7,6},{8,9},{9,8},{10,11... | collective-permute-start | bytes 3538952 | tf_op jit(solution)/shard_map/ppermute | solution.py:19

commit v8 on v7

--- a/solution.py
+++ b/solution.py
@@ -10,7 +10,7 @@
 SCALE = 50.0
 ALL = ("zh", "zl", "y", "x", "core")
 SIZES = (4, 2, 4, 4, 2)
-NEAR = ("zl", "y", "x")
+NEAR = ("x", "y", "zl")
 F32, BF16 = jnp.float32, jnp.bfloat16
 TILE, WIDE = 128, 256
 

time: 119 us -> 119 us (level)
  no operation moved by 1% of the time
where the time goes in v8:
time: 119 us
  blocking collectives  57.2 us (48%)
  starting transfers between devices  26.1 us (22%)
  Pallas kernels  17.9 us (15%)
  waiting for transfers between devices  16.5 us (14%)
    ppermute x11, starting transfers between devices, send(): return lax.ppermute(x, ALL, [(i, to(i) % 256) for i in range(256)])  26.1 us
    all_to_all x1, blocking collectives, on_device(): lax.all_to_all(partial.reshape(32, *share), NEAR, split_axis=0, concat_ax...  22.4 us
    all_to_all x1, blocking collectives, on_device(): lax.all_to_all(copies, NEAR, split_axis=0, concat_axis=0)  20.3 us
    ppermute x11, waiting for transfers between devices, send(): return lax.ppermute(x, ALL, [(i, to(i) % 256) for i in range(256)])  16.5 us
    all_to_all x1, blocking collectives, on_device(): got = lax.all_to_all(copies, 'zh', split_axis=0, concat_axis=0)  14.5 us
    pallas_call x13, Pallas kernels, call(): pl.pallas_call(body, out_shape=out, in_specs=[vmem] * len(arrays), out_sp...  10.9 us
    pallas_call x1, Pallas kernels, on_device(): pl.pallas_call(embed, in_specs=[hbm, hbm], out_specs=[vmem] * 3, out_shap...  3.52 us
    pallas_call x1, Pallas kernels, on_device(): pl.pallas_call(ends, in_specs=[vmem, vmem, vmem, anywhere], out_specs=[an...  2.47 us
  transfers between devices with their start and end apart: 11, of which 4 were waited for; matrix products, arithmetic and copies ran while one was open for 0% of the time, Pallas kernels for 7%

profile of v8, /device:TPU:1, one launch (start us, length us, event | category | flops | bytes accessed | tf_op | source)
XLA Modules:
  0.0 118.7 jit_solution(10326429090534155520)
XLA Ops:
  0.6 0.0 copy-start.1
  0.6 3.5 %embed.1 = (bf16[512,768]{1,0:T(8,128)(2,1)S(1)}, f32[512,768]{1,0:T(8,128)S(1)}, f32[512,1]{1,0:T(8,128)S(1)}) custom-call(bf16[512,1536]{1,0:T(8,128)(2,1)} %frames.3, bf16[1536,768]{1,0:T(8,128)(2,1)} %head.3), custom_call_target="tpu_custom_call" | custom-call | flops 1207959552 | bytes 4194304 | tf_op jit(solution)/shard_map/embed/pallas_call | solution.py:321
  4.2 3.3 %collective-permute-start.2 = (bf16[512,768]{1,0:T(8,128)(2,1)S(1)}, bf16[512,768]{1,0:T(8,128)(2,1)S(1)}, u32[]{:S(2)}, u32[]{:S(2)}) collective-permute-start(bf16[512,768]{1,0:T(8,128)(2,1)S(1)} %get-tuple-element.32.emb), channel_id=1, source_target_pairs={{0,1},{1,0},{2,3},{3,2},{4,5},{5,4},{6,7},{7,6},{8,9},{9,8},{10,11... | collective-permute-start | bytes 2359304 | tf_op jit(solution)/shard_map/ppermute | solution.py:19
  7.5 0.0 collective-permute-start
  7.5 9.0 %collective-permute-start.1 = (bf16[512,768]{1,0:T(8,128)(2,1)S(1)}, bf16[512,768]{1,0:T(8,128)(2,1)S(1)}, u32[]{:S(2)}, u32[]{:S(2)}) collective-permute-start(bf16[512,768]{1,0:T(8,128)(2,1)S(1)} %get-tuple-element.32.emb), channel_id=1, source_target_pairs={{0,254},{1,255},{2,4},{3,5},{4,2},{5,3},{6,8},{7,9},{8,6},{9,7},{1... | collective-permute-start | bytes 2359304 | tf_op jit(solution)/shard_map/ppermute | solution.py:19
  16.6 0.0 collective-permute-done.2.peer
  16.6 0.0 copy-done.1
  16.6 0.0 copy-start
  16.6 1.3 %near.1 = (f32[5,512,512]{2,1,0:T(8,128)S(1)}, f32[512,1]{1,0:T(8,128)S(1)}, f32[512,1]{1,0:T(8,128)S(1)}, f32[512,768]{1,0:T(8,128)S(1)}, f32[512,1]{1,0:T(8,12...) custom-call(bf16[512,768]{1,0:T(8,128)(2,1)S(1)} %get-tuple-element.32.emb, ...), custom_call_target="tpu_custom_call", output_to_operand_aliasing={{3}: (3, {}), {4}: (4, {})} | custom-call | flops 805306368 | bytes 9975808 | tf_op jit(solution)/shard_map/near/pallas_call | solution.py:53
  17.9 0.1 copy-done
  18.0 0.5 turn.1
  18.4 0.7 collective-permute-start.3
  19.2 7.4 %collective-permute-done.even = bf16[512,768]{1,0:T(8,128)(2,1)S(1)} collective-permute-done((bf16[512,768]{1,0:T(8,128)(2,1)S(1)}, bf16[512,768]{1,0:T(8,128)(2,1)S(1)}, u32[]{:S(2)}, u32[]{:S(2)}) %collective-permute-start) | collective-permute-done | bytes 786464 | tf_op jit(solution)/shard_map/ppermute | solution.py:19
  26.6 7.6 %collective-permute-done.1.odd = bf16[512,768]{1,0:T(8,128)(2,1)S(1)} collective-permute-done((bf16[512,768]{1,0:T(8,128)(2,1)S(1)}, bf16[512,768]{1,0:T(8,128)(2,1)S(1)}, u32[]{:S(2)}, u32[]{:S(2)}) %collective-permute-start.1) | collective-permute-done | bytes 786464 | tf_op jit(solution)/shard_map/ppermute | solution.py:19
  34.2 0.0 collective-permute-done.3.token.theirs
  34.2 2.2 %far.1 = (f32[5,512,512]{2,1,0:T(8,128)S(1)}, f32[512,1]{1,0:T(8,128)S(1)}, f32[512,1]{1,0:T(8,128)S(1)}, f32[512,768]{1,0:T(8,128)S(1)}, f32[512,1]{1,0:T(8,128)S(1)}, /*index=5*/f32[4,512]{1,0:T(4,128)S(1)}) custom-call(bf16[512,768]{1,0:T(8,128)(2,1)S(1)} %get-tuple-element.32.emb, ...), custom_call_target="tpu_custom_call", output_to_operand_aliasing={{0}: (7, {}), {1}: (8, {}), {2}: (9, {}), {3}: (10, {}), {4... | custom-call | flops 1207959552 | bytes 17588224 | tf_op jit(solution)/shard_map/far/pallas_call | solution.py:53
  36.4 1.0 collective-permute-start.4
  37.4 0.8 collective-permute-done.4.peer
  38.2 0.1 combine.1
  38.3 0.1 pick.1
  38.4 0.4 collective-permute-start.5
  38.8 0.0 collective-permute-start.6
  38.8 6.9 %collective-permute-start.7 = (f32[4,512]{1,0:T(4,128)S(1)}, f32[4,512]{1,0:T(4,128)S(1)}, u32[]{:S(2)}, u32[]{:S(2)}) collective-permute-start(f32[4,512]{1,0:T(4,128)S(1)} %get-tuple-element.44.token.pair), channel_id=1, source_target_pairs={{0,254},{1,255},{2,4},{3,5},{4,2},{5,3},{6,8},{7,9},{8,6},{9,7},{1... | collective-permute-start | bytes 24584 | tf_op jit(solution)/shard_map/ppermute | solution.py:19
  45.8 0.0 collective-permute-done.5.relay
  45.8 0.8 seal.1
  46.5 0.8 lose.1
  47.3 0.0 collective-permute-done.6.even_note
  47.3 0.0 collective-permute-done.7.odd_note
  47.3 1.6 %finish.2.token.dz_a = bf16[256,768]{1,0:T(8,128)(2,1)S(1)} custom-call(s32[512,1]{1,0:T(8,128)S(1)} %get-tuple-element.35.goal, f32[512,1]{1,0:T(8,128)S(1)} %get-tuple-element.53.inverse, f32[4,512]{1,0:T(4,128)S(1)} %get-tuple-element.44.token.pair, f32[4,512]{1,0:T(4,128)S(1)} %collective-permute-done.6.even_note, ...), custom_call_target="tpu_custom_call" | custom-call | flops 1006632960 | bytes 11175936 | tf_op jit(solution)/shard_map/finish/pallas_call | solution.py:53
  48.9 1.1 collective-permute-start.8
  50.0 1.6 %finish.3.dz_b = bf16[256,768]{1,0:T(8,128)(2,1)S(1)} custom-call(s32[512,1]{1,0:T(8,128)S(1)} %get-tuple-element.35.goal, f32[512,1]{1,0:T(8,128)S(1)} %get-tuple-element.53.inverse, f32[4,512]{1,0:T(4,128)S(1)} %get-tuple-element.44.token.pair, f32[4,512]{1,0:T(4,128)S(1)} %collective-permute-done.6.even_note, ...), custom_call_target="tpu_custom_call" | custom-call | flops 1006632960 | bytes 11565056 | tf_op jit(solution)/shard_map/finish/pallas_call | solution.py:53
  51.6 0.1 collective-permute-start.9
  51.7 0.0 collective-permute-done.8.other_a
  51.7 1.1 head_first.1.part
  52.8 0.6 collective-permute-done.9.other_b
  53.4 0.5 head_last.1
  53.9 22.4 %all_to_all.15.got = bf16[32,48,384]{2,1,0:T(8,128)(2,1)S(1)} all-to-all(bf16[32,48,384]{2,1,0:T(8,128)(2,1)S(1)} %bitcast.4), channel_id=1, replica_groups=mesh['zh'=4,'zl'=2,'y'=4,'x'=4,'core'=2] {'x','y','zl'}, dimensions={0} | all-to-all | bytes 2359296 | tf_op jit(solution)/shard_map/all_to_all | solution.py:384
  76.4 0.2 add_near.1
  76.5 14.5 %all_to_all.16.got = bf16[4,48,384]{2,1,0:T(8,128)(2,1)S(1)} all-to-all(bf16[4,48,384]{2,1,0:T(8,128)(2,1)S(1)} %add_near.1), channel_id=1, replica_groups=mesh['zh'=4,'zl'=2,'y'=4,'x'=4,'core'=2] {'zh'}, dimensions={0} | all-to-all | bytes 294912 | tf_op jit(solution)/shard_map/all_to_all | solution.py:386
  91.0 0.0 copy-start.2
  91.0 0.1 add_far.1
  91.1 20.3 %all_to_all.17 = bf16[32,48,384]{2,1,0:T(8,128)(2,1)S(1)} all-to-all(bf16[32,48,384]{2,1,0:T(8,128)(2,1)S(1)} %add_far.1), channel_id=1, replica_groups=mesh['zh'=4,'zl'=2,'y'=4,'x'=4,'core'=2] {'x','y','zl'}, dimensions={0} | all-to-all | bytes 2359296 | tf_op jit(solution)/shard_map/all_to_all | solution.py:388
  111.4 3.5 %collective-permute-start.10 = (bf16[2,768,384]{2,1,0:T(8,128)(2,1)S(1)}, bf16[2,768,384]{2,1,0:T(8,128)(2,1)S(1)}, u32[]{:S(2)}, u32[]{:S(2)}) collective-permute-start(bf16[2,768,384]{2,1,0:T(8,128)(2,1)S(1)} %bitcast.5), channel_id=1, source_target_pairs={{0,1},{1,0},{2,3},{3,2},{4,5},{5,4},{6,7},{7,6},{8,9},{9,8},{10,11... | collective-permute-start | bytes 3538952 | tf_op jit(solution)/shard_map/ppermute | solution.py:19
  115.0 0.0 copy-done.2
  115.0 2.5 %ends.1 = (bf16[512,1536]{1,0:T(8,128)(2,1)}, bf16[1536,768]{1,0:T(8,128)(2,1)}) custom-call(bf16[256,768]{1,0:T(8,128)(2,1)S(1)} %finish.2.token.dz_a, bf16[256,768]{1,0:T(8,128)(2,1)S(1)} %finish.3.dz_b, bf16[1536,768]{1,0:T(8,128)(2,1)S(1)} %copy-done.2, bf16[2,768,384]{2,1,0:T(8,128)(2,1)S(1)} %bitcast.6), custom_call_target="tpu_custom_call" | custom-call | flops 1207959552 | bytes 4194304 | tf_op jit(solution)/shard_map/ends/pallas_call | solution.py:391
  117.5 0.0 collective-permute-done.10.other
  117.5 1.1 last_half.1
Async XLA Ops:
  0.6 15.9 %copy-start.1 = (s32[512]{0:T(512)S(1)}, s32[512]{0:T(512)}, u32[]{:S(2)}) copy-start(s32[512]{0:T(512)} %param.5) | copy-start | bytes 6148
  4.2 12.4 %collective-permute-start.2 = (bf16[512,768]{1,0:T(8,128)(2,1)S(1)}, bf16[512,768]{1,0:T(8,128)(2,1)S(1)}, u32[]{:S(2)}, u32[]{:S(2)}) collective-permute-start(bf16[512,768]{1,0:T(8,128)(2,1)S(1)} %get-tuple-element.32.emb), channel_id=1, source_target_pairs={{0,1},{1,0},{2,3},{3,2},{4,5},{5,4},{6,7},{7,6},{8,9},{9,8},{10,11... | collective-permute-start | bytes 2359304 | tf_op jit(solution)/shard_map/ppermute | solution.py:19
  7.5 19.1 %collective-permute-start = (bf16[512,768]{1,0:T(8,128)(2,1)S(1)}, bf16[512,768]{1,0:T(8,128)(2,1)S(1)}, u32[]{:S(2)}, u32[]{:S(2)}) collective-permute-start(bf16[512,768]{1,0:T(8,128)(2,1)S(1)} %get-tuple-element.32.emb), channel_id=1, source_target_pairs={{0,2},{1,3},{2,0},{3,1},{4,6},{5,7},{6,4},{7,5},{8,10},{9,11},{10,... | collective-permute-start | bytes 2359304 | tf_op jit(solution)/shard_map/ppermute | solution.py:19
  7.5 26.7 %collective-permute-start.1 = (bf16[512,768]{1,0:T(8,128)(2,1)S(1)}, bf16[512,768]{1,0:T(8,128)(2,1)S(1)}, u32[]{:S(2)}, u32[]{:S(2)}) collective-permute-start(bf16[512,768]{1,0:T(8,128)(2,1)S(1)} %get-tuple-element.32.emb), channel_id=1, source_target_pairs={{0,254},{1,255},{2,4},{3,5},{4,2},{5,3},{6,8},{7,9},{8,6},{9,7},{1... | collective-permute-start | bytes 2359304 | tf_op jit(solution)/shard_map/ppermute | solution.py:19
  16.6 1.4 %copy-start = (bf16[512,1536]{1,0:T(8,128)(2,1)S(1)}, bf16[512,1536]{1,0:T(8,128)(2,1)}, u32[]{:S(2)}) copy-start(bf16[512,1536]{1,0:T(8,128)(2,1)} %frames.3) | copy-start | bytes 4718596
  18.4 15.7 %collective-permute-start.3 = (bf16[768,512]{1,0:T(8,128)(2,1)S(1)}, bf16[768,512]{1,0:T(8,128)(2,1)S(1)}, u32[]{:S(2)}, u32[]{:S(2)}) collective-permute-start(bf16[768,512]{1,0:T(8,128)(2,1)S(1)} %get-tuple-element.38), channel_id=1, source_target_pairs={{0,1},{1,0},{2,3},{3,2},{4,5},{5,4},{6,7},{7,6},{8,9},{9,8},{10,11... | collective-permute-start | bytes 2359304 | tf_op jit(solution)/shard_map/ppermute | solution.py:19
  36.4 1.8 %collective-permute-start.4 = (f32[4,512]{1,0:T(4,128)S(1)}, f32[4,512]{1,0:T(4,128)S(1)}, u32[]{:S(2)}, u32[]{:S(2)}) collective-permute-start(f32[4,512]{1,0:T(4,128)S(1)} %get-tuple-element.43.own), channel_id=1, source_target_pairs={{0,1},{1,0},{2,3},{3,2},{4,5},{5,4},{6,7},{7,6},{8,9},{9,8},{10,11... | collective-permute-start | bytes 24584 | tf_op jit(solution)/shard_map/ppermute | solution.py:19
  38.4 7.3 %collective-permute-start.5 = (bf16[512,768]{1,0:T(8,128)(2,1)S(1)}, bf16[512,768]{1,0:T(8,128)(2,1)S(1)}, u32[]{:S(2)}, u32[]{:S(2)}) collective-permute-start(bf16[512,768]{1,0:T(8,128)(2,1)S(1)} %pick.1), channel_id=1, source_target_pairs={{0,1},{1,0},{2,3},{3,2},{4,5},{5,4},{6,7},{7,6},{8,9},{9,8},{10,11... | collective-permute-start | bytes 2359304 | tf_op jit(solution)/shard_map/ppermute | solution.py:19
  38.8 8.5 %collective-permute-start.6 = (f32[4,512]{1,0:T(4,128)S(1)}, f32[4,512]{1,0:T(4,128)S(1)}, u32[]{:S(2)}, u32[]{:S(2)}) collective-permute-start(f32[4,512]{1,0:T(4,128)S(1)} %get-tuple-element.44.token.pair), channel_id=1, source_target_pairs={{0,2},{1,3},{2,0},{3,1},{4,6},{5,7},{6,4},{7,5},{8,10},{9,11},{10,... | collective-permute-start | bytes 24584 | tf_op jit(solution)/shard_map/ppermute | solution.py:19
  38.8 8.5 %collective-permute-start.7 = (f32[4,512]{1,0:T(4,128)S(1)}, f32[4,512]{1,0:T(4,128)S(1)}, u32[]{:S(2)}, u32[]{:S(2)}) collective-permute-start(f32[4,512]{1,0:T(4,128)S(1)} %get-tuple-element.44.token.pair), channel_id=1, source_target_pairs={{0,254},{1,255},{2,4},{3,5},{4,2},{5,3},{6,8},{7,9},{8,6},{9,7},{1... | collective-permute-start | bytes 24584 | tf_op jit(solution)/shard_map/ppermute | solution.py:19
  48.9 2.8 %collective-permute-start.8 = (bf16[256,768]{1,0:T(8,128)(2,1)S(1)}, bf16[256,768]{1,0:T(8,128)(2,1)S(1)}, u32[]{:S(2)}, u32[]{:S(2)}) collective-permute-start(bf16[256,768]{1,0:T(8,128)(2,1)S(1)} %finish.2.token.dz_a), channel_id=1, source_target_pairs={{0,1},{1,0},{2,3},{3,2},{4,5},{5,4},{6,7},{7,6},{8,9},{9,8},{10,11... | collective-permute-start | bytes 1179656 | tf_op jit(solution)/shard_map/ppermute | solution.py:19
  51.6 1.8 %collective-permute-start.9 = (bf16[256,768]{1,0:T(8,128)(2,1)S(1)}, bf16[256,768]{1,0:T(8,128)(2,1)S(1)}, u32[]{:S(2)}, u32[]{:S(2)}) collective-permute-start(bf16[256,768]{1,0:T(8,128)(2,1)S(1)} %finish.3.dz_b), channel_id=1, source_target_pairs={{0,1},{1,0},{2,3},{3,2},{4,5},{5,4},{6,7},{7,6},{8,9},{9,8},{10,11... | collective-permute-start | bytes 1179656 | tf_op jit(solution)/shard_map/ppermute | solution.py:19
  91.0 24.0 %copy-start.2 = (bf16[1536,768]{1,0:T(8,128)(2,1)S(1)}, bf16[1536,768]{1,0:T(8,128)(2,1)}, u32[]{:S(2)}) copy-start(bf16[1536,768]{1,0:T(8,128)(2,1)} %head.3) | copy-start | bytes 7077892
  111.4 6.0 %collective-permute-start.10 = (bf16[2,768,384]{2,1,0:T(8,128)(2,1)S(1)}, bf16[2,768,384]{2,1,0:T(8,128)(2,1)S(1)}, u32[]{:S(2)}, u32[]{:S(2)}) collective-permute-start(bf16[2,768,384]{2,1,0:T(8,128)(2,1)S(1)} %bitcast.5), channel_id=1, source_target_pairs={{0,1},{1,0},{2,3},{3,2},{4,5},{5,4},{6,7},{7,6},{8,9},{9,8},{10,11... | collective-permute-start | bytes 3538952 | tf_op jit(solution)/shard_map/ppermute | solution.py:19

commit v9 on v7

--- a/solution.py
+++ b/solution.py
@@ -12,7 +12,7 @@
 SIZES = (4, 2, 4, 4, 2)
 NEAR = ("zl", "y", "x")
 F32, BF16 = jnp.float32, jnp.bfloat16
-TILE, WIDE = 128, 256
+TILE, WIDE, SCORES = 128, 256, 512
 
 
 def send(x, to):
@@ -122,8 +122,8 @@
     positives = (offsets[...] + lax.broadcasted_iota(jnp.int32, offsets.shape, 1)).astype(F32)
     goal_row[...] = positives
     goal[...] = to_column(positives).astype(jnp.int32)
-    for r in range(0, emb.shape[0], WIDE):
-        rows = pl.ds(r, WIDE)
+    for r in range(0, emb.shape[0], SCORES):
+        rows = pl.ds(r, SCORES)
         score, p0 = score_tile(0, emb, emb, goal, rows)
         e = jnp.exp(score)
         i = lax.broadcasted_iota(jnp.int32, e.shape, 0) + r
@@ -139,8 +139,8 @@
 
 def add_block(slot, emb, block, goal, e_all, total, pos):
     at = places()[slot]
-    for r in range(0, emb.shape[0], WIDE):
-        rows = pl.ds(r, WIDE)
+    for r in range(0, emb.shape[0], SCORES):
+        rows = pl.ds(r, SCORES)
         score, p = score_tile(at, emb, block, goal, rows)
         e = jnp.exp(score)
         e_all[slot, rows, :] = e
@@ -153,8 +153,8 @@
     e_all, total, pos, unit_out, rnorm_out, note, part,
 ):
     def for_peer(block):
-        for r in range(0, peer.shape[0], WIDE):
-            rows = pl.ds(r, WIDE)
+        for r in range(0, peer.shape[0], SCORES):
+            rows = pl.ds(r, SCORES)
             e = jnp.exp(SCALE * dot_nt(peer[rows, :], block[...]))
             part[rows, :] = jnp.sum(e, axis=1, keepdims=True)
 

time: 119 us -> 119 us (level)
  no operation moved by 1% of the time
where the time goes in v9:
time: 119 us
  blocking collectives  56.2 us (47%)
  starting transfers between devices  26.8 us (23%)
  Pallas kernels  18.3 us (15%)
  waiting for transfers between devices  16.5 us (14%)
    ppermute x11, starting transfers between devices, send(): return lax.ppermute(x, ALL, [(i, to(i) % 256) for i in range(256)])  26.8 us
    all_to_all x1, blocking collectives, on_device(): lax.all_to_all(partial.reshape(32, *share), NEAR, split_axis=0, concat_ax...  21.6 us
    all_to_all x1, blocking collectives, on_device(): lax.all_to_all(copies, NEAR, split_axis=0, concat_axis=0)  19.8 us
    ppermute x11, waiting for transfers between devices, send(): return lax.ppermute(x, ALL, [(i, to(i) % 256) for i in range(256)])  16.5 us
    all_to_all x1, blocking collectives, on_device(): got = lax.all_to_all(copies, 'zh', split_axis=0, concat_axis=0)  14.8 us
    pallas_call x13, Pallas kernels, call(): pl.pallas_call(body, out_shape=out, in_specs=[vmem] * len(arrays), out_sp...  11.2 us
    pallas_call x1, Pallas kernels, on_device(): pl.pallas_call(embed, in_specs=[hbm, hbm], out_specs=[vmem] * 3, out_shap...  3.52 us
    pallas_call x1, Pallas kernels, on_device(): pl.pallas_call(ends, in_specs=[vmem, vmem, vmem, anywhere], out_specs=[an...  2.47 us
  transfers between devices with their start and end apart: 11, of which 4 were waited for; matrix products, arithmetic and copies ran while one was open for 0% of the time, Pallas kernels for 7%

profile of v9, /device:TPU:1, one launch (start us, length us, event | category | flops | bytes accessed | tf_op | source)
XLA Modules:
  0.0 118.7 jit_solution(16537954086378862729)
XLA Ops:
  0.6 0.0 copy-start.1
  0.6 3.5 %embed.1 = (bf16[512,768]{1,0:T(8,128)(2,1)S(1)}, f32[512,768]{1,0:T(8,128)S(1)}, f32[512,1]{1,0:T(8,128)S(1)}) custom-call(bf16[512,1536]{1,0:T(8,128)(2,1)} %frames.3, bf16[1536,768]{1,0:T(8,128)(2,1)} %head.3), custom_call_target="tpu_custom_call" | custom-call | flops 1207959552 | bytes 4194304 | tf_op jit(solution)/shard_map/embed/pallas_call | solution.py:321
  4.2 3.3 %collective-permute-start.2 = (bf16[512,768]{1,0:T(8,128)(2,1)S(1)}, bf16[512,768]{1,0:T(8,128)(2,1)S(1)}, u32[]{:S(2)}, u32[]{:S(2)}) collective-permute-start(bf16[512,768]{1,0:T(8,128)(2,1)S(1)} %get-tuple-element.32.emb), channel_id=1, source_target_pairs={{0,1},{1,0},{2,3},{3,2},{4,5},{5,4},{6,7},{7,6},{8,9},{9,8},{10,11... | collective-permute-start | bytes 2359304 | tf_op jit(solution)/shard_map/ppermute | solution.py:19
  7.5 0.0 collective-permute-start
  7.5 9.0 %collective-permute-start.1 = (bf16[512,768]{1,0:T(8,128)(2,1)S(1)}, bf16[512,768]{1,0:T(8,128)(2,1)S(1)}, u32[]{:S(2)}, u32[]{:S(2)}) collective-permute-start(bf16[512,768]{1,0:T(8,128)(2,1)S(1)} %get-tuple-element.32.emb), channel_id=1, source_target_pairs={{0,254},{1,255},{2,4},{3,5},{4,2},{5,3},{6,8},{7,9},{8,6},{9,7},{1... | collective-permute-start | bytes 2359304 | tf_op jit(solution)/shard_map/ppermute | solution.py:19
  16.6 0.0 collective-permute-done.2.peer
  16.6 0.0 copy-done.1
  16.6 0.0 copy-start
  16.6 1.4 %near.1 = (f32[5,512,512]{2,1,0:T(8,128)S(1)}, f32[512,1]{1,0:T(8,128)S(1)}, f32[512,1]{1,0:T(8,128)S(1)}, f32[512,768]{1,0:T(8,128)S(1)}, f32[512,1]{1,0:T(8,12...) custom-call(bf16[512,768]{1,0:T(8,128)(2,1)S(1)} %get-tuple-element.32.emb, ...), custom_call_target="tpu_custom_call", output_to_operand_aliasing={{3}: (3, {}), {4}: (4, {})} | custom-call | flops 805306368 | bytes 9975808 | tf_op jit(solution)/shard_map/near/pallas_call | solution.py:53
  17.9 0.0 copy-done
  18.0 0.5 turn.1
  18.4 0.7 collective-permute-start.3
  19.2 7.4 %collective-permute-done.even = bf16[512,768]{1,0:T(8,128)(2,1)S(1)} collective-permute-done((bf16[512,768]{1,0:T(8,128)(2,1)S(1)}, bf16[512,768]{1,0:T(8,128)(2,1)S(1)}, u32[]{:S(2)}, u32[]{:S(2)}) %collective-permute-start) | collective-permute-done | bytes 786464 | tf_op jit(solution)/shard_map/ppermute | solution.py:19
  26.6 7.6 %collective-permute-done.1.odd = bf16[512,768]{1,0:T(8,128)(2,1)S(1)} collective-permute-done((bf16[512,768]{1,0:T(8,128)(2,1)S(1)}, bf16[512,768]{1,0:T(8,128)(2,1)S(1)}, u32[]{:S(2)}, u32[]{:S(2)}) %collective-permute-start.1) | collective-permute-done | bytes 786464 | tf_op jit(solution)/shard_map/ppermute | solution.py:19
  34.2 0.0 collective-permute-done.3.token.theirs
  34.2 2.5 %far.1 = (f32[5,512,512]{2,1,0:T(8,128)S(1)}, f32[512,1]{1,0:T(8,128)S(1)}, f32[512,1]{1,0:T(8,128)S(1)}, f32[512,768]{1,0:T(8,128)S(1)}, f32[512,1]{1,0:T(8,128)S(1)}, /*index=5*/f32[4,512]{1,0:T(4,128)S(1)}) custom-call(bf16[512,768]{1,0:T(8,128)(2,1)S(1)} %get-tuple-element.32.emb, ...), custom_call_target="tpu_custom_call", output_to_operand_aliasing={{0}: (7, {}), {1}: (8, {}), {2}: (9, {}), {3}: (10, {}), {4... | custom-call | flops 1207959552 | bytes 17588224 | tf_op jit(solution)/shard_map/far/pallas_call | solution.py:53
  36.7 0.9 collective-permute-start.4
  37.6 0.8 collective-permute-done.4.peer
  38.5 0.1 combine.1
  38.6 0.1 pick.1
  38.7 0.4 collective-permute-start.5
  39.1 0.0 collective-permute-start.6
  39.1 6.9 %collective-permute-start.7 = (f32[4,512]{1,0:T(4,128)S(1)}, f32[4,512]{1,0:T(4,128)S(1)}, u32[]{:S(2)}, u32[]{:S(2)}) collective-permute-start(f32[4,512]{1,0:T(4,128)S(1)} %get-tuple-element.44.token.pair), channel_id=1, source_target_pairs={{0,254},{1,255},{2,4},{3,5},{4,2},{5,3},{6,8},{7,9},{8,6},{9,7},{1... | collective-permute-start | bytes 24584 | tf_op jit(solution)/shard_map/ppermute | solution.py:19
  46.1 0.0 collective-permute-done.5.relay
  46.1 0.8 seal.1
  46.8 0.8 lose.1
  47.6 0.0 collective-permute-done.6.even_note
  47.6 0.0 collective-permute-done.7.odd_note
  47.6 1.6 %finish.2.token.dz_a = bf16[256,768]{1,0:T(8,128)(2,1)S(1)} custom-call(s32[512,1]{1,0:T(8,128)S(1)} %get-tuple-element.35.goal, f32[512,1]{1,0:T(8,128)S(1)} %get-tuple-element.53.inverse, f32[4,512]{1,0:T(4,128)S(1)} %get-tuple-element.44.token.pair, f32[4,512]{1,0:T(4,128)S(1)} %collective-permute-done.6.even_note, ...), custom_call_target="tpu_custom_call" | custom-call | flops 1006632960 | bytes 11175936 | tf_op jit(solution)/shard_map/finish/pallas_call | solution.py:53
  49.3 1.0 collective-permute-start.8
  50.3 1.6 %finish.3.dz_b = bf16[256,768]{1,0:T(8,128)(2,1)S(1)} custom-call(s32[512,1]{1,0:T(8,128)S(1)} %get-tuple-element.35.goal, f32[512,1]{1,0:T(8,128)S(1)} %get-tuple-element.53.inverse, f32[4,512]{1,0:T(4,128)S(1)} %get-tuple-element.44.token.pair, f32[4,512]{1,0:T(4,128)S(1)} %collective-permute-done.6.even_note, ...), custom_call_target="tpu_custom_call" | custom-call | flops 1006632960 | bytes 11565056 | tf_op jit(solution)/shard_map/finish/pallas_call | solution.py:53
  51.9 0.1 collective-permute-start.9
  52.0 0.0 collective-permute-done.8.other_a
  52.0 1.1 head_first.1.part
  53.1 0.6 collective-permute-done.9.other_b
  53.7 0.5 head_last.1
  54.2 21.6 %all_to_all.15.got = bf16[32,48,384]{2,1,0:T(8,128)(2,1)S(1)} all-to-all(bf16[32,48,384]{2,1,0:T(8,128)(2,1)S(1)} %bitcast.4), channel_id=1, replica_groups=mesh['zh'=4,'zl'=2,'y'=4,'x'=4,'core'=2] {'zl','y','x'}, dimensions={0} | all-to-all | bytes 2359296 | tf_op jit(solution)/shard_map/all_to_all | solution.py:384
  75.8 0.2 add_near.1
  76.0 14.8 %all_to_all.16.got = bf16[4,48,384]{2,1,0:T(8,128)(2,1)S(1)} all-to-all(bf16[4,48,384]{2,1,0:T(8,128)(2,1)S(1)} %add_near.1), channel_id=1, replica_groups=mesh['zh'=4,'zl'=2,'y'=4,'x'=4,'core'=2] {'zh'}, dimensions={0} | all-to-all | bytes 294912 | tf_op jit(solution)/shard_map/all_to_all | solution.py:386
  90.8 0.0 copy-start.2
  90.8 0.1 add_far.1
  90.9 19.8 %all_to_all.17 = bf16[32,48,384]{2,1,0:T(8,128)(2,1)S(1)} all-to-all(bf16[32,48,384]{2,1,0:T(8,128)(2,1)S(1)} %add_far.1), channel_id=1, replica_groups=mesh['zh'=4,'zl'=2,'y'=4,'x'=4,'core'=2] {'zl','y','x'}, dimensions={0} | all-to-all | bytes 2359296 | tf_op jit(solution)/shard_map/all_to_all | solution.py:388
  110.7 4.3 %collective-permute-start.10 = (bf16[2,768,384]{2,1,0:T(8,128)(2,1)S(1)}, bf16[2,768,384]{2,1,0:T(8,128)(2,1)S(1)}, u32[]{:S(2)}, u32[]{:S(2)}) collective-permute-start(bf16[2,768,384]{2,1,0:T(8,128)(2,1)S(1)} %bitcast.5), channel_id=1, source_target_pairs={{0,1},{1,0},{2,3},{3,2},{4,5},{5,4},{6,7},{7,6},{8,9},{9,8},{10,11... | collective-permute-start | bytes 3538952 | tf_op jit(solution)/shard_map/ppermute | solution.py:19
  115.0 0.0 copy-done.2
  115.0 2.5 %ends.1 = (bf16[512,1536]{1,0:T(8,128)(2,1)}, bf16[1536,768]{1,0:T(8,128)(2,1)}) custom-call(bf16[256,768]{1,0:T(8,128)(2,1)S(1)} %finish.2.token.dz_a, bf16[256,768]{1,0:T(8,128)(2,1)S(1)} %finish.3.dz_b, bf16[1536,768]{1,0:T(8,128)(2,1)S(1)} %copy-done.2, bf16[2,768,384]{2,1,0:T(8,128)(2,1)S(1)} %bitcast.6), custom_call_target="tpu_custom_call" | custom-call | flops 1207959552 | bytes 4194304 | tf_op jit(solution)/shard_map/ends/pallas_call | solution.py:391
  117.5 0.0 collective-permute-done.10.other
  117.5 1.1 last_half.1
Async XLA Ops:
  0.6 15.9 %copy-start.1 = (s32[512]{0:T(512)S(1)}, s32[512]{0:T(512)}, u32[]{:S(2)}) copy-start(s32[512]{0:T(512)} %param.5) | copy-start | bytes 6148
  4.2 12.4 %collective-permute-start.2 = (bf16[512,768]{1,0:T(8,128)(2,1)S(1)}, bf16[512,768]{1,0:T(8,128)(2,1)S(1)}, u32[]{:S(2)}, u32[]{:S(2)}) collective-permute-start(bf16[512,768]{1,0:T(8,128)(2,1)S(1)} %get-tuple-element.32.emb), channel_id=1, source_target_pairs={{0,1},{1,0},{2,3},{3,2},{4,5},{5,4},{6,7},{7,6},{8,9},{9,8},{10,11... | collective-permute-start | bytes 2359304 | tf_op jit(solution)/shard_map/ppermute | solution.py:19
  7.5 19.1 %collective-permute-start = (bf16[512,768]{1,0:T(8,128)(2,1)S(1)}, bf16[512,768]{1,0:T(8,128)(2,1)S(1)}, u32[]{:S(2)}, u32[]{:S(2)}) collective-permute-start(bf16[512,768]{1,0:T(8,128)(2,1)S(1)} %get-tuple-element.32.emb), channel_id=1, source_target_pairs={{0,2},{1,3},{2,0},{3,1},{4,6},{5,7},{6,4},{7,5},{8,10},{9,11},{10,... | collective-permute-start | bytes 2359304 | tf_op jit(solution)/shard_map/ppermute | solution.py:19
  7.5 26.7 %collective-permute-start.1 = (bf16[512,768]{1,0:T(8,128)(2,1)S(1)}, bf16[512,768]{1,0:T(8,128)(2,1)S(1)}, u32[]{:S(2)}, u32[]{:S(2)}) collective-permute-start(bf16[512,768]{1,0:T(8,128)(2,1)S(1)} %get-tuple-element.32.emb), channel_id=1, source_target_pairs={{0,254},{1,255},{2,4},{3,5},{4,2},{5,3},{6,8},{7,9},{8,6},{9,7},{1... | collective-permute-start | bytes 2359304 | tf_op jit(solution)/shard_map/ppermute | solution.py:19
  16.6 1.4 %copy-start = (bf16[512,1536]{1,0:T(8,128)(2,1)S(1)}, bf16[512,1536]{1,0:T(8,128)(2,1)}, u32[]{:S(2)}) copy-start(bf16[512,1536]{1,0:T(8,128)(2,1)} %frames.3) | copy-start | bytes 4718596
  18.4 15.7 %collective-permute-start.3 = (bf16[768,512]{1,0:T(8,128)(2,1)S(1)}, bf16[768,512]{1,0:T(8,128)(2,1)S(1)}, u32[]{:S(2)}, u32[]{:S(2)}) collective-permute-start(bf16[768,512]{1,0:T(8,128)(2,1)S(1)} %get-tuple-element.38), channel_id=1, source_target_pairs={{0,1},{1,0},{2,3},{3,2},{4,5},{5,4},{6,7},{7,6},{8,9},{9,8},{10,11... | collective-permute-start | bytes 2359304 | tf_op jit(solution)/shard_map/ppermute | solution.py:19
  36.7 1.8 %collective-permute-start.4 = (f32[4,512]{1,0:T(4,128)S(1)}, f32[4,512]{1,0:T(4,128)S(1)}, u32[]{:S(2)}, u32[]{:S(2)}) collective-permute-start(f32[4,512]{1,0:T(4,128)S(1)} %get-tuple-element.43.own), channel_id=1, source_target_pairs={{0,1},{1,0},{2,3},{3,2},{4,5},{5,4},{6,7},{7,6},{8,9},{9,8},{10,11... | collective-permute-start | bytes 24584 | tf_op jit(solution)/shard_map/ppermute | solution.py:19
  38.7 7.3 %collective-permute-start.5 = (bf16[512,768]{1,0:T(8,128)(2,1)S(1)}, bf16[512,768]{1,0:T(8,128)(2,1)S(1)}, u32[]{:S(2)}, u32[]{:S(2)}) collective-permute-start(bf16[512,768]{1,0:T(8,128)(2,1)S(1)} %pick.1), channel_id=1, source_target_pairs={{0,1},{1,0},{2,3},{3,2},{4,5},{5,4},{6,7},{7,6},{8,9},{9,8},{10,11... | collective-permute-start | bytes 2359304 | tf_op jit(solution)/shard_map/ppermute | solution.py:19
  39.1 8.5 %collective-permute-start.6 = (f32[4,512]{1,0:T(4,128)S(1)}, f32[4,512]{1,0:T(4,128)S(1)}, u32[]{:S(2)}, u32[]{:S(2)}) collective-permute-start(f32[4,512]{1,0:T(4,128)S(1)} %get-tuple-element.44.token.pair), channel_id=1, source_target_pairs={{0,2},{1,3},{2,0},{3,1},{4,6},{5,7},{6,4},{7,5},{8,10},{9,11},{10,... | collective-permute-start | bytes 24584 | tf_op jit(solution)/shard_map/ppermute | solution.py:19
  39.1 8.5 %collective-permute-start.7 = (f32[4,512]{1,0:T(4,128)S(1)}, f32[4,512]{1,0:T(4,128)S(1)}, u32[]{:S(2)}, u32[]{:S(2)}) collective-permute-start(f32[4,512]{1,0:T(4,128)S(1)} %get-tuple-element.44.token.pair), channel_id=1, source_target_pairs={{0,254},{1,255},{2,4},{3,5},{4,2},{5,3},{6,8},{7,9},{8,6},{9,7},{1... | collective-permute-start | bytes 24584 | tf_op jit(solution)/shard_map/ppermute | solution.py:19
  49.3 2.8 %collective-permute-start.8 = (bf16[256,768]{1,0:T(8,128)(2,1)S(1)}, bf16[256,768]{1,0:T(8,128)(2,1)S(1)}, u32[]{:S(2)}, u32[]{:S(2)}) collective-permute-start(bf16[256,768]{1,0:T(8,128)(2,1)S(1)} %finish.2.token.dz_a), channel_id=1, source_target_pairs={{0,1},{1,0},{2,3},{3,2},{4,5},{5,4},{6,7},{7,6},{8,9},{9,8},{10,11... | collective-permute-start | bytes 1179656 | tf_op jit(solution)/shard_map/ppermute | solution.py:19
  51.9 1.8 %collective-permute-start.9 = (bf16[256,768]{1,0:T(8,128)(2,1)S(1)}, bf16[256,768]{1,0:T(8,128)(2,1)S(1)}, u32[]{:S(2)}, u32[]{:S(2)}) collective-permute-start(bf16[256,768]{1,0:T(8,128)(2,1)S(1)} %finish.3.dz_b), channel_id=1, source_target_pairs={{0,1},{1,0},{2,3},{3,2},{4,5},{5,4},{6,7},{7,6},{8,9},{9,8},{10,11... | collective-permute-start | bytes 1179656 | tf_op jit(solution)/shard_map/ppermute | solution.py:19
  90.8 24.2 %copy-start.2 = (bf16[1536,768]{1,0:T(8,128)(2,1)S(1)}, bf16[1536,768]{1,0:T(8,128)(2,1)}, u32[]{:S(2)}) copy-start(bf16[1536,768]{1,0:T(8,128)(2,1)} %head.3) | copy-start | bytes 7077892
  110.7 6.8 %collective-permute-start.10 = (bf16[2,768,384]{2,1,0:T(8,128)(2,1)S(1)}, bf16[2,768,384]{2,1,0:T(8,128)(2,1)S(1)}, u32[]{:S(2)}, u32[]{:S(2)}) collective-permute-start(bf16[2,768,384]{2,1,0:T(8,128)(2,1)S(1)} %bitcast.5), channel_id=1, source_target_pairs={{0,1},{1,0},{2,3},{3,2},{4,5},{5,4},{6,7},{7,6},{8,9},{9,8},{10,11... | collective-permute-start | bytes 3538952 | tf_op jit(solution)/shard_map/ppermute | solution.py:19

commit v10 on v7

--- a/solution.py
+++ b/solution.py
@@ -355,7 +355,7 @@
     pair, inverse = call(combine, [note, col], own_note, peer_note, name="combine")
     odd_note = swap_odd(pair)
     even_note = swap_even(pair)
-    (shared,) = call(pick, [shape((rows, width), BF16)], even, odd, pair, name="pick")
+    (shared,) = call(pick, [shape((rows, width), BF16)], even, odd, theirs, name="pick")
     relay = in_chip(shared)
     e_all, total, pos, unit, rnorm = call(
         seal, state, emb, relay, goal, e_all, total, pos, unit, rnorm, kept=keep(3), flops=block_flops, name="seal",

time: 119 us -> 119 us (level)
  transfers between devices with their start and end apart: 11 -> 11, of which waited for: 4 -> 4; matrix products, arithmetic and copies ran while one was open for 0% -> 0% of each run, Pallas kernels for 7% -> 9%
where the time goes in v10:
time: 119 us
  blocking collectives  56.2 us (47%)
  starting transfers between devices  26.6 us (22%)
  Pallas kernels  17.9 us (15%)
  waiting for transfers between devices  16.8 us (14%)
    ppermute x11, starting transfers between devices, send(): return lax.ppermute(x, ALL, [(i, to(i) % 256) for i in range(256)])  26.6 us
    all_to_all x1, blocking collectives, on_device(): lax.all_to_all(partial.reshape(32, *share), NEAR, split_axis=0, concat_ax...  21.6 us
    all_to_all x1, blocking collectives, on_device(): lax.all_to_all(copies, NEAR, split_axis=0, concat_axis=0)  19.8 us
    ppermute x11, waiting for transfers between devices, send(): return lax.ppermute(x, ALL, [(i, to(i) % 256) for i in range(256)])  16.8 us
    all_to_all x1, blocking collectives, on_device(): got = lax.all_to_all(copies, 'zh', split_axis=0, concat_axis=0)  14.8 us
    pallas_call x13, Pallas kernels, call(): pl.pallas_call(body, out_shape=out, in_specs=[vmem] * len(arrays), out_sp...  10.9 us
    pallas_call x1, Pallas kernels, on_device(): pl.pallas_call(embed, in_specs=[hbm, hbm], out_specs=[vmem] * 3, out_shap...  3.52 us
    pallas_call x1, Pallas kernels, on_device(): pl.pallas_call(ends, in_specs=[vmem, vmem, vmem, anywhere], out_specs=[an...  2.46 us
  transfers between devices with their start and end apart: 11, of which 4 were waited for; matrix products, arithmetic and copies ran while one was open for 0% of the time, Pallas kernels for 9%

profile of v10, /device:TPU:1, one launch (start us, length us, event | category | flops | bytes accessed | tf_op | source)
XLA Modules:
  0.0 118.5 jit_solution(9122555918273687160)
XLA Ops:
  0.6 0.0 copy-start.1
  0.6 3.5 %embed.1 = (bf16[512,768]{1,0:T(8,128)(2,1)S(1)}, f32[512,768]{1,0:T(8,128)S(1)}, f32[512,1]{1,0:T(8,128)S(1)}) custom-call(bf16[512,1536]{1,0:T(8,128)(2,1)} %frames.3, bf16[1536,768]{1,0:T(8,128)(2,1)} %head.3), custom_call_target="tpu_custom_call" | custom-call | flops 1207959552 | bytes 4194304 | tf_op jit(solution)/shard_map/embed/pallas_call | solution.py:321
  4.2 3.3 %collective-permute-start.2 = (bf16[512,768]{1,0:T(8,128)(2,1)S(1)}, bf16[512,768]{1,0:T(8,128)(2,1)S(1)}, u32[]{:S(2)}, u32[]{:S(2)}) collective-permute-start(bf16[512,768]{1,0:T(8,128)(2,1)S(1)} %get-tuple-element.32.emb), channel_id=1, source_target_pairs={{0,1},{1,0},{2,3},{3,2},{4,5},{5,4},{6,7},{7,6},{8,9},{9,8},{10,11... | collective-permute-start | bytes 2359304 | tf_op jit(solution)/shard_map/ppermute | solution.py:19
  7.5 0.0 collective-permute-start
  7.5 9.0 %collective-permute-start.1 = (bf16[512,768]{1,0:T(8,128)(2,1)S(1)}, bf16[512,768]{1,0:T(8,128)(2,1)S(1)}, u32[]{:S(2)}, u32[]{:S(2)}) collective-permute-start(bf16[512,768]{1,0:T(8,128)(2,1)S(1)} %get-tuple-element.32.emb), channel_id=1, source_target_pairs={{0,254},{1,255},{2,4},{3,5},{4,2},{5,3},{6,8},{7,9},{8,6},{9,7},{1... | collective-permute-start | bytes 2359304 | tf_op jit(solution)/shard_map/ppermute | solution.py:19
  16.6 0.0 collective-permute-done.2.peer
  16.6 0.0 copy-done.1
  16.6 0.0 copy-start
  16.6 1.3 %near.1 = (f32[5,512,512]{2,1,0:T(8,128)S(1)}, f32[512,1]{1,0:T(8,128)S(1)}, f32[512,1]{1,0:T(8,128)S(1)}, f32[512,768]{1,0:T(8,128)S(1)}, f32[512,1]{1,0:T(8,12...) custom-call(bf16[512,768]{1,0:T(8,128)(2,1)S(1)} %get-tuple-element.32.emb, ...), custom_call_target="tpu_custom_call", output_to_operand_aliasing={{3}: (3, {}), {4}: (4, {})} | custom-call | flops 805306368 | bytes 9975808 | tf_op jit(solution)/shard_map/near/pallas_call | solution.py:53
  17.9 0.1 copy-done
  18.0 0.5 turn.1
  18.4 0.7 collective-permute-start.3
  19.2 7.4 %collective-permute-done.even = bf16[512,768]{1,0:T(8,128)(2,1)S(1)} collective-permute-done((bf16[512,768]{1,0:T(8,128)(2,1)S(1)}, bf16[512,768]{1,0:T(8,128)(2,1)S(1)}, u32[]{:S(2)}, u32[]{:S(2)}) %collective-permute-start) | collective-permute-done | bytes 786464 | tf_op jit(solution)/shard_map/ppermute | solution.py:19
  26.6 7.6 %collective-permute-done.1.odd = bf16[512,768]{1,0:T(8,128)(2,1)S(1)} collective-permute-done((bf16[512,768]{1,0:T(8,128)(2,1)S(1)}, bf16[512,768]{1,0:T(8,128)(2,1)S(1)}, u32[]{:S(2)}, u32[]{:S(2)}) %collective-permute-start.1) | collective-permute-done | bytes 786464 | tf_op jit(solution)/shard_map/ppermute | solution.py:19
  34.2 0.0 collective-permute-done.3.token.theirs
  34.2 0.1 pick.1
  34.3 0.9 collective-permute-start.4
  35.2 2.2 %far.1 = (f32[5,512,512]{2,1,0:T(8,128)S(1)}, f32[512,1]{1,0:T(8,128)S(1)}, f32[512,1]{1,0:T(8,128)S(1)}, f32[512,768]{1,0:T(8,128)S(1)}, f32[512,1]{1,0:T(8,128)S(1)}, /*index=5*/f32[4,512]{1,0:T(4,128)S(1)}) custom-call(bf16[512,768]{1,0:T(8,128)(2,1)S(1)} %get-tuple-element.32.emb, ...), custom_call_target="tpu_custom_call", output_to_operand_aliasing={{0}: (7, {}), {1}: (8, {}), {2}: (9, {}), {3}: (10, {}), {4... | custom-call | flops 1207959552 | bytes 17588224 | tf_op jit(solution)/shard_map/far/pallas_call | solution.py:53
  37.4 0.1 collective-permute-start.5
  37.5 1.1 collective-permute-done.5.peer
  38.6 0.1 combine.1
  38.8 0.1 collective-permute-start.6
  38.9 7.0 %collective-permute-start.7 = (f32[4,512]{1,0:T(4,128)S(1)}, f32[4,512]{1,0:T(4,128)S(1)}, u32[]{:S(2)}, u32[]{:S(2)}) collective-permute-start(f32[4,512]{1,0:T(4,128)S(1)} %get-tuple-element.53.pair), channel_id=1, source_target_pairs={{0,254},{1,255},{2,4},{3,5},{4,2},{5,3},{6,8},{7,9},{8,6},{9,7},{1... | collective-permute-start | bytes 24584 | tf_op jit(solution)/shard_map/ppermute | solution.py:19
  45.9 0.0 collective-permute-done.4.relay
  45.9 0.8 seal.1
  46.7 0.8 lose.1
  47.5 0.0 collective-permute-done.6.even_note
  47.5 0.0 collective-permute-done.7.odd_note
  47.5 1.6 %finish.2.token.dz_a = bf16[256,768]{1,0:T(8,128)(2,1)S(1)} custom-call(s32[512,1]{1,0:T(8,128)S(1)} %get-tuple-element.37.goal, f32[512,1]{1,0:T(8,128)S(1)} %get-tuple-element.52.inverse, f32[4,512]{1,0:T(4,128)S(1)} %get-tuple-element.53.pair, f32[4,512]{1,0:T(4,128)S(1)} %collective-permute-done.6.even_note, ...), custom_call_target="tpu_custom_call" | custom-call | flops 1006632960 | bytes 11175936 | tf_op jit(solution)/shard_map/finish/pallas_call | solution.py:53
  49.1 1.0 collective-permute-start.8
  50.1 1.6 %finish.3.dz_b = bf16[256,768]{1,0:T(8,128)(2,1)S(1)} custom-call(s32[512,1]{1,0:T(8,128)S(1)} %get-tuple-element.37.goal, f32[512,1]{1,0:T(8,128)S(1)} %get-tuple-element.52.inverse, f32[4,512]{1,0:T(4,128)S(1)} %get-tuple-element.53.pair, f32[4,512]{1,0:T(4,128)S(1)} %collective-permute-done.6.even_note, f32[4,512]{1,0:T(4,128)S(1)} %collective-permute-done.7.odd_note, ...), custom_call_target="tpu_custom_call" | custom-call | flops 1006632960 | bytes 11565056 | tf_op jit(solution)/shard_map/finish/pallas_call | solution.py:53
  51.8 0.1 collective-permute-start.9
  51.9 0.0 collective-permute-done.8.other_a
  51.9 1.1 head_first.1.part
  53.0 0.6 collective-permute-done.9.other_b
  53.6 0.5 head_last.1
  54.1 21.6 %all_to_all.15.got = bf16[32,48,384]{2,1,0:T(8,128)(2,1)S(1)} all-to-all(bf16[32,48,384]{2,1,0:T(8,128)(2,1)S(1)} %bitcast.4), channel_id=1, replica_groups=mesh['zh'=4,'zl'=2,'y'=4,'x'=4,'core'=2] {'zl','y','x'}, dimensions={0} | all-to-all | bytes 2359296 | tf_op jit(solution)/shard_map/all_to_all | solution.py:384
  75.7 0.2 add_near.1
  75.8 14.8 %all_to_all.16.got = bf16[4,48,384]{2,1,0:T(8,128)(2,1)S(1)} all-to-all(bf16[4,48,384]{2,1,0:T(8,128)(2,1)S(1)} %add_near.1), channel_id=1, replica_groups=mesh['zh'=4,'zl'=2,'y'=4,'x'=4,'core'=2] {'zh'}, dimensions={0} | all-to-all | bytes 294912 | tf_op jit(solution)/shard_map/all_to_all | solution.py:386
  90.6 0.0 copy-start.2
  90.6 0.1 add_far.1
  90.7 19.8 %all_to_all.17 = bf16[32,48,384]{2,1,0:T(8,128)(2,1)S(1)} all-to-all(bf16[32,48,384]{2,1,0:T(8,128)(2,1)S(1)} %add_far.1), channel_id=1, replica_groups=mesh['zh'=4,'zl'=2,'y'=4,'x'=4,'core'=2] {'zl','y','x'}, dimensions={0} | all-to-all | bytes 2359296 | tf_op jit(solution)/shard_map/all_to_all | solution.py:388
  110.6 4.3 %collective-permute-start.10 = (bf16[2,768,384]{2,1,0:T(8,128)(2,1)S(1)}, bf16[2,768,384]{2,1,0:T(8,128)(2,1)S(1)}, u32[]{:S(2)}, u32[]{:S(2)}) collective-permute-start(bf16[2,768,384]{2,1,0:T(8,128)(2,1)S(1)} %bitcast.5), channel_id=1, source_target_pairs={{0,1},{1,0},{2,3},{3,2},{4,5},{5,4},{6,7},{7,6},{8,9},{9,8},{10,11... | collective-permute-start | bytes 3538952 | tf_op jit(solution)/shard_map/ppermute | solution.py:19
  114.8 0.0 copy-done.2
  114.8 2.5 %ends.1 = (bf16[512,1536]{1,0:T(8,128)(2,1)}, bf16[1536,768]{1,0:T(8,128)(2,1)}) custom-call(bf16[256,768]{1,0:T(8,128)(2,1)S(1)} %finish.2.token.dz_a, bf16[256,768]{1,0:T(8,128)(2,1)S(1)} %finish.3.dz_b, bf16[1536,768]{1,0:T(8,128)(2,1)S(1)} %copy-done.2, bf16[2,768,384]{2,1,0:T(8,128)(2,1)S(1)} %bitcast.6), custom_call_target="tpu_custom_call" | custom-call | flops 1207959552 | bytes 4194304 | tf_op jit(solution)/shard_map/ends/pallas_call | solution.py:391
  117.3 0.0 collective-permute-done.10.other
  117.3 1.1 last_half.1
Async XLA Ops:
  0.6 15.9 %copy-start.1 = (s32[512]{0:T(512)S(1)}, s32[512]{0:T(512)}, u32[]{:S(2)}) copy-start(s32[512]{0:T(512)} %param.5) | copy-start | bytes 6148
  4.2 12.4 %collective-permute-start.2 = (bf16[512,768]{1,0:T(8,128)(2,1)S(1)}, bf16[512,768]{1,0:T(8,128)(2,1)S(1)}, u32[]{:S(2)}, u32[]{:S(2)}) collective-permute-start(bf16[512,768]{1,0:T(8,128)(2,1)S(1)} %get-tuple-element.32.emb), channel_id=1, source_target_pairs={{0,1},{1,0},{2,3},{3,2},{4,5},{5,4},{6,7},{7,6},{8,9},{9,8},{10,11... | collective-permute-start | bytes 2359304 | tf_op jit(solution)/shard_map/ppermute | solution.py:19
  7.5 19.1 %collective-permute-start = (bf16[512,768]{1,0:T(8,128)(2,1)S(1)}, bf16[512,768]{1,0:T(8,128)(2,1)S(1)}, u32[]{:S(2)}, u32[]{:S(2)}) collective-permute-start(bf16[512,768]{1,0:T(8,128)(2,1)S(1)} %get-tuple-element.32.emb), channel_id=1, source_target_pairs={{0,2},{1,3},{2,0},{3,1},{4,6},{5,7},{6,4},{7,5},{8,10},{9,11},{10,... | collective-permute-start | bytes 2359304 | tf_op jit(solution)/shard_map/ppermute | solution.py:19
  7.5 26.7 %collective-permute-start.1 = (bf16[512,768]{1,0:T(8,128)(2,1)S(1)}, bf16[512,768]{1,0:T(8,128)(2,1)S(1)}, u32[]{:S(2)}, u32[]{:S(2)}) collective-permute-start(bf16[512,768]{1,0:T(8,128)(2,1)S(1)} %get-tuple-element.32.emb), channel_id=1, source_target_pairs={{0,254},{1,255},{2,4},{3,5},{4,2},{5,3},{6,8},{7,9},{8,6},{9,7},{1... | collective-permute-start | bytes 2359304 | tf_op jit(solution)/shard_map/ppermute | solution.py:19
  16.6 1.4 %copy-start = (bf16[512,1536]{1,0:T(8,128)(2,1)S(1)}, bf16[512,1536]{1,0:T(8,128)(2,1)}, u32[]{:S(2)}) copy-start(bf16[512,1536]{1,0:T(8,128)(2,1)} %frames.3) | copy-start | bytes 4718596
  18.4 15.7 %collective-permute-start.3 = (bf16[768,512]{1,0:T(8,128)(2,1)S(1)}, bf16[768,512]{1,0:T(8,128)(2,1)S(1)}, u32[]{:S(2)}, u32[]{:S(2)}) collective-permute-start(bf16[768,512]{1,0:T(8,128)(2,1)S(1)} %get-tuple-element.36), channel_id=1, source_target_pairs={{0,1},{1,0},{2,3},{3,2},{4,5},{5,4},{6,7},{7,6},{8,9},{9,8},{10,11... | collective-permute-start | bytes 2359304 | tf_op jit(solution)/shard_map/ppermute | solution.py:19
  34.3 11.6 %collective-permute-start.4 = (bf16[512,768]{1,0:T(8,128)(2,1)S(1)}, bf16[512,768]{1,0:T(8,128)(2,1)S(1)}, u32[]{:S(2)}, u32[]{:S(2)}) collective-permute-start(bf16[512,768]{1,0:T(8,128)(2,1)S(1)} %pick.1), channel_id=1, source_target_pairs={{0,1},{1,0},{2,3},{3,2},{4,5},{5,4},{6,7},{7,6},{8,9},{9,8},{10,11... | collective-permute-start | bytes 2359304 | tf_op jit(solution)/shard_map/ppermute | solution.py:19
  37.4 1.2 %collective-permute-start.5 = (f32[4,512]{1,0:T(4,128)S(1)}, f32[4,512]{1,0:T(4,128)S(1)}, u32[]{:S(2)}, u32[]{:S(2)}) collective-permute-start(f32[4,512]{1,0:T(4,128)S(1)} %get-tuple-element.51.own), channel_id=1, source_target_pairs={{0,1},{1,0},{2,3},{3,2},{4,5},{5,4},{6,7},{7,6},{8,9},{9,8},{10,11... | collective-permute-start | bytes 24584 | tf_op jit(solution)/shard_map/ppermute | solution.py:19
  38.8 8.7 %collective-permute-start.6 = (f32[4,512]{1,0:T(4,128)S(1)}, f32[4,512]{1,0:T(4,128)S(1)}, u32[]{:S(2)}, u32[]{:S(2)}) collective-permute-start(f32[4,512]{1,0:T(4,128)S(1)} %get-tuple-element.53.pair), channel_id=1, source_target_pairs={{0,2},{1,3},{2,0},{3,1},{4,6},{5,7},{6,4},{7,5},{8,10},{9,11},{10,... | collective-permute-start | bytes 24584 | tf_op jit(solution)/shard_map/ppermute | solution.py:19
  38.9 8.6 %collective-permute-start.7 = (f32[4,512]{1,0:T(4,128)S(1)}, f32[4,512]{1,0:T(4,128)S(1)}, u32[]{:S(2)}, u32[]{:S(2)}) collective-permute-start(f32[4,512]{1,0:T(4,128)S(1)} %get-tuple-element.53.pair), channel_id=1, source_target_pairs={{0,254},{1,255},{2,4},{3,5},{4,2},{5,3},{6,8},{7,9},{8,6},{9,7},{1... | collective-permute-start | bytes 24584 | tf_op jit(solution)/shard_map/ppermute | solution.py:19
  49.1 2.7 %collective-permute-start.8 = (bf16[256,768]{1,0:T(8,128)(2,1)S(1)}, bf16[256,768]{1,0:T(8,128)(2,1)S(1)}, u32[]{:S(2)}, u32[]{:S(2)}) collective-permute-start(bf16[256,768]{1,0:T(8,128)(2,1)S(1)} %finish.2.token.dz_a), channel_id=1, source_target_pairs={{0,1},{1,0},{2,3},{3,2},{4,5},{5,4},{6,7},{7,6},{8,9},{9,8},{10,11... | collective-permute-start | bytes 1179656 | tf_op jit(solution)/shard_map/ppermute | solution.py:19
  51.8 1.8 %collective-permute-start.9 = (bf16[256,768]{1,0:T(8,128)(2,1)S(1)}, bf16[256,768]{1,0:T(8,128)(2,1)S(1)}, u32[]{:S(2)}, u32[]{:S(2)}) collective-permute-start(bf16[256,768]{1,0:T(8,128)(2,1)S(1)} %finish.3.dz_b), channel_id=1, source_target_pairs={{0,1},{1,0},{2,3},{3,2},{4,5},{5,4},{6,7},{7,6},{8,9},{9,8},{10,11... | collective-permute-start | bytes 1179656 | tf_op jit(solution)/shard_map/ppermute | solution.py:19
  90.6 24.2 %copy-start.2 = (bf16[1536,768]{1,0:T(8,128)(2,1)S(1)}, bf16[1536,768]{1,0:T(8,128)(2,1)}, u32[]{:S(2)}) copy-start(bf16[1536,768]{1,0:T(8,128)(2,1)} %head.3) | copy-start | bytes 7077892
  110.6 6.8 %collective-permute-start.10 = (bf16[2,768,384]{2,1,0:T(8,128)(2,1)S(1)}, bf16[2,768,384]{2,1,0:T(8,128)(2,1)S(1)}, u32[]{:S(2)}, u32[]{:S(2)}) collective-permute-start(bf16[2,768,384]{2,1,0:T(8,128)(2,1)S(1)} %bitcast.5), channel_id=1, source_target_pairs={{0,1},{1,0},{2,3},{3,2},{4,5},{5,4},{6,7},{7,6},{8,9},{9,8},{10,11... | collective-permute-start | bytes 3538952 | tf_op jit(solution)/shard_map/ppermute | solution.py:19

commit v11 on v7

--- a/solution.py
+++ b/solution.py
@@ -149,7 +149,7 @@
 
 
 def far(
-    emb, even, odd, peer, goal, goal_row, token, e_in, total_in, pos_in, unit, rnorm,
+    emb, odd, even, peer, goal, goal_row, token, e_in, total_in, pos_in, unit, rnorm,
     e_all, total, pos, unit_out, rnorm_out, note, part,
 ):
     def for_peer(block):
@@ -348,7 +348,7 @@
     state, keep = [everything, col, col, tall, col], lambda k: tuple((k + j, j) for j in range(5))
     note = shape((4, rows), F32)
     e_all, total, pos, unit, rnorm, own_note = call(
-        far, state + [note], emb, even, odd, peer, goal, goal_row, theirs, e_all, total, pos, unit, rnorm,
+        far, state + [note], emb, odd, even, peer, goal, goal_row, theirs, e_all, total, pos, unit, rnorm,
         kept=keep(7), scratch=[pltpu.VMEM((rows, 1), F32)], flops=3 * block_flops, name="far",
     )
     peer_note = in_chip(own_note)

time: 119 us -> 119 us (level)
  no operation moved by 1% of the time
where the time goes in v11:
time: 119 us; the launch traced here: 118 us
  blocking collectives  56.2 us (47%)
  starting transfers between devices  26.8 us (23%)
  Pallas kernels  17.9 us (15%)
  waiting for transfers between devices  16.5 us (14%)
    ppermute x11, starting transfers between devices, send(): return lax.ppermute(x, ALL, [(i, to(i) % 256) for i in range(256)])  26.8 us
    all_to_all x1, blocking collectives, on_device(): lax.all_to_all(partial.reshape(32, *share), NEAR, split_axis=0, concat_ax...  21.6 us
    all_to_all x1, blocking collectives, on_device(): lax.all_to_all(copies, NEAR, split_axis=0, concat_axis=0)  19.8 us
    ppermute x11, waiting for transfers between devices, send(): return lax.ppermute(x, ALL, [(i, to(i) % 256) for i in range(256)])  16.5 us
    all_to_all x1, blocking collectives, on_device(): got = lax.all_to_all(copies, 'zh', split_axis=0, concat_axis=0)  14.8 us
    pallas_call x13, Pallas kernels, call(): pl.pallas_call(body, out_shape=out, in_specs=[vmem] * len(arrays), out_sp...  10.9 us
    pallas_call x1, Pallas kernels, on_device(): pl.pallas_call(embed, in_specs=[hbm, hbm], out_specs=[vmem] * 3, out_shap...  3.52 us
    pallas_call x1, Pallas kernels, on_device(): pl.pallas_call(ends, in_specs=[vmem, vmem, vmem, anywhere], out_specs=[an...  2.47 us
  transfers between devices with their start and end apart: 11, of which 4 were waited for; matrix products, arithmetic and copies ran while one was open for 0% of the time, Pallas kernels for 7%

profile of v11, /device:TPU:1, one launch (start us, length us, event | category | flops | bytes accessed | tf_op | source)
XLA Modules:
  0.0 118.4 jit_solution(3209894693592229264)
XLA Ops:
  0.6 0.0 copy-start.1
  0.6 3.5 %embed.1 = (bf16[512,768]{1,0:T(8,128)(2,1)S(1)}, f32[512,768]{1,0:T(8,128)S(1)}, f32[512,1]{1,0:T(8,128)S(1)}) custom-call(bf16[512,1536]{1,0:T(8,128)(2,1)} %frames.3, bf16[1536,768]{1,0:T(8,128)(2,1)} %head.3), custom_call_target="tpu_custom_call" | custom-call | flops 1207959552 | bytes 4194304 | tf_op jit(solution)/shard_map/embed/pallas_call | solution.py:321
  4.2 3.3 %collective-permute-start.2 = (bf16[512,768]{1,0:T(8,128)(2,1)S(1)}, bf16[512,768]{1,0:T(8,128)(2,1)S(1)}, u32[]{:S(2)}, u32[]{:S(2)}) collective-permute-start(bf16[512,768]{1,0:T(8,128)(2,1)S(1)} %get-tuple-element.32.emb), channel_id=1, source_target_pairs={{0,1},{1,0},{2,3},{3,2},{4,5},{5,4},{6,7},{7,6},{8,9},{9,8},{10,11... | collective-permute-start | bytes 2359304 | tf_op jit(solution)/shard_map/ppermute | solution.py:19
  7.5 0.0 collective-permute-start
  7.5 9.0 %collective-permute-start.1 = (bf16[512,768]{1,0:T(8,128)(2,1)S(1)}, bf16[512,768]{1,0:T(8,128)(2,1)S(1)}, u32[]{:S(2)}, u32[]{:S(2)}) collective-permute-start(bf16[512,768]{1,0:T(8,128)(2,1)S(1)} %get-tuple-element.32.emb), channel_id=1, source_target_pairs={{0,254},{1,255},{2,4},{3,5},{4,2},{5,3},{6,8},{7,9},{8,6},{9,7},{1... | collective-permute-start | bytes 2359304 | tf_op jit(solution)/shard_map/ppermute | solution.py:19
  16.6 0.0 collective-permute-done.2.peer
  16.6 0.0 copy-done.1
  16.6 0.0 copy-start
  16.6 1.3 %near.1 = (f32[5,512,512]{2,1,0:T(8,128)S(1)}, f32[512,1]{1,0:T(8,128)S(1)}, f32[512,1]{1,0:T(8,128)S(1)}, f32[512,768]{1,0:T(8,128)S(1)}, f32[512,1]{1,0:T(8,12...) custom-call(bf16[512,768]{1,0:T(8,128)(2,1)S(1)} %get-tuple-element.32.emb, ...), custom_call_target="tpu_custom_call", output_to_operand_aliasing={{3}: (3, {}), {4}: (4, {})} | custom-call | flops 805306368 | bytes 9975808 | tf_op jit(solution)/shard_map/near/pallas_call | solution.py:53
  17.9 0.1 copy-done
  18.0 0.5 turn.1
  18.4 0.7 collective-permute-start.3
  19.2 7.4 %collective-permute-done.even = bf16[512,768]{1,0:T(8,128)(2,1)S(1)} collective-permute-done((bf16[512,768]{1,0:T(8,128)(2,1)S(1)}, bf16[512,768]{1,0:T(8,128)(2,1)S(1)}, u32[]{:S(2)}, u32[]{:S(2)}) %collective-permute-start) | collective-permute-done | bytes 786464 | tf_op jit(solution)/shard_map/ppermute | solution.py:19
  26.6 7.6 %collective-permute-done.1.odd = bf16[512,768]{1,0:T(8,128)(2,1)S(1)} collective-permute-done((bf16[512,768]{1,0:T(8,128)(2,1)S(1)}, bf16[512,768]{1,0:T(8,128)(2,1)S(1)}, u32[]{:S(2)}, u32[]{:S(2)}) %collective-permute-start.1) | collective-permute-done | bytes 786464 | tf_op jit(solution)/shard_map/ppermute | solution.py:19
  34.2 0.0 collective-permute-done.3.token.theirs
  34.2 2.2 %far.1 = (f32[5,512,512]{2,1,0:T(8,128)S(1)}, f32[512,1]{1,0:T(8,128)S(1)}, f32[512,1]{1,0:T(8,128)S(1)}, f32[512,768]{1,0:T(8,128)S(1)}, f32[512,1]{1,0:T(8,128)S(1)}, /*index=5*/f32[4,512]{1,0:T(4,128)S(1)}) custom-call(bf16[512,768]{1,0:T(8,128)(2,1)S(1)} %get-tuple-element.32.emb, ...), custom_call_target="tpu_custom_call", output_to_operand_aliasing={{0}: (7, {}), {1}: (8, {}), {2}: (9, {}), {3}: (10, {}), {4... | custom-call | flops 1207959552 | bytes 17588224 | tf_op jit(solution)/shard_map/far/pallas_call | solution.py:53
  36.4 1.0 collective-permute-start.4
  37.4 0.8 collective-permute-done.4.peer
  38.2 0.1 combine.1
  38.3 0.1 pick.1
  38.4 0.4 collective-permute-start.5
  38.8 0.0 collective-permute-start.6
  38.8 6.9 %collective-permute-start.7 = (f32[4,512]{1,0:T(4,128)S(1)}, f32[4,512]{1,0:T(4,128)S(1)}, u32[]{:S(2)}, u32[]{:S(2)}) collective-permute-start(f32[4,512]{1,0:T(4,128)S(1)} %get-tuple-element.44.token.pair), channel_id=1, source_target_pairs={{0,254},{1,255},{2,4},{3,5},{4,2},{5,3},{6,8},{7,9},{8,6},{9,7},{1... | collective-permute-start | bytes 24584 | tf_op jit(solution)/shard_map/ppermute | solution.py:19
  45.8 0.0 collective-permute-done.5.relay
  45.8 0.8 seal.1
  46.5 0.8 lose.1
  47.3 0.0 collective-permute-done.6.even_note
  47.3 0.0 collective-permute-done.7.odd_note
  47.3 1.6 %finish.2.token.dz_a = bf16[256,768]{1,0:T(8,128)(2,1)S(1)} custom-call(s32[512,1]{1,0:T(8,128)S(1)} %get-tuple-element.35.goal, f32[512,1]{1,0:T(8,128)S(1)} %get-tuple-element.53.inverse, f32[4,512]{1,0:T(4,128)S(1)} %get-tuple-element.44.token.pair, f32[4,512]{1,0:T(4,128)S(1)} %collective-permute-done.6.even_note, ...), custom_call_target="tpu_custom_call" | custom-call | flops 1006632960 | bytes 11175936 | tf_op jit(solution)/shard_map/finish/pallas_call | solution.py:53
  49.0 1.1 collective-permute-start.8
  50.0 1.6 %finish.3.dz_b = bf16[256,768]{1,0:T(8,128)(2,1)S(1)} custom-call(s32[512,1]{1,0:T(8,128)S(1)} %get-tuple-element.35.goal, f32[512,1]{1,0:T(8,128)S(1)} %get-tuple-element.53.inverse, f32[4,512]{1,0:T(4,128)S(1)} %get-tuple-element.44.token.pair, f32[4,512]{1,0:T(4,128)S(1)} %collective-permute-done.6.even_note, ...), custom_call_target="tpu_custom_call" | custom-call | flops 1006632960 | bytes 11565056 | tf_op jit(solution)/shard_map/finish/pallas_call | solution.py:53
  51.6 0.1 collective-permute-start.9
  51.7 0.0 collective-permute-done.8.other_a
  51.8 1.1 head_first.1.part
  52.9 0.6 collective-permute-done.9.other_b
  53.5 0.5 head_last.1
  53.9 21.6 %all_to_all.15.got = bf16[32,48,384]{2,1,0:T(8,128)(2,1)S(1)} all-to-all(bf16[32,48,384]{2,1,0:T(8,128)(2,1)S(1)} %bitcast.4), channel_id=1, replica_groups=mesh['zh'=4,'zl'=2,'y'=4,'x'=4,'core'=2] {'zl','y','x'}, dimensions={0} | all-to-all | bytes 2359296 | tf_op jit(solution)/shard_map/all_to_all | solution.py:384
  75.6 0.2 add_near.1
  75.7 14.8 %all_to_all.16.got = bf16[4,48,384]{2,1,0:T(8,128)(2,1)S(1)} all-to-all(bf16[4,48,384]{2,1,0:T(8,128)(2,1)S(1)} %add_near.1), channel_id=1, replica_groups=mesh['zh'=4,'zl'=2,'y'=4,'x'=4,'core'=2] {'zh'}, dimensions={0} | all-to-all | bytes 294912 | tf_op jit(solution)/shard_map/all_to_all | solution.py:386
  90.5 0.0 copy-start.2
  90.5 0.1 add_far.1
  90.6 19.8 %all_to_all.17 = bf16[32,48,384]{2,1,0:T(8,128)(2,1)S(1)} all-to-all(bf16[32,48,384]{2,1,0:T(8,128)(2,1)S(1)} %add_far.1), channel_id=1, replica_groups=mesh['zh'=4,'zl'=2,'y'=4,'x'=4,'core'=2] {'zl','y','x'}, dimensions={0} | all-to-all | bytes 2359296 | tf_op jit(solution)/shard_map/all_to_all | solution.py:388
  110.4 4.3 %collective-permute-start.10 = (bf16[2,768,384]{2,1,0:T(8,128)(2,1)S(1)}, bf16[2,768,384]{2,1,0:T(8,128)(2,1)S(1)}, u32[]{:S(2)}, u32[]{:S(2)}) collective-permute-start(bf16[2,768,384]{2,1,0:T(8,128)(2,1)S(1)} %bitcast.5), channel_id=1, source_target_pairs={{0,1},{1,0},{2,3},{3,2},{4,5},{5,4},{6,7},{7,6},{8,9},{9,8},{10,11... | collective-permute-start | bytes 3538952 | tf_op jit(solution)/shard_map/ppermute | solution.py:19
  114.7 0.0 copy-done.2
  114.7 2.5 %ends.1 = (bf16[512,1536]{1,0:T(8,128)(2,1)}, bf16[1536,768]{1,0:T(8,128)(2,1)}) custom-call(bf16[256,768]{1,0:T(8,128)(2,1)S(1)} %finish.2.token.dz_a, bf16[256,768]{1,0:T(8,128)(2,1)S(1)} %finish.3.dz_b, bf16[1536,768]{1,0:T(8,128)(2,1)S(1)} %copy-done.2, bf16[2,768,384]{2,1,0:T(8,128)(2,1)S(1)} %bitcast.6), custom_call_target="tpu_custom_call" | custom-call | flops 1207959552 | bytes 4194304 | tf_op jit(solution)/shard_map/ends/pallas_call | solution.py:391
  117.2 0.0 collective-permute-done.10.other
  117.2 1.1 last_half.1
Async XLA Ops:
  0.6 15.9 %copy-start.1 = (s32[512]{0:T(512)S(1)}, s32[512]{0:T(512)}, u32[]{:S(2)}) copy-start(s32[512]{0:T(512)} %param.5) | copy-start | bytes 6148
  4.2 12.4 %collective-permute-start.2 = (bf16[512,768]{1,0:T(8,128)(2,1)S(1)}, bf16[512,768]{1,0:T(8,128)(2,1)S(1)}, u32[]{:S(2)}, u32[]{:S(2)}) collective-permute-start(bf16[512,768]{1,0:T(8,128)(2,1)S(1)} %get-tuple-element.32.emb), channel_id=1, source_target_pairs={{0,1},{1,0},{2,3},{3,2},{4,5},{5,4},{6,7},{7,6},{8,9},{9,8},{10,11... | collective-permute-start | bytes 2359304 | tf_op jit(solution)/shard_map/ppermute | solution.py:19
  7.5 19.1 %collective-permute-start = (bf16[512,768]{1,0:T(8,128)(2,1)S(1)}, bf16[512,768]{1,0:T(8,128)(2,1)S(1)}, u32[]{:S(2)}, u32[]{:S(2)}) collective-permute-start(bf16[512,768]{1,0:T(8,128)(2,1)S(1)} %get-tuple-element.32.emb), channel_id=1, source_target_pairs={{0,2},{1,3},{2,0},{3,1},{4,6},{5,7},{6,4},{7,5},{8,10},{9,11},{10,... | collective-permute-start | bytes 2359304 | tf_op jit(solution)/shard_map/ppermute | solution.py:19
  7.5 26.7 %collective-permute-start.1 = (bf16[512,768]{1,0:T(8,128)(2,1)S(1)}, bf16[512,768]{1,0:T(8,128)(2,1)S(1)}, u32[]{:S(2)}, u32[]{:S(2)}) collective-permute-start(bf16[512,768]{1,0:T(8,128)(2,1)S(1)} %get-tuple-element.32.emb), channel_id=1, source_target_pairs={{0,254},{1,255},{2,4},{3,5},{4,2},{5,3},{6,8},{7,9},{8,6},{9,7},{1... | collective-permute-start | bytes 2359304 | tf_op jit(solution)/shard_map/ppermute | solution.py:19
  16.6 1.4 %copy-start = (bf16[512,1536]{1,0:T(8,128)(2,1)S(1)}, bf16[512,1536]{1,0:T(8,128)(2,1)}, u32[]{:S(2)}) copy-start(bf16[512,1536]{1,0:T(8,128)(2,1)} %frames.3) | copy-start | bytes 4718596
  18.4 15.7 %collective-permute-start.3 = (bf16[768,512]{1,0:T(8,128)(2,1)S(1)}, bf16[768,512]{1,0:T(8,128)(2,1)S(1)}, u32[]{:S(2)}, u32[]{:S(2)}) collective-permute-start(bf16[768,512]{1,0:T(8,128)(2,1)S(1)} %get-tuple-element.38), channel_id=1, source_target_pairs={{0,1},{1,0},{2,3},{3,2},{4,5},{5,4},{6,7},{7,6},{8,9},{9,8},{10,11... | collective-permute-start | bytes 2359304 | tf_op jit(solution)/shard_map/ppermute | solution.py:19
  36.4 1.8 %collective-permute-start.4 = (f32[4,512]{1,0:T(4,128)S(1)}, f32[4,512]{1,0:T(4,128)S(1)}, u32[]{:S(2)}, u32[]{:S(2)}) collective-permute-start(f32[4,512]{1,0:T(4,128)S(1)} %get-tuple-element.43.own), channel_id=1, source_target_pairs={{0,1},{1,0},{2,3},{3,2},{4,5},{5,4},{6,7},{7,6},{8,9},{9,8},{10,11... | collective-permute-start | bytes 24584 | tf_op jit(solution)/shard_map/ppermute | solution.py:19
  38.4 7.3 %collective-permute-start.5 = (bf16[512,768]{1,0:T(8,128)(2,1)S(1)}, bf16[512,768]{1,0:T(8,128)(2,1)S(1)}, u32[]{:S(2)}, u32[]{:S(2)}) collective-permute-start(bf16[512,768]{1,0:T(8,128)(2,1)S(1)} %pick.1), channel_id=1, source_target_pairs={{0,1},{1,0},{2,3},{3,2},{4,5},{5,4},{6,7},{7,6},{8,9},{9,8},{10,11... | collective-permute-start | bytes 2359304 | tf_op jit(solution)/shard_map/ppermute | solution.py:19
  38.8 8.5 %collective-permute-start.6 = (f32[4,512]{1,0:T(4,128)S(1)}, f32[4,512]{1,0:T(4,128)S(1)}, u32[]{:S(2)}, u32[]{:S(2)}) collective-permute-start(f32[4,512]{1,0:T(4,128)S(1)} %get-tuple-element.44.token.pair), channel_id=1, source_target_pairs={{0,2},{1,3},{2,0},{3,1},{4,6},{5,7},{6,4},{7,5},{8,10},{9,11},{10,... | collective-permute-start | bytes 24584 | tf_op jit(solution)/shard_map/ppermute | solution.py:19
  38.8 8.5 %collective-permute-start.7 = (f32[4,512]{1,0:T(4,128)S(1)}, f32[4,512]{1,0:T(4,128)S(1)}, u32[]{:S(2)}, u32[]{:S(2)}) collective-permute-start(f32[4,512]{1,0:T(4,128)S(1)} %get-tuple-element.44.token.pair), channel_id=1, source_target_pairs={{0,254},{1,255},{2,4},{3,5},{4,2},{5,3},{6,8},{7,9},{8,6},{9,7},{1... | collective-permute-start | bytes 24584 | tf_op jit(solution)/shard_map/ppermute | solution.py:19
  49.0 2.8 %collective-permute-start.8 = (bf16[256,768]{1,0:T(8,128)(2,1)S(1)}, bf16[256,768]{1,0:T(8,128)(2,1)S(1)}, u32[]{:S(2)}, u32[]{:S(2)}) collective-permute-start(bf16[256,768]{1,0:T(8,128)(2,1)S(1)} %finish.2.token.dz_a), channel_id=1, source_target_pairs={{0,1},{1,0},{2,3},{3,2},{4,5},{5,4},{6,7},{7,6},{8,9},{9,8},{10,11... | collective-permute-start | bytes 1179656 | tf_op jit(solution)/shard_map/ppermute | solution.py:19
  51.6 1.8 %collective-permute-start.9 = (bf16[256,768]{1,0:T(8,128)(2,1)S(1)}, bf16[256,768]{1,0:T(8,128)(2,1)S(1)}, u32[]{:S(2)}, u32[]{:S(2)}) collective-permute-start(bf16[256,768]{1,0:T(8,128)(2,1)S(1)} %finish.3.dz_b), channel_id=1, source_target_pairs={{0,1},{1,0},{2,3},{3,2},{4,5},{5,4},{6,7},{7,6},{8,9},{9,8},{10,11... | collective-permute-start | bytes 1179656 | tf_op jit(solution)/shard_map/ppermute | solution.py:19
  90.5 24.2 %copy-start.2 = (bf16[1536,768]{1,0:T(8,128)(2,1)S(1)}, bf16[1536,768]{1,0:T(8,128)(2,1)}, u32[]{:S(2)}) copy-start(bf16[1536,768]{1,0:T(8,128)(2,1)} %head.3) | copy-start | bytes 7077892
  110.4 6.8 %collective-permute-start.10 = (bf16[2,768,384]{2,1,0:T(8,128)(2,1)S(1)}, bf16[2,768,384]{2,1,0:T(8,128)(2,1)S(1)}, u32[]{:S(2)}, u32[]{:S(2)}) collective-permute-start(bf16[2,768,384]{2,1,0:T(8,128)(2,1)S(1)} %bitcast.5), channel_id=1, source_target_pairs={{0,1},{1,0},{2,3},{3,2},{4,5},{5,4},{6,7},{7,6},{8,9},{9,8},{10,11... | collective-permute-start | bytes 3538952 | tf_op jit(solution)/shard_map/ppermute | solution.py:19
